TPU v7x, 256 devices: a whole 4x4x8 slice. The times are simulated.
256 devices in a mesh: trunk: 8 (over y_hi, x), adapter: 32 (over z, y_lo, core).
Axes of the slice: x: 4, y: 4 (y_hi: 2, y_lo: 2; y = y_hi * 2 + y_lo), z: 8, core: 2. Of those that a mesh axis runs over, the one named last changes fastest.
Arguments:
- states: bfloat16 [3072, 8192], P('trunk', 'adapter'), may hold values from -6 to 6
- opponent: int32 [3072], P('trunk'), may hold values from 0 to 511, as said below
- proj_gate: bfloat16 [8192, 20480], P('trunk', 'adapter'), may hold values from -0.0625 to 0.0625
- proj_up: bfloat16 [8192, 20480], P('trunk', 'adapter'), may hold values from -0.0625 to 0.0625
- adapter_down: bfloat16 [512, 8192, 64], P('trunk', 'adapter'), may hold values from -0.0625 to 0.0625
- adapter_up: bfloat16 [512, 64, 20480], P('trunk', None, 'adapter'), may hold values from -0.75 to 0.75
Outputs:
- hidden: bfloat16 [3072, 20480], P('trunk', 'adapter')
Inputs may be any that keep to these rules, and one draw needn't show every extreme that they name: `opponent`: rows come in aligned blocks of 384. In every block, for exactly one k the opponents 64 * k to 64 * k + 63 are named by exactly 96 rows; the other 288 rows of the block are split as evenly as possible over the other values of k.
All inputs are finite; a program needn't handle non-finite values.
Results may differ from a plain program's by a relative error of at most 0.0052.
Values may be sent and summed in bfloat16 or wider, within the bound.
No kernel may reach another device: no remote copies, remote signals or barrier semaphores. Data moves between devices by JAX's collectives and lax.ppermute only.
A program may use at most 128 MiB of HBM per device.

v0:
```python
import jax
import jax.numpy as jnp
from jax import lax
from jax.sharding import PartitionSpec as P


def on_device(states, opponent, proj_gate, proj_up, adapter_down, adapter_up):
    rows = states.shape[0]
    owners = lax.axis_size("trunk")
    per_owner = adapter_down.shape[0]
    capacity = 2 * rows // owners
    slots = owners * capacity
    target = opponent // per_owner
    choose = (target[:, None] == jnp.arange(owners, dtype=jnp.int32)[None, :]).astype(jnp.int32)
    position = jnp.sum((jnp.cumsum(choose, axis=0) - choose) * choose, axis=1)
    slot_of_row = target * capacity + position
    placed = slot_of_row[None, :] == jnp.arange(slots, dtype=jnp.int32)[:, None]
    placement = placed.astype(jnp.bfloat16)
    send_rows = jnp.dot(placement, states, preferred_element_type=jnp.float32).astype(jnp.bfloat16)
    send_ids = jnp.sum(jnp.where(placed, (opponent % per_owner + 1)[None, :], 0), axis=1) - 1
    send_rows = send_rows.reshape(owners, capacity, states.shape[1])
    send_ids = send_ids.reshape(owners, capacity)
    recv_rows, recv_ids = (
        lax.all_to_all(send_rows, "trunk", split_axis=0, concat_axis=0, tiled=True),
        lax.all_to_all(send_ids, "trunk", split_axis=0, concat_axis=0, tiled=True),
    )
    flat_rows = recv_rows.reshape(slots, recv_rows.shape[2])
    local_ids = recv_ids.reshape(slots)
    select = local_ids[:, None] == jnp.arange(per_owner, dtype=jnp.int32)[None, :]
    products = jnp.einsum(
        "sd,jdk->sjk", flat_rows, adapter_down, preferred_element_type=jnp.float32
    )
    partial_rank = jnp.sum(jnp.where(select[:, :, None], products, 0.0), axis=1)
    total_rank = lax.psum(partial_rank, "adapter")
    whole = lax.all_gather(states, "adapter", axis=1, tiled=True)
    gate_sum = jnp.dot(
        whole,
        lax.all_gather(proj_gate, "trunk", axis=0, tiled=True),
        preferred_element_type=jnp.float32,
    )
    up_sum = jnp.dot(
        whole,
        lax.all_gather(proj_up, "trunk", axis=0, tiled=True),
        preferred_element_type=jnp.float32,
    )
    rank_half = total_rank.astype(jnp.bfloat16)
    spread = jnp.where(select[:, :, None], rank_half[:, None, :], jnp.zeros((), jnp.bfloat16))
    offsets = jnp.einsum(
        "sjk,jkh->sh", spread, adapter_up, preferred_element_type=jnp.float32
    ).astype(jnp.bfloat16)
    returned = lax.all_to_all(
        offsets.reshape(owners, capacity, offsets.shape[1]),
        "trunk",
        split_axis=0,
        concat_axis=0,
        tiled=True,
    )
    returned_flat = returned.reshape(slots, returned.shape[2])
    row_offset = lax.dot_general(
        placement, returned_flat, (((0,), (0,)), ((), ())), preferred_element_type=jnp.float32
    )
    hidden = jax.nn.silu(gate_sum + row_offset) * up_sum
    return hidden.astype(jnp.bfloat16)


def solution(mesh):
    placed = (
        P("trunk", "adapter"),
        P("trunk"),
        P("trunk", "adapter"),
        P("trunk", "adapter"),
        P("trunk", "adapter", None),
        P("trunk", None, "adapter"),
    )
    return jax.shard_map(
        on_device, mesh=mesh, in_specs=placed, out_specs=P("trunk", "adapter"), check_vma=False
    )
```

profile of v0, /device:TPU:1, one launch (start us, length us, event | category | flops | bytes accessed | tf_op | source)
XLA Modules:
  0.0 394.1 jit_solution(5881803617353631079)
XLA Ops:
  6.5 0.7 all-gather.4.cloned.1.call-update
  7.3 0.7 all-gather.6.cloned.1.call-update
  8.1 0.7 all-gather.8.cloned.1.call-update
  8.7 0.7 add_select_fusion.1
  9.4 0.9 reduce-window.6
  10.3 0.2 slice_reduce_fusion
  10.9 0.7 sub.18
  11.6 7.5 %all-to-all-start = ((s32[8,1,96]{2,1,0:T(1,128)}), s32[8,1,96]{2,1,0:T(1,128)S(1)}, u32[]{:S(2)}, u32[]{:S(2)}) async-start(s32[8,1,96]{2,1,0:T(1,128)} %sub.18), calls=%async_computation | async-start | bytes 8192 | tf_op jit(solution)/shard_map/all_to_all | solution.py:25
  19.0 2.0 convolution_convert_fusion
  21.1 4.5 %all-to-all-done = s32[8,1,96]{2,1,0:T(1,128)S(1)} async-done(((s32[8,1,96]{2,1,0:T(1,128)}), s32[8,1,96]{2,1,0:T(1,128)S(1)}, u32[]{:S(2)}, u32[]{:S(2)}) %all-to-all-start) | async-done | bytes 3104 | tf_op jit(solution)/shard_map/all_to_all | solution.py:25
  25.5 3.5 all-to-all-start.1
  29.0 0.5 broadcast.84
  29.5 0.6 reduce.5
  30.2 7.4 %all-to-all-done.1 = bf16[8,96,256]{2,1,0:T(8,128)(2,1)S(1)} async-done(((bf16[8,96,256]{2,1,0:T(8,128)(2,1)}), bf16[8,96,256]{2,1,0:T(8,128)(2,1)S(1)}, u32[]{:S(2)}, u32[]{:S(2)}) %all-to-all-start.1) | async-done | bytes 393248 | tf_op jit(solution)/shard_map/all_to_all | solution.py:24
  37.5 1.8 fusion.17
  39.4 2.3 select_reduce_fusion
  41.6 108.5 %all-reduce.1 = bf16[768,64]{0,1:T(8,128)(2,1)S(1)} all-reduce(f32[768,64]{0,1:T(8,128)S(1)} %select_reduce_fusion), channel_id=1, replica_groups=mesh['trunk'=8,'adapter'=32] {'adapter'}, use_global_device_ids=true, to_apply=%region_5.6 | all-reduce | flops 49152 | bytes 294912 | tf_op jit(solution)/shard_map/psum | solution.py:34
  150.1 9.5 %bitcast_convert_fusion = bf16[768,640]{1,0:T(8,128)(2,1)} fusion(bf16[64,64,640]{2,1,0:T(8,128)(2,1)} %param.11, pred[768,64]{0,1:T(8,128)(4,1)S(1)} %iota_compare_fusion.3, bf16[768,64]{0,1:T(8,128)(2,1)S(1)} %all-reduce.1), kind=kOutput, calls=%fused_computation.6 | convolution fusion | flops 4030169088 | bytes 6373376 | tf_op jit(solution)/shard_map/sjk,jkh->sh/dot_general | solution.py:48
  159.6 3.7 all-to-all-start.2
  163.4 79.2 %all-gather.6.cloned.1.call-done = bf16[8192,640]{1,0:T(8,128)(2,1)} async-done(((bf16[1024,640]{1,0:T(8,128)(2,1)}), bf16[8192,640]{1,0:T(8,128)(2,1)}) %all-gather.6.cloned.1.call-update) | async-done | bytes 10485776 | tf_op jit(solution)/shard_map/all_gather | solution.py:38
  242.6 11.0 %fusion.16 = f32[384,640]{1,0:T(8,128)} fusion(bf16[384,8192]{1,0:T(8,128)(2,1)} %all-gather.4.cloned.1.call-done, bf16[8192,640]{1,0:T(8,128)(2,1)} %all-gather.6.cloned.1.call-done), kind=kOutput, calls=%fused_computation.35 | convolution fusion | flops 4026531840 | bytes 17760256 | tf_op jit(solution)/shard_map/dot_general | solution.py:36
  253.6 2.9 convolution_add_fusion
  256.5 120.0 %all-gather.8.cloned.1.call-done = bf16[8192,640]{1,0:T(8,128)(2,1)} async-done(((bf16[1024,640]{1,0:T(8,128)(2,1)}), bf16[8192,640]{1,0:T(8,128)(2,1)}) %all-gather.8.cloned.1.call-update) | async-done | bytes 10485776 | tf_op jit(solution)/shard_map/all_gather | solution.py:43
  376.5 11.1 %fusion.7 = bf16[384,640]{1,0:T(8,128)(2,1)} fusion(bf16[384,8192]{1,0:T(8,128)(2,1)} %all-gather.4.cloned.1.call-done, bf16[8192,640]{1,0:T(8,128)(2,1)} %all-gather.8.cloned.1.call-done, f32[384,640]{1,0:T(8,128)} %convolution_add_fusion), kind=kOutput, calls=%fused_computation.9 | convolution fusion | flops 4028006400 | bytes 18251776 | tf_op jit(solution)/shard_map/dot_general | solution.py:41
  (15 shorter events, 0.6 us)
Async XLA Ops:
  6.5 31.0 %copy-start = (bf16[64,256,64]{1,2,0:T(8,128)(2,1)S(1)}, bf16[64,256,64]{1,2,0:T(8,128)(2,1)}, u32[]{:S(2)}) copy-start(bf16[64,256,64]{1,2,0:T(8,128)(2,1)} %param.10) | copy-start | bytes 6291460
  6.5 156.9 %all-gather.4.cloned.1.call-start = ((), (), s32[]{:S(2)}) async-start(), calls=%async_computation.3 | async-start | bytes 6488064 | tf_op jit(solution)/shard_map/all_gather | solution.py:35
  7.3 235.4 %all-gather.6.cloned.1.call-start = ((), (), s32[]{:S(2)}) async-start(), calls=%async_computation.4 | async-start | bytes 11796480 | tf_op jit(solution)/shard_map/all_gather | solution.py:38
  8.0 368.5 %all-gather.8.cloned.1.call-start = ((), (), s32[]{:S(2)}) async-start(), calls=%async_computation.5 | async-start | bytes 11796480 | tf_op jit(solution)/shard_map/all_gather | solution.py:43
  11.6 14.0 %all-to-all-start = ((s32[8,1,96]{2,1,0:T(1,128)}), s32[8,1,96]{2,1,0:T(1,128)S(1)}, u32[]{:S(2)}, u32[]{:S(2)}) async-start(s32[8,1,96]{2,1,0:T(1,128)} %sub.18), calls=%async_computation | async-start | bytes 8192 | tf_op jit(solution)/shard_map/all_to_all | solution.py:25
  25.5 12.0 %all-to-all-start.1 = ((bf16[8,96,256]{2,1,0:T(8,128)(2,1)}), bf16[8,96,256]{2,1,0:T(8,128)(2,1)S(1)}, u32[]{:S(2)}, u32[]{:S(2)}) async-start(bf16[8,96,256]{2,1,0:T(8,128)(2,1)} %bitcast.3), calls=%async_computation.1 | async-start | bytes 786432 | tf_op jit(solution)/shard_map/all_to_all | solution.py:24
  159.6 94.0 %all-to-all-start.2 = ((bf16[8,96,640]{2,1,0:T(8,128)(2,1)}), bf16[8,96,640]{2,1,0:T(8,128)(2,1)S(1)}, u32[]{:S(2)}, u32[]{:S(2)}) async-start(bf16[8,96,640]{2,1,0:T(8,128)(2,1)} %bitcast.33), calls=%async_computation.2 | async-start | bytes 1966080 | tf_op jit(solution)/shard_map/all_to_all | solution.py:51
Sparse Core Ops, SparseCore 0:
  9.1 87.5 all-gather.3
  99.3 143.2 all-gather.5
  245.2 131.2 all-gather.7
where the time goes:
time: 395 us; the launch traced here: 394 us
  waiting for transfers between devices  213 us (54%)
  blocking collectives  109 us (28%)
  matrix products  38.3 us (10%)
  starting transfers between devices  14.7 us (4%)
  between operations  13.2 us (3%)
  other arithmetic  4.76 us (1%)
    all_gather x1, waiting for transfers between devices, on_device(): lax.all_gather(proj_up, 'trunk', axis=0, tiled=True)  120 us
    psum x1, blocking collectives, on_device(): total_rank = lax.psum(partial_rank, 'adapter')  109 us
    all_gather x1, waiting for transfers between devices, on_device(): lax.all_gather(proj_gate, 'trunk', axis=0, tiled=True)  79.2 us
    dot_general x1, matrix products, on_device(): jnp.dot(whole, lax.all_gather(proj_up, 'trunk', axis=0, tiled=True), pref...  11.1 us
    dot_general x1, matrix products, on_device(): jnp.dot(whole, lax.all_gather(proj_gate, 'trunk', axis=0, tiled=True), pr...  11 us
    dot_general x1, matrix products, on_device(): jnp.einsum('sjk,jkh->sh', spread, adapter_up, preferred_element_type=jnp....  9.51 us
  transfers between devices with their start and end apart: 6, of which 4 were waited for; matrix products, arithmetic and copies ran while one was open for 8% of the time, Pallas kernels for 0%

commit v1 on v0

v1 whole, which is shorter than its diff:
```python
import functools

import jax
import jax.numpy as jnp
from jax import lax
from jax.experimental import pallas as pl
from jax.experimental.pallas import tpu as pltpu
from jax.sharding import Mesh, PartitionSpec as P

TRUNK = ("yh", "x")
ADAPTER = ("z", "yl", "c")
SWAP = [(0, 1), (1, 0)]
NX, NZ = 4, 8
LANES = 128
VMEM_SPEC = pl.BlockSpec(memory_space=pltpu.VMEM)
COST = pl.CostEstimate(flops=8 * 10**9, bytes_accessed=16 * 2**20, transcendentals=0)


def after(value, *others):
    return lax.optimization_barrier((value, others))[0]


def start_pairs(flip):
    pairs = []
    for xs in range(NX):
        for h in range(2):
            for xd in range(NX):
                for yl in range(2):
                    source = (xs * NZ + h * NX + xd) * 2 + yl
                    z = 2 * ((xs - xd) % NX) + h
                    pairs.append((source, (xd * NZ + z) * 2 + (yl ^ flip)))
    return pairs


def finish_pairs(step):
    pairs = []
    for x in range(NX):
        for z in range(NZ):
            turn = 2 * (z % 2) - 1
            to = (x + z // 2 + (0, turn, -turn, 2)[step]) % NX
            pairs.append((x * NZ + z, to * NZ + z))
    return pairs


def gather_ring(mine, other):
    width = mine.shape[1]
    own = jnp.concatenate([mine, other], axis=1)
    odd = [(i, (i - 1 + 2 * (i % 2)) % NZ) for i in range(NZ)]
    even = [(i, (i + 1 - 2 * (i % 2)) % NZ) for i in range(NZ)]
    p1, q1 = lax.ppermute(own, "z", odd), lax.ppermute(own, "z", even)
    p2, q2 = lax.ppermute(q1, "z", odd), lax.ppermute(p1, "z", even)
    p3, q3 = lax.ppermute(q2, "z", odd), lax.ppermute(p2, "z", even)
    last = (
        lax.ppermute(q3[:, :width], "z", odd),
        lax.ppermute(p3[:, width:], "z", even),
    )

    def twin(piece):
        return tuple(lax.ppermute(part, "c", SWAP) for part in piece)

    def group(near, far):
        return (near, twin(near), far, twin(far))

    groups = [
        group((own,), (q1,)),
        group((p2,), (p1,)),
        group((q2,), (q3,)),
        group(last, (p3,)),
    ]
    return groups, (p1, p2, p3)


def multiply_kernel(shape, n_far, flags, *refs):
    count = len(shape)
    n_rows = sum(parts for group in shape for parts in group)
    row_refs, refs = refs[:n_rows], refs[n_rows:]
    own_ref, far_refs, refs = refs[0], refs[1 : 1 + n_far], refs[1 + n_far :]
    out_refs, (lhs, rhs, lhs_sems, rhs_sems) = refs[:count], refs[count:]
    side, yl, core = flags[0], flags[1], flags[2]
    depth = own_ref.shape[0]
    width = depth // 4
    weights = []
    for n in range(8):
        far, source_yl, source_core = n // 4, (n // 2) % 2, n % 2
        block = side if far == 0 else 1 - side
        c = jnp.where(core == source_core, 0, 1)
        y = jnp.where(yl == source_yl, 0, 1)
        to = pl.multiple_of(block * depth + (c * 2 + y) * width, width)
        if far:
            first = (n % 4) * width
            ref = far_refs[first * n_far // depth]
            ref = ref.at[pl.ds(first % (depth // n_far), width), :]
        else:
            ref = own_ref.at[pl.ds((n % 4) * width, width), :]
        weights.append(pltpu.make_async_copy(ref, rhs.at[pl.ds(to, width), :], rhs_sems.at[n]))
    for copy in weights:
        copy.start()
    index = 0
    waits = []
    for group, pieces in enumerate(shape):
        copies = []
        for piece, parts in enumerate(pieces):
            for part in range(parts):
                span = 2 * width // parts
                copies.append(
                    pltpu.make_async_copy(
                        row_refs[index],
                        lhs.at[group, :, pl.ds(piece * 2 * width + part * span, span)],
                        lhs_sems.at[index],
                    )
                )
                index += 1
        for copy in copies:
            copy.start()
        waits.append(copies)
    for copy in weights:
        copy.wait()
    for group, copies in enumerate(waits):
        for copy in copies:
            copy.wait()
        out_refs[group][...] = jnp.dot(
            lhs[group], rhs[...], preferred_element_type=jnp.float32
        ).astype(jnp.bfloat16)


def multiply(groups, weights, weights_far, flags, *others):
    shape = [[len(piece) for piece in group] for group in groups]
    arrays = [part for group in groups for piece in group for part in piece]
    count, rows = len(groups), arrays[0].shape[0]
    depth, hidden = weights.shape
    n_far = len(weights_far)
    anywhere = pl.BlockSpec(memory_space=pl.ANY)
    return pl.pallas_call(
        functools.partial(multiply_kernel, shape, n_far),
        out_shape=[jax.ShapeDtypeStruct((rows, hidden), jnp.bfloat16)] * count,
        in_specs=[pl.BlockSpec(memory_space=pltpu.SMEM)]
        + [anywhere] * (len(arrays) + 1 + n_far),
        out_specs=[VMEM_SPEC] * count,
        scratch_shapes=[
            pltpu.VMEM((count, rows, 2 * depth), jnp.bfloat16),
            pltpu.VMEM((2 * depth, hidden), jnp.bfloat16),
            pltpu.SemaphoreType.DMA((len(arrays),)),
            pltpu.SemaphoreType.DMA((8,)),
        ],
        compiler_params=pltpu.CompilerParams(vmem_limit_bytes=14 * 2**20),
        cost_estimate=COST,
        name="multiply",
    )(after(flags, *others), *arrays, weights, *weights_far)


def names_of(recv_ref, tile, rows):
    return recv_ref[pl.ds(tile * rows, rows), 256:].astype(jnp.float32)


def opponent_of(lanes, first, rank):
    return (first + 1 + lax.broadcasted_iota(jnp.int32, (1, lanes), 1) // rank).astype(jnp.float32)


def down_kernel(recv_ref, down_ref, out_ref, total):
    slots, rank, width = recv_ref.shape[0], 64, 256
    tiles = 3
    rows = slots // tiles
    total[...] = jnp.zeros_like(total)

    def step(chunk, carry):
        maps = down_ref[pl.ds(pl.multiple_of(chunk * 4 * rank, 4 * rank), 4 * rank), :]
        for tile in range(tiles):
            at = pl.ds(tile * rows, rows)
            product = lax.dot_general(
                recv_ref[at, :width], maps, (((1,), (1,)), ((), ())),
                preferred_element_type=jnp.float32,
            )
            names = names_of(recv_ref, tile, rows)
            first = names == opponent_of(LANES, chunk * 4, rank)
            second = names == opponent_of(LANES, chunk * 4 + 2, rank)
            total[at, :] += jnp.where(first, product[:, :LANES], 0.0) + jnp.where(
                second, product[:, LANES:], 0.0
            )
        return carry

    lax.fori_loop(0, down_ref.shape[0] // (4 * rank), step, 0)
    both = total[...] + pltpu.roll(total[...], rank, 1)
    n = out_ref.shape[0]
    low = both[: 16 * n].reshape(n, 16, LANES)
    high = both[16 * n :].reshape(n, 8, LANES)
    left = lax.broadcasted_iota(jnp.int32, (1, 1, LANES), 2) < rank
    out_ref[:, :8, :] = jnp.where(left, low[:, :8], high)
    out_ref[:, 8:, :] = jnp.where(left, low[:, 8:], 0.0)


def up_kernel(rank_ref, recv_ref, up_ref, out_ref, whole, spread):
    slots, rank = recv_ref.shape[0], 64
    n = rank_ref.shape[0]
    packed = rank_ref[...].astype(jnp.float32)
    left = lax.broadcasted_iota(jnp.int32, (1, LANES), 1) < rank
    low = packed.reshape(n * 16, LANES)
    high = packed[:, :8].reshape(n * 8, LANES)
    whole[: n * 16, :] = jnp.where(left, low, pltpu.roll(low, rank, 1))
    whole[n * 16 :, :] = jnp.where(left, pltpu.roll(high, rank, 1), high)
    tiles = 3
    rows = slots // tiles

    def step(tile, carry):
        at = pl.ds(pl.multiple_of(tile * rows, rows), rows)
        names = recv_ref[at, 256:].astype(jnp.float32)
        values = whole[at, :]
        for pair in range(up_ref.shape[0] // LANES):
            mine = names == opponent_of(LANES, pair * 2, rank)
            spread[:, pair * LANES : (pair + 1) * LANES] = jnp.where(mine, values, 0.0).astype(
                jnp.bfloat16
            )
        out_ref[at, :] = jnp.dot(
            spread[...], up_ref[...], preferred_element_type=jnp.float32
        ).astype(out_ref.dtype)
        return carry

    lax.fori_loop(0, tiles, step, 0)


def on_device(states, opponent, proj_gate, proj_up, adapter_down, adapter_up):
    rows, width = states.shape
    hidden = proj_gate.shape[1]
    owners = lax.axis_size(TRUNK)
    n_adapter = lax.axis_size(ADAPTER)
    per_owner, _, rank = adapter_down.shape
    capacity = 2 * rows // owners
    slots = owners * capacity
    side = jnp.where(lax.axis_index("z") % 2 == lax.axis_index("yh"), 0, 1)
    flags = jnp.stack([side, lax.axis_index("yl"), lax.axis_index("c")]).astype(jnp.int32)

    mine = lax.ppermute(states, ("x", "z", "yl"), start_pairs(0))
    other = lax.ppermute(states, ("x", "z", "yl"), start_pairs(1))
    cut = proj_up.shape[0] // 2
    up_far = [lax.ppermute(part, "yh", SWAP) for part in (proj_up[:cut], proj_up[cut:])]

    target = opponent // per_owner
    choose = target[:, None] == jnp.arange(owners, dtype=jnp.int32)[None, :]
    count = jnp.arange(rows, dtype=jnp.int32)
    before = (count[:, None] > count[None, :]).astype(jnp.bfloat16)
    ahead = jnp.dot(before, choose.astype(jnp.bfloat16), preferred_element_type=jnp.float32)
    position = jnp.sum(jnp.where(choose, ahead, 0.0), axis=1).astype(jnp.int32)
    placed = (
        (target * capacity + position)[None, :] == jnp.arange(slots, dtype=jnp.int32)[:, None]
    ).astype(jnp.bfloat16)
    number = jnp.broadcast_to((opponent % per_owner + 1)[:, None], (rows, LANES))
    payload = jnp.concatenate([states, number.astype(jnp.bfloat16)], axis=1)
    send = jnp.dot(placed, payload, preferred_element_type=jnp.float32).astype(jnp.bfloat16)
    recv = lax.all_to_all(
        send.reshape(owners, capacity, width + LANES), TRUNK, 0, 0, tiled=True
    ).reshape(slots, width + LANES)

    groups, steps = gather_ring(*after((mine, other), send))
    gate_far = [
        lax.ppermute(after(part, before), "yh", SWAP)
        for part, before in ((proj_gate[:cut], steps[0]), (proj_gate[cut:], steps[1]))
    ]

    partial_rank = pl.pallas_call(
        down_kernel,
        out_shape=jax.ShapeDtypeStruct((n_adapter, 16, LANES), jnp.float32),
        in_specs=[VMEM_SPEC] * 2,
        out_specs=VMEM_SPEC,
        scratch_shapes=[pltpu.VMEM((slots, LANES), jnp.float32)],
        compiler_params=pltpu.CompilerParams(vmem_limit_bytes=14 * 2**20),
        cost_estimate=COST,
        name="down",
    )(after(recv, up_far[0], steps[0]), jnp.transpose(adapter_down, (0, 2, 1)).reshape(per_owner * rank, width))
    rank_parts = lax.all_to_all(partial_rank, ADAPTER, 0, 0, tiled=True)
    rank_sum = jnp.sum(rank_parts, axis=0).astype(jnp.bfloat16)
    rank_half = lax.all_to_all(
        jnp.broadcast_to(rank_sum[None], (n_adapter, 16, LANES)), ADAPTER, 0, 0, tiled=True
    )

    ups, gates, last = [], [], []

    def finish(some, sums, weights, weights_far, *others):
        parts = multiply([groups[i] for i in some], weights, weights_far, flags, *others, *last)
        last[:] = [parts[0]]
        for at, i in enumerate(some):
            sums.append(lax.ppermute(parts[at], ("x", "z"), finish_pairs(i)))

    finish([0, 1], ups, proj_up, up_far, rank_sum)
    offsets = pl.pallas_call(
        up_kernel,
        out_shape=jax.ShapeDtypeStruct((slots, hidden), jnp.bfloat16),
        in_specs=[VMEM_SPEC] * 3,
        out_specs=VMEM_SPEC,
        scratch_shapes=[
            pltpu.VMEM((slots, LANES), jnp.float32),
            pltpu.VMEM((slots // 3, per_owner * rank), jnp.bfloat16),
        ],
        compiler_params=pltpu.CompilerParams(vmem_limit_bytes=18 * 2**20),
        cost_estimate=COST,
        name="up",
    )(after(rank_half, last[0], gate_far[0]), recv, adapter_up.reshape(per_owner * rank, hidden))
    returned = lax.all_to_all(
        offsets.reshape(owners, capacity, hidden), TRUNK, 0, 0, tiled=True
    ).reshape(slots, hidden)
    finish([2, 3], ups, proj_up, up_far, offsets)
    finish([0, 1], gates, proj_gate, gate_far, ups[0])
    finish([2, 3], gates, proj_gate, gate_far, ups[1])
    offset = lax.dot_general(
        placed, returned, (((0,), (0,)), ((), ())), preferred_element_type=jnp.float32
    )
    up_sum = functools.reduce(jnp.add, [value.astype(jnp.float32) for value in ups])
    gate_sum = functools.reduce(jnp.add, [value.astype(jnp.float32) for value in gates])
    return (jax.nn.silu(gate_sum + offset) * up_sum).astype(jnp.bfloat16)


def solution(mesh):
    fine = Mesh(mesh.devices.reshape(2, NX, NZ, 2, 2), TRUNK + ADAPTER)
    placed = (
        P(TRUNK, ADAPTER),
        P(TRUNK),
        P(TRUNK, ADAPTER),
        P(TRUNK, ADAPTER),
        P(TRUNK, ADAPTER, None),
        P(TRUNK, None, ADAPTER),
    )
    return jax.shard_map(
        on_device, mesh=fine, in_specs=placed, out_specs=P(TRUNK, ADAPTER), check_vma=False
    )
```

time: 395 us -> 214 us (0.54)
  the two profiles are of different devices: /device:TPU:1 before, /device:TPU:128 now
where the time goes in v1:
time: 214 us; the launch traced here: 212 us
  starting transfers between devices  84.5 us (39%)
  waiting for transfers between devices  62.6 us (29%)
  Pallas kernels  38.5 us (18%)
  local copies, waits for them, and re-layouts  17.2 us (8%)
  other arithmetic  4.87 us (2%)
  matrix products  4.45 us (2%)
    ppermute x8, starting transfers between devices, finish(): sums.append(lax.ppermute(parts[at], ('x', 'z'), finish_pairs(i)))  28.7 us
    pallas_call x4, Pallas kernels, multiply(): pl.pallas_call(functools.partial(multiply_kernel, shape, n_far), out_shap...  27.2 us
    ppermute x8, waiting for transfers between devices, finish(): sums.append(lax.ppermute(parts[at], ('x', 'z'), finish_pairs(i)))  20.4 us
    unnamed x39, local copies, waits for them, and re-layouts  10.7 us
    ppermute x1, waiting for transfers between devices, on_device(): mine = lax.ppermute(states, ('x', 'z', 'yl'), start_pairs(0))  10.3 us
    all_to_all x1, waiting for transfers between devices, on_device(): lax.all_to_all(send.reshape(owners, capacity, width + LANES), TRUNK, 0, 0...  10.1 us
    all_to_all x1, starting transfers between devices, on_device(): rank_parts = lax.all_to_all(partial_rank, ADAPTER, 0, 0, tiled=True)  8.68 us
    all_to_all x1, starting transfers between devices, on_device(): lax.all_to_all(jnp.broadcast_to(rank_sum[None], (n_adapter, 16, LANES)),...  8.26 us
  transfers between devices with their start and end apart: 35, of which 10 were waited for; matrix products, arithmetic and copies ran while one was open for 6% of the time, Pallas kernels for 18%

profile of v1, /device:TPU:128, one launch (start us, length us, event | category | flops | bytes accessed | tf_op | source)
XLA Modules:
  0.0 212.4 jit_solution(10187648713799572203)
XLA Ops:
  2.1 7.0 %collective-permute-start.1 = (bf16[384,256]{1,0:T(8,128)(2,1)}, bf16[384,256]{1,0:T(8,128)(2,1)S(1)}, u32[]{:S(2)}, u32[]{:S(2)}) collective-permute-start(bf16[384,256]{1,0:T(8,128)(2,1)} %param.6), channel_id=1, source_target_pairs={{0,2},{2,0},{4,58},{6,56},{8,82},{10,80},{12,106},{14,104},{16,6},... | collective-permute-start | bytes 589832 | tf_op jit(solution)/shard_map/ppermute | solution.py:232
  12.4 10.3 %collective-permute-done = bf16[384,256]{1,0:T(8,128)(2,1)S(1)} collective-permute-done((bf16[384,256]{1,0:T(8,128)(2,1)}, bf16[384,256]{1,0:T(8,128)(2,1)S(1)}, u32[]{:S(2)}, u32[]{:S(2)}) %collective-permute-start) | collective-permute-done | bytes 196640 | tf_op jit(solution)/shard_map/ppermute | solution.py:231
  22.7 5.2 %collective-permute-done.1 = bf16[384,256]{1,0:T(8,128)(2,1)S(1)} collective-permute-done((bf16[384,256]{1,0:T(8,128)(2,1)}, bf16[384,256]{1,0:T(8,128)(2,1)S(1)}, u32[]{:S(2)}, u32[]{:S(2)}) %collective-permute-start.1) | collective-permute-done | bytes 196640 | tf_op jit(solution)/shard_map/ppermute | solution.py:232
  32.3 4.7 %all-to-all-start = ((bf16[8,96,384]{2,1,0:T(8,128)(2,1)}), bf16[8,96,384]{2,1,0:T(8,128)(2,1)S(1)}, u32[]{:S(2)}, u32[]{:S(2)}) async-start(bf16[8,96,384]{2,1,0:T(8,128)(2,1)} %bitcast.17), calls=%async_computation | async-start | bytes 1179648 | tf_op jit(solution)/shard_map/all_to_all | solution.py:248
  37.0 3.2 %collective-permute-done.7.refs_6_ = bf16[384,512]{1,0:T(8,128)(2,1)} collective-permute-done((bf16[384,512]{1,0:T(8,128)(2,1)S(1)}, bf16[384,512]{1,0:T(8,128)(2,1)}, u32[]{:S(2)}, u32[]{:S(2)}) %collective-permute-start.7) | collective-permute-done | bytes 393248 | tf_op jit(solution)/shard_map/ppermute | solution.py:50
  44.9 10.1 %all-to-all-done = bf16[8,96,384]{2,1,0:T(8,128)(2,1)S(1)} async-done(((bf16[8,96,384]{2,1,0:T(8,128)(2,1)}), bf16[8,96,384]{2,1,0:T(8,128)(2,1)S(1)}, u32[]{:S(2)}, u32[]{:S(2)}) %all-to-all-start) | async-done | bytes 589856 | tf_op jit(solution)/shard_map/all_to_all | solution.py:248
  60.7 5.7 %down.1 = f32[32,16,128]{2,1,0:T(8,128)} custom-call(bf16[768,384]{1,0:T(8,128)(2,1)S(1)} %bitcast.13, bf16[4096,256]{1,0:T(8,128)(2,1)S(1)} %bitcast.16), custom_call_target="tpu_custom_call" | custom-call | flops 8000000000 | bytes 16777216 | tf_op jit(solution)/shard_map/down/pallas_call | solution.py:258
  66.4 8.7 %all-to-all-start.1 = ((f32[32,16,128]{2,1,0:T(8,128)}), f32[32,16,128]{2,1,0:T(8,128)}, u32[]{:S(2)}, u32[]{:S(2)}) async-start(f32[32,16,128]{2,1,0:T(8,128)} %down.1), calls=%async_computation.1 | async-start | bytes 524288 | tf_op jit(solution)/shard_map/all_to_all | solution.py:268
  77.5 5.6 %all-to-all-done.1 = f32[32,16,128]{2,1,0:T(8,128)} async-done(((f32[32,16,128]{2,1,0:T(8,128)}), f32[32,16,128]{2,1,0:T(8,128)}, u32[]{:S(2)}, u32[]{:S(2)}) %all-to-all-start.1) | async-done | bytes 262176 | tf_op jit(solution)/shard_map/all_to_all | solution.py:268
  84.7 8.3 %all-to-all-start.2 = ((bf16[32,16,128]{2,1,0:T(8,128)(2,1)}), bf16[32,16,128]{2,1,0:T(8,128)(2,1)S(1)}, u32[]{:S(2)}, u32[]{:S(2)}) async-start(bf16[32,16,128]{2,1,0:T(8,128)(2,1)} %broadcast_in_dim.10), calls=%async_computation.2 | async-start | bytes 262144 | tf_op jit(solution)/shard_map/all_to_all | solution.py:270
  102.4 7.1 %multiply.4 = (bf16[384,640]{1,0:T(8,128)(2,1)}, bf16[384,640]{1,0:T(8,128)(2,1)}) custom-call(s32[3]{0:T(128)S(1)} %pad_add_fusion.flags, bf16[384,512]{1,0:T(8,128)(2,1)S(1)} %copy-done.4, bf16[384,512]{1,0:T(8,128)(2,1)} %collective-permute-done.2.refs_1_, bf16[384,512]{1,0:T(8,128)(2,1)} %collective-permute-done.3.refs_2_, ...), custom_call_target="tpu_custom_call" | custom-call | flops 8000000000 | bytes 16777216 | tf_op jit(solution)/shard_map/multiply/pallas_call | solution.py:133
  109.6 5.2 %collective-permute-done.12.refs_9_.refs_11_ = bf16[512,640]{1,0:T(8,128)(2,1)S(1)} collective-permute-done((bf16[512,640]{1,0:T(8,128)(2,1)}, bf16[512,640]{1,0:T(8,128)(2,1)S(1)}, u32[]{:S(2)}, u32[]{:S(2)}) %collective-permute-start.12) | collective-permute-done | bytes 655392 | tf_op jit(solution)/shard_map/ppermute | solution.py:254
  118.7 5.6 %up.1 = bf16[768,640]{1,0:T(8,128)(2,1)S(1)} custom-call(bf16[32,16,128]{2,1,0:T(8,128)(2,1)S(1)} %all-to-all-done.2.rank_ref, bf16[768,384]{1,0:T(8,128)(2,1)S(1)} %bitcast.14, bf16[4096,640]{1,0:T(8,128)(2,1)S(1)} %bitcast.15), custom_call_target="tpu_custom_call" | custom-call | flops 8000000000 | bytes 16777216 | tf_op jit(solution)/shard_map/up/pallas_call | solution.py:283
  125.2 4.8 %all-to-all-start.3 = ((bf16[8,96,640]{2,1,0:T(8,128)(2,1)}), bf16[8,96,640]{2,1,0:T(8,128)(2,1)}, u32[]{:S(2)}, u32[]{:S(2)}) async-start(bf16[8,96,640]{2,1,0:T(8,128)(2,1)} %bitcast.12), calls=%async_computation.3 | async-start | bytes 1966080 | tf_op jit(solution)/shard_map/all_to_all | solution.py:296
  130.0 3.5 %collective-permute-start.23 = (bf16[512,640]{1,0:T(8,128)(2,1)}, bf16[512,640]{1,0:T(8,128)(2,1)S(1)}, u32[]{:S(2)}, u32[]{:S(2)}) collective-permute-start(bf16[512,640]{1,0:T(8,128)(2,1)} %get-tuple-element.31), channel_id=1, source_target_pairs={{0,128},{128,0},{1,129},{129,1},{2,130},{130,2},{3,131},{131,3},{4... | collective-permute-start | bytes 1966088 | tf_op jit(solution)/shard_map/ppermute | solution.py:254
  133.6 4.9 %collective-permute-start.11 = (bf16[384,640]{1,0:T(8,128)(2,1)}, bf16[384,640]{1,0:T(8,128)(2,1)S(1)}, u32[]{:S(2)}, u32[]{:S(2)}) collective-permute-start(bf16[384,640]{1,0:T(8,128)(2,1)} %get-tuple-element.24), channel_id=1, source_target_pairs={{0,0},{4,4},{8,40},{12,44},{16,80},{20,84},{24,120},{28,124},{32,3... | collective-permute-start | bytes 1474568 | tf_op jit(solution)/shard_map/ppermute | solution.py:280
  142.2 6.4 %multiply.5 = (bf16[384,640]{1,0:T(8,128)(2,1)}, bf16[384,640]{1,0:T(8,128)(2,1)S(1)}) custom-call(s32[3]{0:T(128)S(1)} %pad_add_fusion.flags, bf16[384,512]{1,0:T(8,128)(2,1)} %collective-permute-done.13.refs_0_, bf16[384,512]{1,0:T(8,128)(2,1)} %collective-permute-done.14.refs_1_, bf16[384,512]{1,0:T(8,128)(2,1)} %collective-permute-done.15.refs_2_, ...), custom_call_target="tpu_custom_call" | custom-call | flops 8000000000 | bytes 16777216 | tf_op jit(solution)/shard_map/multiply/pallas_call | solution.py:133
  149.3 4.8 %collective-permute-start.29 = (bf16[384,640]{1,0:T(8,128)(2,1)}, bf16[384,640]{1,0:T(8,128)(2,1)}, u32[]{:S(2)}, u32[]{:S(2)}) collective-permute-start(bf16[384,640]{1,0:T(8,128)(2,1)} %get-tuple-element.29), channel_id=1, source_target_pairs={{0,32},{4,100},{8,72},{12,12},{16,112},{20,52},{24,24},{28,92},{32... | collective-permute-start | bytes 1474568 | tf_op jit(solution)/shard_map/ppermute | solution.py:280
  159.1 6.3 %multiply.6 = (bf16[384,640]{1,0:T(8,128)(2,1)S(1)}, bf16[384,640]{1,0:T(8,128)(2,1)S(1)}) custom-call(s32[3]{0:T(128)S(1)} %pad_add_fusion.flags, bf16[384,512]{1,0:T(8,128)(2,1)S(1)} %copy-done.5, bf16[384,512]{1,0:T(8,128)(2,1)} %collective-permute-done.2.refs_1_, bf16[384,512]{1,0:T(8,128)(2,1)} %collective-permute-done.3.refs_2_, ...), custom_call_target="tpu_custom_call" | custom-call | flops 8000000000 | bytes 16777216 | tf_op jit(solution)/shard_map/multiply/pallas_call | solution.py:133
  165.8 7.2 %multiply.7 = (bf16[384,640]{1,0:T(8,128)(2,1)S(1)}, bf16[384,640]{1,0:T(8,128)(2,1)}) custom-call(s32[3]{0:T(128)S(1)} %pad_add_fusion.flags, bf16[384,512]{1,0:T(8,128)(2,1)} %collective-permute-done.13.refs_0_, bf16[384,512]{1,0:T(8,128)(2,1)} %collective-permute-done.14.refs_1_, bf16[384,512]{1,0:T(8,128)(2,1)} %collective-permute-done.15.refs_2_, ...), custom_call_target="tpu_custom_call" | custom-call | flops 8000000000 | bytes 16777216 | tf_op jit(solution)/shard_map/multiply/pallas_call | solution.py:133
  173.1 4.4 %collective-permute-start.27 = (bf16[384,640]{1,0:T(8,128)(2,1)S(1)}, bf16[384,640]{1,0:T(8,128)(2,1)}, u32[]{:S(2)}, u32[]{:S(2)}) collective-permute-start(bf16[384,640]{1,0:T(8,128)(2,1)S(1)} %get-tuple-element.36), channel_id=1, source_target_pairs={{0,32},{4,100},{8,72},{12,12},{16,112},{20,52},{24,24},{28,92},{32... | collective-permute-start | bytes 1474568 | tf_op jit(solution)/shard_map/ppermute | solution.py:280
  177.4 5.2 %collective-permute-start.28 = (bf16[384,640]{1,0:T(8,128)(2,1)}, bf16[384,640]{1,0:T(8,128)(2,1)}, u32[]{:S(2)}, u32[]{:S(2)}) collective-permute-start(bf16[384,640]{1,0:T(8,128)(2,1)} %get-tuple-element.37), channel_id=1, source_target_pairs={{0,64},{4,68},{8,104},{12,108},{16,16},{20,20},{24,56},{28,60},{32... | collective-permute-start | bytes 1474568 | tf_op jit(solution)/shard_map/ppermute | solution.py:280
  185.4 4.2 %collective-permute-start.24 = (bf16[384,640]{1,0:T(8,128)(2,1)S(1)}, bf16[384,640]{1,0:T(8,128)(2,1)}, u32[]{:S(2)}, u32[]{:S(2)}) collective-permute-start(bf16[384,640]{1,0:T(8,128)(2,1)S(1)} %get-tuple-element.32), channel_id=1, source_target_pairs={{0,0},{4,4},{8,40},{12,44},{16,80},{20,84},{24,120},{28,124},{32,3... | collective-permute-start | bytes 1474568 | tf_op jit(solution)/shard_map/ppermute | solution.py:280
  191.7 17.6 %collective-permute-done.25 = bf16[384,640]{1,0:T(8,128)(2,1)} collective-permute-done((bf16[384,640]{1,0:T(8,128)(2,1)S(1)}, bf16[384,640]{1,0:T(8,128)(2,1)}, u32[]{:S(2)}, u32[]{:S(2)}) %collective-permute-start.25) | collective-permute-done | bytes 491552 | tf_op jit(solution)/shard_map/ppermute | solution.py:280
  (106 shorter events, 55.7 us)
Async XLA Ops:
  0.0 22.7 %collective-permute-start = (bf16[384,256]{1,0:T(8,128)(2,1)}, bf16[384,256]{1,0:T(8,128)(2,1)S(1)}, u32[]{:S(2)}, u32[]{:S(2)}) collective-permute-start(bf16[384,256]{1,0:T(8,128)(2,1)} %param.6), channel_id=1, source_target_pairs={{0,0},{2,2},{4,56},{6,58},{8,80},{10,82},{12,104},{14,106},{16,4},... | collective-permute-start | bytes 589832 | tf_op jit(solution)/shard_map/ppermute | solution.py:231
  2.1 25.9 %collective-permute-start.1 = (bf16[384,256]{1,0:T(8,128)(2,1)}, bf16[384,256]{1,0:T(8,128)(2,1)S(1)}, u32[]{:S(2)}, u32[]{:S(2)}) collective-permute-start(bf16[384,256]{1,0:T(8,128)(2,1)} %param.6), channel_id=1, source_target_pairs={{0,2},{2,0},{4,58},{6,56},{8,82},{10,80},{12,106},{14,104},{16,6},... | collective-permute-start | bytes 589832 | tf_op jit(solution)/shard_map/ppermute | solution.py:232
  29.4 25.7 %collective-permute-start.9 = (bf16[512,640]{1,0:T(8,128)(2,1)}, bf16[512,640]{1,0:T(8,128)(2,1)S(1)}, u32[]{:S(2)}, u32[]{:S(2)}) collective-permute-start(bf16[512,640]{1,0:T(8,128)(2,1)} %get-tuple-element.42), channel_id=1, source_target_pairs={{0,128},{128,0},{1,129},{129,1},{2,130},{130,2},{3,131},{131,3},{4... | collective-permute-start | bytes 1966088 | tf_op jit(solution)/shard_map/ppermute | solution.py:234
  32.3 22.7 %all-to-all-start = ((bf16[8,96,384]{2,1,0:T(8,128)(2,1)}), bf16[8,96,384]{2,1,0:T(8,128)(2,1)S(1)}, u32[]{:S(2)}, u32[]{:S(2)}) async-start(bf16[8,96,384]{2,1,0:T(8,128)(2,1)} %bitcast.17), calls=%async_computation | async-start | bytes 1179648 | tf_op jit(solution)/shard_map/all_to_all | solution.py:248
  40.3 18.8 %collective-permute-start.5 = (bf16[384,512]{1,0:T(8,128)(2,1)}, bf16[384,512]{1,0:T(8,128)(2,1)}, u32[]{:S(2)}, u32[]{:S(2)}) collective-permute-start(bf16[384,512]{1,0:T(8,128)(2,1)} %collective-permute-done.3.refs_2_), channel_id=1, source_target_pairs={{0,28},{4,8},{8,4},{12,16},{16,12},{20,24},{24,20},{28,0},{1,29},{... | collective-permute-start | bytes 1179656 | tf_op jit(solution)/shard_map/ppermute | solution.py:51
  42.0 57.1 %collective-permute-start.10 = (bf16[512,640]{1,0:T(8,128)(2,1)}, bf16[512,640]{1,0:T(8,128)(2,1)}, u32[]{:S(2)}, u32[]{:S(2)}) collective-permute-start(bf16[512,640]{1,0:T(8,128)(2,1)} %get-tuple-element.41), channel_id=1, source_target_pairs={{0,128},{128,0},{1,129},{129,1},{2,130},{130,2},{3,131},{131,3},{4... | collective-permute-start | bytes 1966088 | tf_op jit(solution)/shard_map/ppermute | solution.py:234
  55.9 19.8 %collective-permute-start.18 = (bf16[384,512]{1,0:T(8,128)(2,1)}, bf16[384,512]{1,0:T(8,128)(2,1)}, u32[]{:S(2)}, u32[]{:S(2)}) collective-permute-start(bf16[384,512]{1,0:T(8,128)(2,1)} %collective-permute-done.13.refs_0_), channel_id=1, source_target_pairs={{0,28},{4,8},{8,4},{12,16},{16,12},{20,24},{24,20},{28,0},{1,29},{... | collective-permute-start | bytes 1179656 | tf_op jit(solution)/shard_map/ppermute | solution.py:52
  75.1 21.2 %collective-permute-start.2 = (bf16[384,512]{1,0:T(8,128)(2,1)}, bf16[384,512]{1,0:T(8,128)(2,1)}, u32[]{:S(2)}, u32[]{:S(2)}) collective-permute-start(bf16[384,512]{1,0:T(8,128)(2,1)} %copy-done.3), channel_id=1, source_target_pairs={{0,1},{1,0},{2,3},{3,2},{4,5},{5,4},{6,7},{7,6},{8,9},{9,8},{10,11... | collective-permute-start | bytes 1179656 | tf_op jit(solution)/shard_map/ppermute | solution.py:59
  75.3 23.8 %collective-permute-start.8 = (bf16[384,512]{1,0:T(8,128)(2,1)}, bf16[384,512]{1,0:T(8,128)(2,1)}, u32[]{:S(2)}, u32[]{:S(2)}) collective-permute-start(bf16[384,512]{1,0:T(8,128)(2,1)} %collective-permute-done.7.refs_6_), channel_id=1, source_target_pairs={{0,1},{1,0},{2,3},{3,2},{4,5},{5,4},{6,7},{7,6},{8,9},{9,8},{10,11... | collective-permute-start | bytes 1179656 | tf_op jit(solution)/shard_map/ppermute | solution.py:59
  75.7 24.2 %collective-permute-start.4 = (bf16[384,512]{1,0:T(8,128)(2,1)}, bf16[384,512]{1,0:T(8,128)(2,1)}, u32[]{:S(2)}, u32[]{:S(2)}) collective-permute-start(bf16[384,512]{1,0:T(8,128)(2,1)} %collective-permute-done.3.refs_2_), channel_id=1, source_target_pairs={{0,1},{1,0},{2,3},{3,2},{4,5},{5,4},{6,7},{7,6},{8,9},{9,8},{10,11... | collective-permute-start | bytes 1179656 | tf_op jit(solution)/shard_map/ppermute | solution.py:59
  75.8 24.5 %collective-permute-start.6 = (bf16[384,512]{1,0:T(8,128)(2,1)}, bf16[384,512]{1,0:T(8,128)(2,1)}, u32[]{:S(2)}, u32[]{:S(2)}) collective-permute-start(bf16[384,512]{1,0:T(8,128)(2,1)} %collective-permute-done.5.refs_4_), channel_id=1, source_target_pairs={{0,1},{1,0},{2,3},{3,2},{4,5},{5,4},{6,7},{7,6},{8,9},{9,8},{10,11... | collective-permute-start | bytes 1179656 | tf_op jit(solution)/shard_map/ppermute | solution.py:59
  84.7 30.9 %all-to-all-start.2 = ((bf16[32,16,128]{2,1,0:T(8,128)(2,1)}), bf16[32,16,128]{2,1,0:T(8,128)(2,1)S(1)}, u32[]{:S(2)}, u32[]{:S(2)}) async-start(bf16[32,16,128]{2,1,0:T(8,128)(2,1)} %broadcast_in_dim.10), calls=%async_computation.2 | async-start | bytes 262144 | tf_op jit(solution)/shard_map/all_to_all | solution.py:270
  99.2 30.9 %collective-permute-start.14 = (bf16[384,512]{1,0:T(8,128)(2,1)}, bf16[384,512]{1,0:T(8,128)(2,1)}, u32[]{:S(2)}, u32[]{:S(2)}) collective-permute-start(bf16[384,512]{1,0:T(8,128)(2,1)} %collective-permute-done.13.refs_0_), channel_id=1, source_target_pairs={{0,1},{1,0},{2,3},{3,2},{4,5},{5,4},{6,7},{7,6},{8,9},{9,8},{10,11... | collective-permute-start | bytes 1179656 | tf_op jit(solution)/shard_map/ppermute | solution.py:59
  100.3 38.1 %collective-permute-start.22 = (bf16[384,512]{1,0:T(8,128)(2,1)}, bf16[384,512]{1,0:T(8,128)(2,1)}, u32[]{:S(2)}, u32[]{:S(2)}) collective-permute-start(bf16[384,512]{1,0:T(8,128)(2,1)} %collective-permute-done.18.refs_8_), channel_id=1, source_target_pairs={{0,1},{1,0},{2,3},{3,2},{4,5},{5,4},{6,7},{7,6},{8,9},{9,8},{10,11... | collective-permute-start | bytes 1179656 | tf_op jit(solution)/shard_map/ppermute | solution.py:59
  115.6 25.5 %collective-permute-start.16 = (bf16[384,512]{1,0:T(8,128)(2,1)}, bf16[384,512]{1,0:T(8,128)(2,1)}, u32[]{:S(2)}, u32[]{:S(2)}) collective-permute-start(bf16[384,512]{1,0:T(8,128)(2,1)} %collective-permute-done.15.refs_2_), channel_id=1, source_target_pairs={{0,1},{1,0},{2,3},{3,2},{4,5},{5,4},{6,7},{7,6},{8,9},{9,8},{10,11... | collective-permute-start | bytes 1179656 | tf_op jit(solution)/shard_map/ppermute | solution.py:59
  116.1 25.0 %collective-permute-start.20 = (bf16[384,256]{1,0:T(8,128)(2,1)}, bf16[384,256]{1,0:T(8,128)(2,1)}, u32[]{:S(2)}, u32[]{:S(2)}) collective-permute-start(bf16[384,256]{1,0:T(8,128)(2,1)} %collective-permute-done.17.refs_4_), channel_id=1, source_target_pairs={{0,1},{1,0},{2,3},{3,2},{4,5},{5,4},{6,7},{7,6},{8,9},{9,8},{10,11... | collective-permute-start | bytes 589832 | tf_op jit(solution)/shard_map/ppermute | solution.py:59
  125.2 64.4 %all-to-all-start.3 = ((bf16[8,96,640]{2,1,0:T(8,128)(2,1)}), bf16[8,96,640]{2,1,0:T(8,128)(2,1)}, u32[]{:S(2)}, u32[]{:S(2)}) async-start(bf16[8,96,640]{2,1,0:T(8,128)(2,1)} %bitcast.12), calls=%async_computation.3 | async-start | bytes 1966080 | tf_op jit(solution)/shard_map/all_to_all | solution.py:296
  130.0 29.0 %collective-permute-start.23 = (bf16[512,640]{1,0:T(8,128)(2,1)}, bf16[512,640]{1,0:T(8,128)(2,1)S(1)}, u32[]{:S(2)}, u32[]{:S(2)}) collective-permute-start(bf16[512,640]{1,0:T(8,128)(2,1)} %get-tuple-element.31), channel_id=1, source_target_pairs={{0,128},{128,0},{1,129},{129,1},{2,130},{130,2},{3,131},{131,3},{4... | collective-permute-start | bytes 1966088 | tf_op jit(solution)/shard_map/ppermute | solution.py:254
  133.6 23.0 %collective-permute-start.11 = (bf16[384,640]{1,0:T(8,128)(2,1)}, bf16[384,640]{1,0:T(8,128)(2,1)S(1)}, u32[]{:S(2)}, u32[]{:S(2)}) collective-permute-start(bf16[384,640]{1,0:T(8,128)(2,1)} %get-tuple-element.24), channel_id=1, source_target_pairs={{0,0},{4,4},{8,40},{12,44},{16,80},{20,84},{24,120},{28,124},{32,3... | collective-permute-start | bytes 1474568 | tf_op jit(solution)/shard_map/ppermute | solution.py:280
  138.5 27.3 %collective-permute-start.26 = (bf16[384,640]{1,0:T(8,128)(2,1)}, bf16[384,640]{1,0:T(8,128)(2,1)S(1)}, u32[]{:S(2)}, u32[]{:S(2)}) collective-permute-start(bf16[384,640]{1,0:T(8,128)(2,1)} %get-tuple-element.34), channel_id=1, source_target_pairs={{0,96},{4,36},{8,8},{12,76},{16,48},{20,116},{24,88},{28,28},{32,0... | collective-permute-start | bytes 1474568 | tf_op jit(solution)/shard_map/ppermute | solution.py:280
  148.6 36.0 %collective-permute-start.30 = (bf16[384,640]{1,0:T(8,128)(2,1)S(1)}, bf16[384,640]{1,0:T(8,128)(2,1)S(1)}, u32[]{:S(2)}, u32[]{:S(2)}) collective-permute-start(bf16[384,640]{1,0:T(8,128)(2,1)S(1)} %get-tuple-element.38), channel_id=1, source_target_pairs={{0,64},{4,68},{8,104},{12,108},{16,16},{20,20},{24,56},{28,60},{32... | collective-permute-start | bytes 1474568 | tf_op jit(solution)/shard_map/ppermute | solution.py:280
  149.3 42.3 %collective-permute-start.29 = (bf16[384,640]{1,0:T(8,128)(2,1)}, bf16[384,640]{1,0:T(8,128)(2,1)}, u32[]{:S(2)}, u32[]{:S(2)}) collective-permute-start(bf16[384,640]{1,0:T(8,128)(2,1)} %get-tuple-element.29), channel_id=1, source_target_pairs={{0,32},{4,100},{8,72},{12,12},{16,112},{20,52},{24,24},{28,92},{32... | collective-permute-start | bytes 1474568 | tf_op jit(solution)/shard_map/ppermute | solution.py:280
  182.7 26.6 %collective-permute-start.25 = (bf16[384,640]{1,0:T(8,128)(2,1)S(1)}, bf16[384,640]{1,0:T(8,128)(2,1)}, u32[]{:S(2)}, u32[]{:S(2)}) collective-permute-start(bf16[384,640]{1,0:T(8,128)(2,1)S(1)} %get-tuple-element.33), channel_id=1, source_target_pairs={{0,96},{4,36},{8,8},{12,76},{16,48},{20,116},{24,88},{28,28},{32,0... | collective-permute-start | bytes 1474568 | tf_op jit(solution)/shard_map/ppermute | solution.py:280
  185.4 23.9 %collective-permute-start.24 = (bf16[384,640]{1,0:T(8,128)(2,1)S(1)}, bf16[384,640]{1,0:T(8,128)(2,1)}, u32[]{:S(2)}, u32[]{:S(2)}) collective-permute-start(bf16[384,640]{1,0:T(8,128)(2,1)S(1)} %get-tuple-element.32), channel_id=1, source_target_pairs={{0,0},{4,4},{8,40},{12,44},{16,80},{20,84},{24,120},{28,124},{32,3... | collective-permute-start | bytes 1474568 | tf_op jit(solution)/shard_map/ppermute | solution.py:280
  (30 other events, 360.8 us)

commit v2 on v1

v2 whole, which is shorter than its diff:
```python
import jax
import jax.numpy as jnp
from jax import lax
from jax.experimental import pallas as pl
from jax.experimental.pallas import tpu as pltpu
from jax.sharding import Mesh, PartitionSpec as P

TRUNK = ("yh", "x")
ADAPTER = ("z", "yl", "c")
SWAP = [(0, 1), (1, 0)]
NX, NZ = 4, 8
LANES = 128
HBM_SPEC = pl.BlockSpec(memory_space=pltpu.HBM)
VMEM_SPEC = pl.BlockSpec(memory_space=pltpu.VMEM)
COST = pl.CostEstimate(flops=8 * 10**9, bytes_accessed=16 * 2**20, transcendentals=0)


def after(value, *others):
    return lax.optimization_barrier((value, others))[0]


def start_pairs(flip):
    pairs = []
    for xs in range(NX):
        for h in range(2):
            for xd in range(NX):
                for yl in range(2):
                    source = (xs * NZ + h * NX + xd) * 2 + yl
                    pairs.append((source, (xd * NZ + h * NX + xs) * 2 + (yl ^ flip)))
    return pairs


def multiply_kernel(flags, rows_ref, own_ref, far_low, far_high, *refs):
    out_ref, lhs, rhs, lhs_sems, rhs_sems = refs[-5:]
    yh, yl = flags[0], flags[1]
    depth = own_ref.shape[0]
    width = depth // 4
    weights = []
    for n in range(8):
        block = yh if n < 4 else 1 - yh
        ref = own_ref if n < 4 else (far_low if n < 6 else far_high)
        first = (n % 4 if n < 4 else n % 2) * width
        source_yl, source_core = (n // 2) % 2, n % 2
        y = jnp.where(yl == source_yl, 0, 1)
        to = pl.multiple_of(block * depth + (source_core * 2 + y) * width, width)
        weights.append(
            pltpu.make_async_copy(
                ref.at[pl.ds(first, width), :],
                rhs.at[pl.ds(to, width), :],
                rhs_sems.at[n],
            )
        )
    for copy in weights:
        copy.start()
    rows = [
        [
            pltpu.make_async_copy(
                rows_ref.at[(h * NX + x) * 2 + core],
                lhs.at[x, :, pl.ds((h * 2 + core) * 2 * width, 2 * width)],
                lhs_sems.at[x, h * 2 + core],
            )
            for h in range(2)
            for core in range(2)
        ]
        for x in range(NX)
    ]
    for copies in rows:
        for copy in copies:
            copy.start()
    for copy in weights:
        copy.wait()
    for x, copies in enumerate(rows):
        for copy in copies:
            copy.wait()
        out_ref[x] = jnp.dot(
            lhs[x], rhs[...], preferred_element_type=jnp.float32
        ).astype(jnp.bfloat16)


def multiply(rows, weights, weights_far, flags, *others):
    count = rows.shape[1]
    depth, hidden = weights.shape
    return pl.pallas_call(
        multiply_kernel,
        out_shape=jax.ShapeDtypeStruct((NX, count, hidden), jnp.bfloat16),
        in_specs=[pl.BlockSpec(memory_space=pltpu.SMEM)] + [HBM_SPEC] * (4 + len(others)),
        out_specs=VMEM_SPEC,
        scratch_shapes=[
            pltpu.VMEM((NX, count, 2 * depth), jnp.bfloat16),
            pltpu.VMEM((2 * depth, hidden), jnp.bfloat16),
            pltpu.SemaphoreType.DMA((NX, 4)),
            pltpu.SemaphoreType.DMA((8,)),
        ],
        compiler_params=pltpu.CompilerParams(vmem_limit_bytes=56 * 2**20),
        cost_estimate=COST,
        name="multiply",
    )(flags, rows, weights, *weights_far, *others)


def names_of(recv_ref, tile, rows):
    return recv_ref[pl.ds(tile * rows, rows), 256:].astype(jnp.float32)


def opponent_of(lanes, first, rank):
    return (first + 1 + lax.broadcasted_iota(jnp.int32, (1, lanes), 1) // rank).astype(jnp.float32)


def down_kernel(recv_ref, down_ref, _, out_ref, total):
    slots, rank, width = recv_ref.shape[0], 64, 256
    tiles = 3
    rows = slots // tiles
    total[...] = jnp.zeros_like(total)

    def step(chunk, carry):
        maps = down_ref[pl.ds(pl.multiple_of(chunk * 4 * rank, 4 * rank), 4 * rank), :]
        for tile in range(tiles):
            at = pl.ds(tile * rows, rows)
            product = lax.dot_general(
                recv_ref[at, :width], maps, (((1,), (1,)), ((), ())),
                preferred_element_type=jnp.float32,
            )
            names = names_of(recv_ref, tile, rows)
            first = names == opponent_of(LANES, chunk * 4, rank)
            second = names == opponent_of(LANES, chunk * 4 + 2, rank)
            total[at, :] += jnp.where(first, product[:, :LANES], 0.0) + jnp.where(
                second, product[:, LANES:], 0.0
            )
        return carry

    lax.fori_loop(0, down_ref.shape[0] // (4 * rank), step, 0)
    both = total[...] + pltpu.roll(total[...], rank, 1)
    n = out_ref.shape[0]
    low = both[: 16 * n].reshape(n, 16, LANES)
    high = both[16 * n :].reshape(n, 8, LANES)
    left = lax.broadcasted_iota(jnp.int32, (1, 1, LANES), 2) < rank
    out_ref[:, :8, :] = jnp.where(left, low[:, :8], high)
    out_ref[:, 8:, :] = jnp.where(left, low[:, 8:], 0.0)


def sum_kernel(parts_ref, _, out_ref):
    total = jnp.sum(parts_ref[...], axis=0).astype(jnp.bfloat16)
    out_ref[...] = jnp.broadcast_to(total[None], out_ref.shape)


def up_kernel(rank_ref, recv_ref, up_ref, _, __, out_ref, whole, spread):
    slots, rank = recv_ref.shape[0], 64
    n = rank_ref.shape[0]
    packed = rank_ref[...].astype(jnp.float32)
    left = lax.broadcasted_iota(jnp.int32, (1, LANES), 1) < rank
    low = packed.reshape(n * 16, LANES)
    high = packed[:, :8].reshape(n * 8, LANES)
    whole[: n * 16, :] = jnp.where(left, low, pltpu.roll(low, rank, 1))
    whole[n * 16 :, :] = jnp.where(left, pltpu.roll(high, rank, 1), high)
    tiles = 3
    rows = slots // tiles

    def step(tile, carry):
        at = pl.ds(pl.multiple_of(tile * rows, rows), rows)
        names = recv_ref[at, 256:].astype(jnp.float32)
        values = whole[at, :]
        for pair in range(up_ref.shape[0] // LANES):
            mine = names == opponent_of(LANES, pair * 2, rank)
            spread[:, pair * LANES : (pair + 1) * LANES] = jnp.where(mine, values, 0.0).astype(
                jnp.bfloat16
            )
        out_ref[at, :] = jnp.dot(
            spread[...], up_ref[...], preferred_element_type=jnp.float32
        ).astype(out_ref.dtype)
        return carry

    lax.fori_loop(0, tiles, step, 0)


def on_device(states, opponent, proj_gate, proj_up, adapter_down, adapter_up):
    rows, width = states.shape
    hidden = proj_gate.shape[1]
    owners = lax.axis_size(TRUNK)
    n_adapter = lax.axis_size(ADAPTER)
    per_owner, _, rank = adapter_down.shape
    capacity = 2 * rows // owners
    slots = owners * capacity
    flags = jnp.stack([lax.axis_index("yh"), lax.axis_index("yl")]).astype(jnp.int32)

    mine = lax.ppermute(states, ("x", "z", "yl"), start_pairs(0))
    other = lax.ppermute(states, ("x", "z", "yl"), start_pairs(1))
    cut = proj_up.shape[0] // 2
    up_far, gate_far = (
        [lax.ppermute(part, "yh", SWAP) for part in (weights[:cut], weights[cut:])]
        for weights in (proj_up, proj_gate)
    )

    target = opponent // per_owner
    choose = target[:, None] == jnp.arange(owners, dtype=jnp.int32)[None, :]
    count = jnp.arange(rows, dtype=jnp.int32)
    before = (count[:, None] > count[None, :]).astype(jnp.bfloat16)
    ahead = jnp.dot(before, choose.astype(jnp.bfloat16), preferred_element_type=jnp.float32)
    position = jnp.sum(jnp.where(choose, ahead, 0.0), axis=1).astype(jnp.int32)
    placed = (
        (target * capacity + position)[None, :] == jnp.arange(slots, dtype=jnp.int32)[:, None]
    ).astype(jnp.bfloat16)
    number = jnp.broadcast_to((opponent % per_owner + 1)[:, None], (rows, LANES))
    payload = jnp.concatenate([states, number.astype(jnp.bfloat16)], axis=1)
    send = jnp.dot(placed, payload, preferred_element_type=jnp.float32).astype(jnp.bfloat16)
    recv = lax.all_to_all(
        send.reshape(owners, capacity, width + LANES), TRUNK, 0, 0, tiled=True
    ).reshape(slots, width + LANES)

    mine, other = after((mine, other), send)
    gathered = lax.all_gather(jnp.concatenate([mine, other], axis=1), ("z", "c"), axis=0)

    partial_rank = pl.pallas_call(
        down_kernel,
        out_shape=jax.ShapeDtypeStruct((n_adapter, 16, LANES), jnp.float32),
        in_specs=[VMEM_SPEC] * 2 + [HBM_SPEC],
        out_specs=VMEM_SPEC,
        scratch_shapes=[pltpu.VMEM((slots, LANES), jnp.float32)],
        compiler_params=pltpu.CompilerParams(vmem_limit_bytes=14 * 2**20),
        cost_estimate=COST,
        name="down",
    )(recv, jnp.transpose(adapter_down, (0, 2, 1)).reshape(per_owner * rank, width), up_far[0])
    rank_parts = lax.all_to_all(partial_rank, ADAPTER, 0, 0, tiled=True)
    rank_sum = pl.pallas_call(
        sum_kernel,
        out_shape=jax.ShapeDtypeStruct((n_adapter, 16, LANES), jnp.bfloat16),
        in_specs=[VMEM_SPEC, HBM_SPEC],
        out_specs=VMEM_SPEC,
        cost_estimate=COST,
        name="sum",
    )(rank_parts, up_far[1])
    rank_half = lax.all_to_all(rank_sum, ADAPTER, 0, 0, tiled=True)
    ups = multiply(gathered, proj_up, up_far, flags, rank_half, gate_far[0])
    up_sum = lax.psum_scatter(ups, "x", scatter_dimension=0, tiled=False)
    offsets = pl.pallas_call(
        up_kernel,
        out_shape=jax.ShapeDtypeStruct((slots, hidden), jnp.bfloat16),
        in_specs=[VMEM_SPEC] * 3 + [HBM_SPEC] * 2,
        out_specs=VMEM_SPEC,
        scratch_shapes=[
            pltpu.VMEM((slots, LANES), jnp.float32),
            pltpu.VMEM((slots // 3, per_owner * rank), jnp.bfloat16),
        ],
        compiler_params=pltpu.CompilerParams(vmem_limit_bytes=18 * 2**20),
        cost_estimate=COST,
        name="up",
    )(rank_half, recv, adapter_up.reshape(per_owner * rank, hidden), ups, gate_far[1])
    returned = lax.all_to_all(
        offsets.reshape(owners, capacity, hidden), TRUNK, 0, 0, tiled=True
    ).reshape(slots, hidden)
    gates = multiply(gathered, proj_gate, gate_far, flags, offsets)
    gate_parts = lax.all_to_all(after(gates, returned), "x", 0, 0, tiled=True)
    offset = lax.dot_general(
        placed, returned, (((0,), (0,)), ((), ())), preferred_element_type=jnp.float32
    )
    gate_sum = jnp.sum(gate_parts.astype(jnp.float32), axis=0)
    return (jax.nn.silu(gate_sum + offset) * up_sum.astype(jnp.float32)).astype(jnp.bfloat16)


def solution(mesh):
    fine = Mesh(mesh.devices.reshape(2, NX, NZ, 2, 2), TRUNK + ADAPTER)
    placed = (
        P(TRUNK, ADAPTER),
        P(TRUNK),
        P(TRUNK, ADAPTER),
        P(TRUNK, ADAPTER),
        P(TRUNK, ADAPTER, None),
        P(TRUNK, None, ADAPTER),
    )
    return jax.shard_map(
        on_device, mesh=fine, in_specs=placed, out_specs=P(TRUNK, ADAPTER), check_vma=False
    )
```

time: 214 us -> 202 us (0.944)
  the two profiles are of different devices: /device:TPU:128 before, /device:TPU:1 now
where the time goes in v2:
time: 202 us; the launch traced here: 201 us
  starting transfers between devices  70.4 us (35%)
  Pallas kernels  39.4 us (20%)
  waiting for transfers between devices  32.1 us (16%)
  blocking collectives  27.6 us (14%)
  between operations  13.5 us (7%)
  local copies, waits for them, and re-layouts  10.4 us (5%)
  matrix products  5.12 us (3%)
  other arithmetic  2.36 us (1%)
    all_to_all x1, blocking collectives, on_device(): gate_parts = lax.all_to_all(after(gates, returned), 'x', 0, 0, tiled=True)  27.6 us
    all_to_all x1, starting transfers between devices, on_device(): lax.all_to_all(send.reshape(owners, capacity, width + LANES), TRUNK, 0, 0...  25.5 us
    pallas_call x2, Pallas kernels, multiply(): pl.pallas_call(multiply_kernel, out_shape=jax.ShapeDtypeStruct((NX, count...  25.5 us
    all_to_all x1, starting transfers between devices, on_device(): rank_parts = lax.all_to_all(partial_rank, ADAPTER, 0, 0, tiled=True)  17.4 us
    ppermute x4, starting transfers between devices, on_device(): lax.ppermute(part, 'yh', SWAP)  12 us
    all_to_all x1, waiting for transfers between devices, on_device(): lax.all_to_all(offsets.reshape(owners, capacity, hidden), TRUNK, 0, 0, ti...  9.03 us
    all_to_all x1, waiting for transfers between devices, on_device(): lax.all_to_all(send.reshape(owners, capacity, width + LANES), TRUNK, 0, 0...  8.64 us
    unnamed x22, local copies, waits for them, and re-layouts  8.33 us
  transfers between devices with their start and end apart: 12, of which 5 were waited for; matrix products, arithmetic and copies ran while one was open for 3% of the time, Pallas kernels for 20%

profile of v2, /device:TPU:1, one launch (start us, length us, event | category | flops | bytes accessed | tf_op | source)
XLA Modules:
  0.0 200.9 jit_solution(1442524514920899434)
XLA Ops:
  8.1 2.1 %collective-permute-start.1 = (bf16[384,256]{1,0:T(8,128)(2,1)}, bf16[384,256]{1,0:T(8,128)(2,1)S(1)}, u32[]{:S(2)}, u32[]{:S(2)}) collective-permute-start(bf16[384,256]{1,0:T(8,128)(2,1)} %param.6), channel_id=1, source_target_pairs={{0,2},{2,0},{4,34},{6,32},{8,66},{10,64},{12,98},{14,96},{16,18},{... | collective-permute-start | bytes 589832 | tf_op jit(solution)/shard_map/ppermute | solution.py:185
  11.3 2.3 %convolution_convert_fusion = bf16[768,384]{1,0:T(8,128)(2,1)} fusion(s32[384]{0:T(512)S(1)} %convert_add_fusion, bf16[384,128]{1,0:T(8,128)(2,1)S(1)} %broadcast_in_dim.7, bf16[384,256]{1,0:T(8,128)(2,1)} %param.6), kind=kOutput, calls=%fused_computation.2 | convolution fusion | flops 227672064 | bytes 886272 | tf_op jit(solution)/shard_map/dot_general | solution.py:203
  15.7 3.9 %collective-permute-start.4 = (bf16[512,640]{1,0:T(8,128)(2,1)}, bf16[512,640]{1,0:T(8,128)(2,1)S(1)}, u32[]{:S(2)}, u32[]{:S(2)}) collective-permute-start(bf16[512,640]{1,0:T(8,128)(2,1)} %get-tuple-element.12), channel_id=1, source_target_pairs={{0,128},{128,0},{1,129},{129,1},{2,130},{130,2},{3,131},{131,3},{4... | collective-permute-start | bytes 1966088 | tf_op jit(solution)/shard_map/ppermute | solution.py:188
  19.6 25.5 %all-to-all-start = ((bf16[8,96,384]{2,1,0:T(8,128)(2,1)}), bf16[8,96,384]{2,1,0:T(8,128)(2,1)S(1)}, u32[]{:S(2)}, u32[]{:S(2)}) async-start(bf16[8,96,384]{2,1,0:T(8,128)(2,1)} %bitcast.3), calls=%async_computation | async-start | bytes 1179648 | tf_op jit(solution)/shard_map/all_to_all | solution.py:204
  45.2 3.0 %collective-permute-start.5 = (bf16[512,640]{1,0:T(8,128)(2,1)S(1)}, bf16[512,640]{1,0:T(8,128)(2,1)}, u32[]{:S(2)}, u32[]{:S(2)}) collective-permute-start(bf16[512,640]{1,0:T(8,128)(2,1)S(1)} %get-tuple-element.11), channel_id=1, source_target_pairs={{0,128},{128,0},{1,129},{129,1},{2,130},{130,2},{3,131},{131,3},{4... | collective-permute-start | bytes 1966088 | tf_op jit(solution)/shard_map/ppermute | solution.py:188
  48.1 8.6 %all-to-all-done = bf16[8,96,384]{2,1,0:T(8,128)(2,1)S(1)} async-done(((bf16[8,96,384]{2,1,0:T(8,128)(2,1)}), bf16[8,96,384]{2,1,0:T(8,128)(2,1)S(1)}, u32[]{:S(2)}, u32[]{:S(2)}) %all-to-all-start) | async-done | bytes 589856 | tf_op jit(solution)/shard_map/all_to_all | solution.py:204
  56.8 1.8 copy-done.4
  58.6 5.8 %down.1 = f32[32,16,128]{2,1,0:T(8,128)} custom-call(bf16[768,384]{1,0:T(8,128)(2,1)S(1)} %bitcast.15, bf16[4096,256]{1,0:T(8,128)(2,1)S(1)} %bitcast.18, bf16[512,640]{1,0:T(8,128)(2,1)S(1)} %collective-permute-done.4._.far_low), custom_call_target="tpu_custom_call" | custom-call | flops 8000000000 | bytes 16777216 | tf_op jit(solution)/shard_map/down/pallas_call | solution.py:211
  64.4 17.4 %all-to-all-start.1 = ((f32[32,16,128]{2,1,0:T(8,128)}), f32[32,16,128]{2,1,0:T(8,128)S(1)}, u32[]{:S(2)}, u32[]{:S(2)}) async-start(f32[32,16,128]{2,1,0:T(8,128)} %down.1), calls=%async_computation.1 | async-start | bytes 524288 | tf_op jit(solution)/shard_map/all_to_all | solution.py:221
  82.7 2.6 %collective-permute-start.2 = (bf16[512,640]{1,0:T(8,128)(2,1)S(1)}, bf16[512,640]{1,0:T(8,128)(2,1)S(1)}, u32[]{:S(2)}, u32[]{:S(2)}) collective-permute-start(bf16[512,640]{1,0:T(8,128)(2,1)S(1)} %get-tuple-element.14), channel_id=1, source_target_pairs={{0,128},{128,0},{1,129},{129,1},{2,130},{130,2},{3,131},{131,3},{4... | collective-permute-start | bytes 1966088 | tf_op jit(solution)/shard_map/ppermute | solution.py:188
  85.3 7.9 %all-to-all-done.1.parts_ref = f32[32,16,128]{2,1,0:T(8,128)S(1)} async-done(((f32[32,16,128]{2,1,0:T(8,128)}), f32[32,16,128]{2,1,0:T(8,128)S(1)}, u32[]{:S(2)}, u32[]{:S(2)}) %all-to-all-start.1) | async-done | bytes 262176 | tf_op jit(solution)/shard_map/all_to_all | solution.py:221
  93.9 1.6 sum.1
  95.6 5.0 %all-to-all-start.2 = ((bf16[32,16,128]{2,1,0:T(8,128)(2,1)}), bf16[32,16,128]{2,1,0:T(8,128)(2,1)S(1)}, u32[]{:S(2)}, u32[]{:S(2)}) async-start(bf16[32,16,128]{2,1,0:T(8,128)(2,1)} %sum.1), calls=%async_computation.2 | async-start | bytes 262144 | tf_op jit(solution)/shard_map/all_to_all | solution.py:230
  100.6 2.6 %collective-permute-start.3 = (bf16[512,640]{1,0:T(8,128)(2,1)}, bf16[512,640]{1,0:T(8,128)(2,1)S(1)}, u32[]{:S(2)}, u32[]{:S(2)}) collective-permute-start(bf16[512,640]{1,0:T(8,128)(2,1)} %get-tuple-element.13), channel_id=1, source_target_pairs={{0,128},{128,0},{1,129},{129,1},{2,130},{130,2},{3,131},{131,3},{4... | collective-permute-start | bytes 1966088 | tf_op jit(solution)/shard_map/ppermute | solution.py:188
  103.8 6.1 %all-to-all-done.2.refs_0_.rank_ref = bf16[32,16,128]{2,1,0:T(8,128)(2,1)S(1)} async-done(((bf16[32,16,128]{2,1,0:T(8,128)(2,1)}), bf16[32,16,128]{2,1,0:T(8,128)(2,1)S(1)}, u32[]{:S(2)}, u32[]{:S(2)}) %all-to-all-start.2) | async-done | bytes 131104 | tf_op jit(solution)/shard_map/all_to_all | solution.py:230
  110.6 12.7 %multiply.2._ = bf16[4,384,640]{2,1,0:T(8,128)(2,1)} custom-call(s32[2]{0:T(128)} %pad_add_fusion.flags, bf16[16,384,512]{2,1,0:T(8,128)(2,1)} %bitcast.20, bf16[1024,640]{1,0:T(8,128)(2,1)} %own_ref.2, bf16[512,640]{1,0:T(8,128)(2,1)} %copy-done.5, bf16[512,640]{1,0:T(8,128)(2,1)} %collective-permute-done.5._.far_high, bf16[32,16,128]{2,1,0:T(8,128)(2,1)} %copy-done.1, ...), custom_call_target="tpu_custom_call" | custom-call | flops 8000000000 | bytes 16777216 | tf_op jit(solution)/shard_map/multiply/pallas_call | solution.py:83
  123.4 1.7 copy-done
  126.0 2.5 %copy-done.3 = bf16[64,64,640]{2,1,0:T(8,128)(2,1)S(1)} copy-done((bf16[64,64,640]{2,1,0:T(8,128)(2,1)S(1)}, bf16[64,64,640]{2,1,0:T(8,128)(2,1)}, u32[]{:S(2)}) %copy-start.3) | copy-done | bytes 5242904
  128.5 6.5 %up.1.refs_0_ = bf16[768,640]{1,0:T(8,128)(2,1)} custom-call(bf16[32,16,128]{2,1,0:T(8,128)(2,1)S(1)} %copy-done.2, bf16[768,384]{1,0:T(8,128)(2,1)S(1)} %bitcast.16, bf16[4096,640]{1,0:T(8,128)(2,1)S(1)} %bitcast.17, bf16[4,384,640]{2,1,0:T(8,128)(2,1)S(1)} %copy-done, bf16[512,640]{1,0:T(8,128)(2,1)S(1)} %collective-permute-done.3.__.far_high), custom_call_target="tpu_custom_call" | custom-call | flops 8000000000 | bytes 16777216 | tf_op jit(solution)/shard_map/up/pallas_call | solution.py:233
  135.0 6.7 %all-to-all-start.3 = ((bf16[8,96,640]{2,1,0:T(8,128)(2,1)}), bf16[8,96,640]{2,1,0:T(8,128)(2,1)S(1)}, u32[]{:S(2)}, u32[]{:S(2)}) async-start(bf16[8,96,640]{2,1,0:T(8,128)(2,1)} %bitcast.8), calls=%async_computation.3 | async-start | bytes 1966080 | tf_op jit(solution)/shard_map/all_to_all | solution.py:246
  141.7 12.8 %multiply.3 = bf16[4,384,640]{2,1,0:T(8,128)(2,1)} custom-call(s32[2]{0:T(128)} %pad_add_fusion.flags, bf16[16,384,512]{2,1,0:T(8,128)(2,1)} %bitcast.21, bf16[1024,640]{1,0:T(8,128)(2,1)} %own_ref.3, bf16[512,640]{1,0:T(8,128)(2,1)} %copy-done.10, bf16[512,640]{1,0:T(8,128)(2,1)} %copy-done.6, bf16[768,640]{1,0:T(8,128)(2,1)} %up.1.refs_0_), custom_call_target="tpu_custom_call" | custom-call | flops 8000000000 | bytes 16777216 | tf_op jit(solution)/shard_map/multiply/pallas_call | solution.py:83
  154.5 9.0 %all-to-all-done.3 = bf16[8,96,640]{2,1,0:T(8,128)(2,1)S(1)} async-done(((bf16[8,96,640]{2,1,0:T(8,128)(2,1)}), bf16[8,96,640]{2,1,0:T(8,128)(2,1)S(1)}, u32[]{:S(2)}, u32[]{:S(2)}) %all-to-all-start.3) | async-done | bytes 983072 | tf_op jit(solution)/shard_map/all_to_all | solution.py:246
  163.6 27.6 %all_to_all.25 = bf16[4,384,640]{2,1,0:T(8,128)(2,1)S(1)} all-to-all(bf16[4,384,640]{2,1,0:T(8,128)(2,1)} %multiply.3), channel_id=1, replica_groups=mesh['yh'=2,'x'=4,'z'=8,'yl'=2,'c'=2] {'x'}, dimensions={0} | all-to-all | bytes 3932160 | tf_op jit(solution)/shard_map/all_to_all | solution.py:250
  191.5 2.6 %fusion.1 = bf16[384,640]{1,0:T(8,128)(2,1)} fusion(bf16[1,384,640]{2,1,0:T(8,128)(2,1)} %reduce-scatter.2.cloned.1.call-done, f32[384,640]{1,0:T(8,128)S(1)} %convert_reduce_fusion, bf16[768,640]{1,0:T(8,128)(2,1)S(1)} %bitcast.19, s32[384]{0:T(512)S(1)} %convert_add_fusion), kind=kOutput, calls=%fused_computation.7 | convolution fusion | flops 379748352 | bytes 2950656 | tf_op jit(solution)/shard_map/dot_general | solution.py:251
  (41 shorter events, 8.9 us)
Async XLA Ops:
  6.5 103.4 %all-gather.3.cloned.1.call-start = ((), (), s32[]{:S(2)}) async-start(), calls=%async_computation.7 | async-start | bytes 6684672 | tf_op jit(solution)/shard_map/all_gather | solution.py:209
  6.5 7.1 %collective-permute-start = (bf16[384,256]{1,0:T(8,128)(2,1)}, bf16[384,256]{1,0:T(8,128)(2,1)S(1)}, u32[]{:S(2)}, u32[]{:S(2)}) collective-permute-start(bf16[384,256]{1,0:T(8,128)(2,1)} %param.6), channel_id=1, source_target_pairs={{0,0},{2,2},{4,32},{6,34},{8,64},{10,66},{12,96},{14,98},{16,16},{... | collective-permute-start | bytes 589832 | tf_op jit(solution)/shard_map/ppermute | solution.py:184
  8.1 5.8 %collective-permute-start.1 = (bf16[384,256]{1,0:T(8,128)(2,1)}, bf16[384,256]{1,0:T(8,128)(2,1)S(1)}, u32[]{:S(2)}, u32[]{:S(2)}) collective-permute-start(bf16[384,256]{1,0:T(8,128)(2,1)} %param.6), channel_id=1, source_target_pairs={{0,2},{2,0},{4,34},{6,32},{8,66},{10,64},{12,98},{14,96},{16,18},{... | collective-permute-start | bytes 589832 | tf_op jit(solution)/shard_map/ppermute | solution.py:185
  11.3 3.5 %copy-start.7 = (bf16[1024,640]{1,0:T(8,128)(2,1)S(1)}, bf16[1024,640]{1,0:T(8,128)(2,1)}, u32[]{:S(2)}) copy-start(bf16[1024,640]{1,0:T(8,128)(2,1)} %own_ref.2) | copy-start | bytes 3932164
  15.7 41.1 %collective-permute-start.4 = (bf16[512,640]{1,0:T(8,128)(2,1)}, bf16[512,640]{1,0:T(8,128)(2,1)S(1)}, u32[]{:S(2)}, u32[]{:S(2)}) collective-permute-start(bf16[512,640]{1,0:T(8,128)(2,1)} %get-tuple-element.12), channel_id=1, source_target_pairs={{0,128},{128,0},{1,129},{129,1},{2,130},{130,2},{3,131},{131,3},{4... | collective-permute-start | bytes 1966088 | tf_op jit(solution)/shard_map/ppermute | solution.py:188
  19.6 37.2 %all-to-all-start = ((bf16[8,96,384]{2,1,0:T(8,128)(2,1)}), bf16[8,96,384]{2,1,0:T(8,128)(2,1)S(1)}, u32[]{:S(2)}, u32[]{:S(2)}) async-start(bf16[8,96,384]{2,1,0:T(8,128)(2,1)} %bitcast.3), calls=%async_computation | async-start | bytes 1179648 | tf_op jit(solution)/shard_map/all_to_all | solution.py:204
  45.2 40.1 %collective-permute-start.5 = (bf16[512,640]{1,0:T(8,128)(2,1)S(1)}, bf16[512,640]{1,0:T(8,128)(2,1)}, u32[]{:S(2)}, u32[]{:S(2)}) collective-permute-start(bf16[512,640]{1,0:T(8,128)(2,1)S(1)} %get-tuple-element.11), channel_id=1, source_target_pairs={{0,128},{128,0},{1,129},{129,1},{2,130},{130,2},{3,131},{131,3},{4... | collective-permute-start | bytes 1966088 | tf_op jit(solution)/shard_map/ppermute | solution.py:188
  56.8 7.6 %copy-start.5 = (bf16[512,640]{1,0:T(8,128)(2,1)}, bf16[512,640]{1,0:T(8,128)(2,1)S(1)}, u32[]{:S(2)}) copy-start(bf16[512,640]{1,0:T(8,128)(2,1)S(1)} %collective-permute-done.4._.far_low) | copy-start | bytes 1966084
  56.8 1.8 copy-start.4
  58.6 23.1 %copy-start.8 = (bf16[1024,640]{1,0:T(8,128)(2,1)S(1)}, bf16[1024,640]{1,0:T(8,128)(2,1)}, u32[]{:S(2)}) copy-start(bf16[1024,640]{1,0:T(8,128)(2,1)} %own_ref.3) | copy-start | bytes 3932164
  64.4 28.8 %all-to-all-start.1 = ((f32[32,16,128]{2,1,0:T(8,128)}), f32[32,16,128]{2,1,0:T(8,128)S(1)}, u32[]{:S(2)}, u32[]{:S(2)}) async-start(f32[32,16,128]{2,1,0:T(8,128)} %down.1), calls=%async_computation.1 | async-start | bytes 524288 | tf_op jit(solution)/shard_map/all_to_all | solution.py:221
  82.7 21.1 %collective-permute-start.2 = (bf16[512,640]{1,0:T(8,128)(2,1)S(1)}, bf16[512,640]{1,0:T(8,128)(2,1)S(1)}, u32[]{:S(2)}, u32[]{:S(2)}) collective-permute-start(bf16[512,640]{1,0:T(8,128)(2,1)S(1)} %get-tuple-element.14), channel_id=1, source_target_pairs={{0,128},{128,0},{1,129},{129,1},{2,130},{130,2},{3,131},{131,3},{4... | collective-permute-start | bytes 1966088 | tf_op jit(solution)/shard_map/ppermute | solution.py:188
  93.2 0.7 copy-start.9
  95.6 14.4 %all-to-all-start.2 = ((bf16[32,16,128]{2,1,0:T(8,128)(2,1)}), bf16[32,16,128]{2,1,0:T(8,128)(2,1)S(1)}, u32[]{:S(2)}, u32[]{:S(2)}) async-start(bf16[32,16,128]{2,1,0:T(8,128)(2,1)} %sum.1), calls=%async_computation.2 | async-start | bytes 262144 | tf_op jit(solution)/shard_map/all_to_all | solution.py:230
  100.6 90.9 %reduce-scatter.2.cloned.1.call-start = ((), (), s32[]{:S(2)}) async-start(), calls=%async_computation.6 | async-start | bytes 2457600 | tf_op jit(solution)/shard_map/reduce_scatter | solution.py:232
  100.6 22.7 %collective-permute-start.3 = (bf16[512,640]{1,0:T(8,128)(2,1)}, bf16[512,640]{1,0:T(8,128)(2,1)S(1)}, u32[]{:S(2)}, u32[]{:S(2)}) collective-permute-start(bf16[512,640]{1,0:T(8,128)(2,1)} %get-tuple-element.13), channel_id=1, source_target_pairs={{0,128},{128,0},{1,129},{129,1},{2,130},{130,2},{3,131},{131,3},{4... | collective-permute-start | bytes 1966088 | tf_op jit(solution)/shard_map/ppermute | solution.py:188
  103.8 6.1 %copy-start.10 = (bf16[512,640]{1,0:T(8,128)(2,1)}, bf16[512,640]{1,0:T(8,128)(2,1)S(1)}, u32[]{:S(2)}) copy-start(bf16[512,640]{1,0:T(8,128)(2,1)S(1)} %collective-permute-done.2.refs_1_.far_low) | copy-start | bytes 1966084
  109.9 0.7 copy-start.1
  123.3 1.8 copy-start
  123.4 11.7 %copy-start.6 = (bf16[512,640]{1,0:T(8,128)(2,1)}, bf16[512,640]{1,0:T(8,128)(2,1)S(1)}, u32[]{:S(2)}) copy-start(bf16[512,640]{1,0:T(8,128)(2,1)S(1)} %collective-permute-done.3.__.far_high) | copy-start | bytes 1966084
  125.1 0.9 copy-start.2
  126.0 2.5 %copy-start.3 = (bf16[64,64,640]{2,1,0:T(8,128)(2,1)S(1)}, bf16[64,64,640]{2,1,0:T(8,128)(2,1)}, u32[]{:S(2)}) copy-start(bf16[64,64,640]{2,1,0:T(8,128)(2,1)} %param.11) | copy-start | bytes 15728644
  135.0 28.5 %all-to-all-start.3 = ((bf16[8,96,640]{2,1,0:T(8,128)(2,1)}), bf16[8,96,640]{2,1,0:T(8,128)(2,1)S(1)}, u32[]{:S(2)}, u32[]{:S(2)}) async-start(bf16[8,96,640]{2,1,0:T(8,128)(2,1)} %bitcast.8), calls=%async_computation.3 | async-start | bytes 1966080 | tf_op jit(solution)/shard_map/all_to_all | solution.py:246
Sparse Core Ops, SparseCore 0:
  14.9 74.9 all-gather.2
  123.5 37.7 reduce-scatter.1

commit v3 on v2

--- a/solution.py
+++ b/solution.py
@@ -1,3 +1,5 @@
+import functools
+
 import jax
 import jax.numpy as jnp
 from jax import lax
@@ -30,9 +32,15 @@
     return pairs
 
 
-def multiply_kernel(flags, rows_ref, own_ref, far_low, far_high, *refs):
-    out_ref, lhs, rhs, lhs_sems, rhs_sems = refs[-5:]
-    yh, yl = flags[0], flags[1]
+def multiply_kernel(shifts, flags, rows_ref, own_ref, far_low, far_high, *refs):
+    lhs, rhs, lhs_sems, rhs_sems = refs[-4:]
+    yh, yl, here = flags[0], flags[1], flags[2]
+    count = lhs.shape[0]
+    if shifts is None:
+        groups, outs = range(count), [refs[-5].at[n] for n in range(count)]
+    else:
+        groups = [lax.rem(here + shift, NX) for shift in shifts]
+        outs = refs[-4 - count : -4]
     depth = own_ref.shape[0]
     width = depth // 4
     weights = []
@@ -56,39 +64,45 @@
         [
             pltpu.make_async_copy(
                 rows_ref.at[(h * NX + x) * 2 + core],
-                lhs.at[x, :, pl.ds((h * 2 + core) * 2 * width, 2 * width)],
-                lhs_sems.at[x, h * 2 + core],
+                lhs.at[n, :, pl.ds((h * 2 + core) * 2 * width, 2 * width)],
+                lhs_sems.at[n, h * 2 + core],
             )
             for h in range(2)
             for core in range(2)
         ]
-        for x in range(NX)
+        for n, x in enumerate(groups)
     ]
     for copies in rows:
         for copy in copies:
             copy.start()
     for copy in weights:
         copy.wait()
-    for x, copies in enumerate(rows):
+    for n, copies in enumerate(rows):
         for copy in copies:
             copy.wait()
-        out_ref[x] = jnp.dot(
-            lhs[x], rhs[...], preferred_element_type=jnp.float32
+        outs[n][...] = jnp.dot(
+            lhs[n], rhs[...], preferred_element_type=jnp.float32
         ).astype(jnp.bfloat16)
 
 
-def multiply(rows, weights, weights_far, flags, *others):
-    count = rows.shape[1]
+def multiply(rows, weights, weights_far, flags, shifts, *others):
+    size = rows.shape[1]
     depth, hidden = weights.shape
+    count = NX if shifts is None else len(shifts)
+    if shifts is None:
+        outs, specs = jax.ShapeDtypeStruct((NX, size, hidden), jnp.bfloat16), VMEM_SPEC
+    else:
+        outs = [jax.ShapeDtypeStruct((size, hidden), jnp.bfloat16)] * count
+        specs = [VMEM_SPEC] * count
     return pl.pallas_call(
-        multiply_kernel,
-        out_shape=jax.ShapeDtypeStruct((NX, count, hidden), jnp.bfloat16),
+        functools.partial(multiply_kernel, shifts),
+        out_shape=outs,
         in_specs=[pl.BlockSpec(memory_space=pltpu.SMEM)] + [HBM_SPEC] * (4 + len(others)),
-        out_specs=VMEM_SPEC,
+        out_specs=specs,
         scratch_shapes=[
-            pltpu.VMEM((NX, count, 2 * depth), jnp.bfloat16),
+            pltpu.VMEM((count, size, 2 * depth), jnp.bfloat16),
             pltpu.VMEM((2 * depth, hidden), jnp.bfloat16),
-            pltpu.SemaphoreType.DMA((NX, 4)),
+            pltpu.SemaphoreType.DMA((count, 4)),
             pltpu.SemaphoreType.DMA((8,)),
         ],
         compiler_params=pltpu.CompilerParams(vmem_limit_bytes=56 * 2**20),
@@ -137,12 +151,14 @@
     out_ref[:, 8:, :] = jnp.where(left, low[:, 8:], 0.0)
 
 
-def sum_kernel(parts_ref, _, out_ref):
+def sum_kernel(parts_ref, *refs):
+    out_ref = refs[-1]
     total = jnp.sum(parts_ref[...], axis=0).astype(jnp.bfloat16)
     out_ref[...] = jnp.broadcast_to(total[None], out_ref.shape)
 
 
-def up_kernel(rank_ref, recv_ref, up_ref, _, __, out_ref, whole, spread):
+def up_kernel(rank_ref, recv_ref, up_ref, *refs):
+    out_ref, whole, spread = refs[-3:]
     slots, rank = recv_ref.shape[0], 64
     n = rank_ref.shape[0]
     packed = rank_ref[...].astype(jnp.float32)
@@ -179,7 +195,7 @@
     per_owner, _, rank = adapter_down.shape
     capacity = 2 * rows // owners
     slots = owners * capacity
-    flags = jnp.stack([lax.axis_index("yh"), lax.axis_index("yl")]).astype(jnp.int32)
+    flags = jnp.stack([lax.axis_index(name) for name in ("yh", "yl", "x")]).astype(jnp.int32)
 
     mine = lax.ppermute(states, ("x", "z", "yl"), start_pairs(0))
     other = lax.ppermute(states, ("x", "z", "yl"), start_pairs(1))
@@ -219,21 +235,29 @@
         name="down",
     )(recv, jnp.transpose(adapter_down, (0, 2, 1)).reshape(per_owner * rank, width), up_far[0])
     rank_parts = lax.all_to_all(partial_rank, ADAPTER, 0, 0, tiled=True)
+    ups = multiply(gathered, proj_up, up_far, flags, None, partial_rank)
+    up_sum = lax.psum_scatter(ups, "x", scatter_dimension=0, tiled=False)
     rank_sum = pl.pallas_call(
         sum_kernel,
         out_shape=jax.ShapeDtypeStruct((n_adapter, 16, LANES), jnp.bfloat16),
-        in_specs=[VMEM_SPEC, HBM_SPEC],
+        in_specs=[VMEM_SPEC] + [HBM_SPEC] * 2,
         out_specs=VMEM_SPEC,
         cost_estimate=COST,
         name="sum",
-    )(rank_parts, up_far[1])
+    )(rank_parts, ups, gate_far[0])
     rank_half = lax.all_to_all(rank_sum, ADAPTER, 0, 0, tiled=True)
-    ups = multiply(gathered, proj_up, up_far, flags, rank_half, gate_far[0])
-    up_sum = lax.psum_scatter(ups, "x", scatter_dimension=0, tiled=False)
+
+    def send_on(part, shift):
+        return lax.ppermute(part, "x", [(i, (i + shift) % NX) for i in range(NX)])
+
+    first = multiply(gathered, proj_gate, gate_far, flags, (2, 1), rank_sum)
+    second = multiply(gathered, proj_gate, gate_far, flags, (3, 0), first[0])
+    sent = [send_on(first[0], 2), send_on(first[1], 1)]
+    gate_parts = sent + [send_on(second[0], 3), second[1]]
     offsets = pl.pallas_call(
         up_kernel,
         out_shape=jax.ShapeDtypeStruct((slots, hidden), jnp.bfloat16),
-        in_specs=[VMEM_SPEC] * 3 + [HBM_SPEC] * 2,
+        in_specs=[VMEM_SPEC] * 3 + [HBM_SPEC] * 3,
         out_specs=VMEM_SPEC,
         scratch_shapes=[
             pltpu.VMEM((slots, LANES), jnp.float32),
@@ -242,16 +266,14 @@
         compiler_params=pltpu.CompilerParams(vmem_limit_bytes=18 * 2**20),
         cost_estimate=COST,
         name="up",
-    )(rank_half, recv, adapter_up.reshape(per_owner * rank, hidden), ups, gate_far[1])
+    )(rank_half, recv, adapter_up.reshape(per_owner * rank, hidden), second[1], *sent)
     returned = lax.all_to_all(
         offsets.reshape(owners, capacity, hidden), TRUNK, 0, 0, tiled=True
     ).reshape(slots, hidden)
-    gates = multiply(gathered, proj_gate, gate_far, flags, offsets)
-    gate_parts = lax.all_to_all(after(gates, returned), "x", 0, 0, tiled=True)
     offset = lax.dot_general(
         placed, returned, (((0,), (0,)), ((), ())), preferred_element_type=jnp.float32
     )
-    gate_sum = jnp.sum(gate_parts.astype(jnp.float32), axis=0)
+    gate_sum = functools.reduce(jnp.add, [part.astype(jnp.float32) for part in gate_parts])
     return (jax.nn.silu(gate_sum + offset) * up_sum.astype(jnp.float32)).astype(jnp.bfloat16)
 
 

time: 202 us -> 206 us (1.020)
  blocking collectives: 27.6 us -> 0 us
  waiting for transfers between devices: 32.1 us -> 56.5 us
  starting transfers between devices: 70.4 us -> 74.1 us
  Pallas kernels: 39.4 us -> 42 us
    ppermute x0 -> x3, waiting for transfers between devices: none -> 31.5 us  [send_on(): return lax.ppermute(part, 'x', [(i, (i + shift) % NX) for i in range(NX)])]
    all_to_all x1 -> x0, blocking collectives: 27.6 us -> none  [on_device(): gate_parts = lax.all_to_all(after(gates, returned), 'x', 0, 0, tiled=True)]
    all_gather x1, waiting for transfers between devices: 0.01 us -> 12.3 us  [on_device(): lax.all_gather(jnp.concatenate([mine, other], axis=1), ('z', 'c'), axis=0)]
    all_to_all x1, waiting for transfers between devices: 9.03 us -> 0.01 us  [on_device(): lax.all_to_all(offsets.reshape(owners, capacity, hidden), TRUNK, 0, 0, ti...]
    all_to_all x1, waiting for transfers between devices: 7.91 us -> 0.01 us  [on_device(): rank_parts = lax.all_to_all(partial_rank, ADAPTER, 0, 0, tiled=True)]
    ppermute x4, waiting for transfers between devices: 0.01 us -> 7.1 us  [on_device(): lax.ppermute(part, 'yh', SWAP)]
    ppermute x0 -> x3, starting transfers between devices: none -> 6.79 us  [send_on(): return lax.ppermute(part, 'x', [(i, (i + shift) % NX) for i in range(NX)])]
    all_to_all x1, waiting for transfers between devices: 6.12 us -> 0.01 us  [on_device(): rank_half = lax.all_to_all(rank_sum, ADAPTER, 0, 0, tiled=True)]
  transfers between devices with their start and end apart: 12 -> 15, of which waited for: 5 -> 7; matrix products, arithmetic and copies ran while one was open for 3% -> 4% of each run, Pallas kernels for 20% -> 21%
where the time goes in v3:
time: 206 us; the launch traced here: 204 us
  starting transfers between devices  74.1 us (36%)
  waiting for transfers between devices  56.5 us (27%)
  Pallas kernels  42 us (20%)
  between operations  13.5 us (7%)
  local copies, waits for them, and re-layouts  9.89 us (5%)
  matrix products  5.49 us (3%)
  other arithmetic  2.12 us (1%)
    ppermute x3, waiting for transfers between devices, send_on(): return lax.ppermute(part, 'x', [(i, (i + shift) % NX) for i in range(NX)])  31.5 us
    pallas_call x3, Pallas kernels, multiply(): pl.pallas_call(functools.partial(multiply_kernel, shifts), out_shape=outs...  28.1 us
    all_to_all x1, starting transfers between devices, on_device(): lax.all_to_all(send.reshape(owners, capacity, width + LANES), TRUNK, 0, 0...  25.5 us
    all_to_all x1, starting transfers between devices, on_device(): rank_parts = lax.all_to_all(partial_rank, ADAPTER, 0, 0, tiled=True)  17.3 us
    all_gather x1, waiting for transfers between devices, on_device(): lax.all_gather(jnp.concatenate([mine, other], axis=1), ('z', 'c'), axis=0)  12.3 us
    ppermute x4, starting transfers between devices, on_device(): lax.ppermute(part, 'yh', SWAP)  9.85 us
    ppermute x4, waiting for transfers between devices, on_device(): lax.ppermute(part, 'yh', SWAP)  7.1 us
    ppermute x3, starting transfers between devices, send_on(): return lax.ppermute(part, 'x', [(i, (i + shift) % NX) for i in range(NX)])  6.79 us
  transfers between devices with their start and end apart: 15, of which 7 were waited for; matrix products, arithmetic and copies ran while one was open for 4% of the time, Pallas kernels for 21%

profile of v3, /device:TPU:1, one launch (start us, length us, event | category | flops | bytes accessed | tf_op | source)
XLA Modules:
  0.0 203.7 jit_solution(4133830974761210573)
XLA Ops:
  8.1 2.1 %collective-permute-start.1 = (bf16[384,256]{1,0:T(8,128)(2,1)}, bf16[384,256]{1,0:T(8,128)(2,1)S(1)}, u32[]{:S(2)}, u32[]{:S(2)}) collective-permute-start(bf16[384,256]{1,0:T(8,128)(2,1)} %param.6), channel_id=1, source_target_pairs={{0,2},{2,0},{4,34},{6,32},{8,66},{10,64},{12,98},{14,96},{16,18},{... | collective-permute-start | bytes 589832 | tf_op jit(solution)/shard_map/ppermute | solution.py:201
  11.3 2.4 %convolution_convert_fusion = bf16[768,384]{1,0:T(8,128)(2,1)} fusion(s32[384]{0:T(512)S(1)} %convert_add_fusion, bf16[384,128]{1,0:T(8,128)(2,1)S(1)} %broadcast_in_dim.7, bf16[384,256]{1,0:T(8,128)(2,1)} %param.6), kind=kOutput, calls=%fused_computation | convolution fusion | flops 227672064 | bytes 886272 | tf_op jit(solution)/shard_map/dot_general | solution.py:219
  15.9 3.9 %collective-permute-start.4 = (bf16[512,640]{1,0:T(8,128)(2,1)}, bf16[512,640]{1,0:T(8,128)(2,1)S(1)}, u32[]{:S(2)}, u32[]{:S(2)}) collective-permute-start(bf16[512,640]{1,0:T(8,128)(2,1)} %get-tuple-element.20), channel_id=1, source_target_pairs={{0,128},{128,0},{1,129},{129,1},{2,130},{130,2},{3,131},{131,3},{4... | collective-permute-start | bytes 1966088 | tf_op jit(solution)/shard_map/ppermute | solution.py:204
  19.8 25.5 %all-to-all-start = ((bf16[8,96,384]{2,1,0:T(8,128)(2,1)}), bf16[8,96,384]{2,1,0:T(8,128)(2,1)S(1)}, u32[]{:S(2)}, u32[]{:S(2)}) async-start(bf16[8,96,384]{2,1,0:T(8,128)(2,1)} %bitcast.4), calls=%async_computation | async-start | bytes 1179648 | tf_op jit(solution)/shard_map/all_to_all | solution.py:220
  45.4 3.0 %collective-permute-start.5 = (bf16[512,640]{1,0:T(8,128)(2,1)}, bf16[512,640]{1,0:T(8,128)(2,1)}, u32[]{:S(2)}, u32[]{:S(2)}) collective-permute-start(bf16[512,640]{1,0:T(8,128)(2,1)} %get-tuple-element.19), channel_id=1, source_target_pairs={{0,128},{128,0},{1,129},{129,1},{2,130},{130,2},{3,131},{131,3},{4... | collective-permute-start | bytes 1966088 | tf_op jit(solution)/shard_map/ppermute | solution.py:204
  48.3 2.5 %fusion.13 = (bf16[512,640]{1,0:T(8,128)(2,1)}, bf16[512,640]{1,0:T(8,128)(2,1)}) fusion(bf16[1024,640]{1,0:T(8,128)(2,1)} %own_ref.5), kind=kLoop, calls=%fused_computation.29 | loop fusion | bytes 2621440 | tf_op jit(solution)/shard_map/slice | solution.py:204
  51.7 5.3 %all-to-all-done = bf16[8,96,384]{2,1,0:T(8,128)(2,1)S(1)} async-done(((bf16[8,96,384]{2,1,0:T(8,128)(2,1)}), bf16[8,96,384]{2,1,0:T(8,128)(2,1)S(1)}, u32[]{:S(2)}, u32[]{:S(2)}) %all-to-all-start) | async-done | bytes 589856 | tf_op jit(solution)/shard_map/all_to_all | solution.py:220
  57.0 5.7 %down.1.refs_0_ = f32[32,16,128]{2,1,0:T(8,128)} custom-call(bf16[768,384]{1,0:T(8,128)(2,1)S(1)} %bitcast.16, bf16[4096,256]{1,0:T(8,128)(2,1)S(1)} %bitcast.19, bf16[512,640]{1,0:T(8,128)(2,1)S(1)} %collective-permute-done.4._.far_low), custom_call_target="tpu_custom_call" | custom-call | flops 8000000000 | bytes 16777216 | tf_op jit(solution)/shard_map/down/pallas_call | solution.py:227
  62.7 17.3 %all-to-all-start.1 = ((f32[32,16,128]{2,1,0:T(8,128)}), f32[32,16,128]{2,1,0:T(8,128)S(1)}, u32[]{:S(2)}, u32[]{:S(2)}) async-start(f32[32,16,128]{2,1,0:T(8,128)} %down.1.refs_0_), calls=%async_computation.1 | async-start | bytes 524288 | tf_op jit(solution)/shard_map/all_to_all | solution.py:237
  80.1 12.3 %all-gather.3.cloned.1.call-done = bf16[6144,512]{1,0:T(8,128)(2,1)} async-done(((bf16[384,512]{1,0:T(8,128)(2,1)}), bf16[6144,512]{1,0:T(8,128)(2,1)}) %all-gather.3.cloned.1.call-update) | async-done | bytes 6291472 | tf_op jit(solution)/shard_map/all_gather | solution.py:225
  92.4 12.7 %multiply.3.refs_0_ = bf16[4,384,640]{2,1,0:T(8,128)(2,1)} custom-call(s32[3]{0:T(128)} %pad_add_fusion.flags, bf16[16,384,512]{2,1,0:T(8,128)(2,1)} %bitcast.21, bf16[1024,640]{1,0:T(8,128)(2,1)} %own_ref.3, bf16[512,640]{1,0:T(8,128)(2,1)} %copy-done.2, bf16[512,640]{1,0:T(8,128)(2,1)} %collective-permute-done.5.far_high, f32[32,16,128]{2,1,0:T(8,128)} %down.1.refs_0_), custom_call_target="tpu_custom_call" | custom-call | flops 8000000000 | bytes 16777216 | tf_op jit(solution)/shard_map/multiply/pallas_call | solution.py:97
  106.2 2.8 %collective-permute-start.3 = (bf16[512,640]{1,0:T(8,128)(2,1)S(1)}, bf16[512,640]{1,0:T(8,128)(2,1)S(1)}, u32[]{:S(2)}, u32[]{:S(2)}) collective-permute-start(bf16[512,640]{1,0:T(8,128)(2,1)S(1)} %copy-done.6), channel_id=1, source_target_pairs={{0,128},{128,0},{1,129},{129,1},{2,130},{130,2},{3,131},{131,3},{4... | collective-permute-start | bytes 1966088 | tf_op jit(solution)/shard_map/ppermute | solution.py:204
  111.3 6.1 %all-to-all-start.2 = ((bf16[32,16,128]{2,1,0:T(8,128)(2,1)}), bf16[32,16,128]{2,1,0:T(8,128)(2,1)S(1)}, u32[]{:S(2)}, u32[]{:S(2)}) async-start(bf16[32,16,128]{2,1,0:T(8,128)(2,1)} %sum.1.refs_0_), calls=%async_computation.2 | async-start | bytes 262144 | tf_op jit(solution)/shard_map/all_to_all | solution.py:248
  117.5 7.1 %collective-permute-done.3.far_high = bf16[512,640]{1,0:T(8,128)(2,1)S(1)} collective-permute-done((bf16[512,640]{1,0:T(8,128)(2,1)S(1)}, bf16[512,640]{1,0:T(8,128)(2,1)S(1)}, u32[]{:S(2)}, u32[]{:S(2)}) %collective-permute-start.3) | collective-permute-done | bytes 655392 | tf_op jit(solution)/shard_map/ppermute | solution.py:204
  125.4 7.7 %multiply.4 = (bf16[384,640]{1,0:T(8,128)(2,1)}, bf16[384,640]{1,0:T(8,128)(2,1)}) custom-call(s32[3]{0:T(128)} %pad_add_fusion.flags, bf16[16,384,512]{2,1,0:T(8,128)(2,1)} %bitcast.22, bf16[1024,640]{1,0:T(8,128)(2,1)} %own_ref.5, bf16[512,640]{1,0:T(8,128)(2,1)} %collective-permute-done.2.refs_1_.far_low, bf16[512,640]{1,0:T(8,128)(2,1)} %copy-done.8, ...), custom_call_target="tpu_custom_call" | custom-call | flops 8000000000 | bytes 16777216 | tf_op jit(solution)/shard_map/multiply/pallas_call | solution.py:97
  133.2 4.0 %collective-permute-start.6 = (bf16[384,640]{1,0:T(8,128)(2,1)}, bf16[384,640]{1,0:T(8,128)(2,1)S(1)}, u32[]{:S(2)}, u32[]{:S(2)}) collective-permute-start(bf16[384,640]{1,0:T(8,128)(2,1)} %get-tuple-element.13.refs_0_), channel_id=1, source_target_pairs={{0,64},{32,96},{64,0},{96,32},{1,65},{33,97},{65,1},{97,33},{2,66}... | collective-permute-start | bytes 1474568 | tf_op jit(solution)/shard_map/ppermute | solution.py:251
  137.2 7.6 %multiply.5 = (bf16[384,640]{1,0:T(8,128)(2,1)}, bf16[384,640]{1,0:T(8,128)(2,1)}) custom-call(s32[3]{0:T(128)} %pad_add_fusion.flags, bf16[16,384,512]{2,1,0:T(8,128)(2,1)} %bitcast.23, bf16[1024,640]{1,0:T(8,128)(2,1)} %own_ref.5, bf16[512,640]{1,0:T(8,128)(2,1)} %collective-permute-done.2.refs_1_.far_low, bf16[512,640]{1,0:T(8,128)(2,1)} %copy-done.8, ...), custom_call_target="tpu_custom_call" | custom-call | flops 8000000000 | bytes 16777216 | tf_op jit(solution)/shard_map/multiply/pallas_call | solution.py:97
  146.3 11.6 %collective-permute-done.6.refs_1_ = bf16[384,640]{1,0:T(8,128)(2,1)S(1)} collective-permute-done((bf16[384,640]{1,0:T(8,128)(2,1)}, bf16[384,640]{1,0:T(8,128)(2,1)S(1)}, u32[]{:S(2)}, u32[]{:S(2)}) %collective-permute-start.6) | collective-permute-done | bytes 491552 | tf_op jit(solution)/shard_map/ppermute | solution.py:251
  157.9 2.5 %copy-done = bf16[64,64,640]{2,1,0:T(8,128)(2,1)S(1)} copy-done((bf16[64,64,640]{2,1,0:T(8,128)(2,1)S(1)}, bf16[64,64,640]{2,1,0:T(8,128)(2,1)}, u32[]{:S(2)}) %copy-start) | copy-done | bytes 5242904
  161.4 6.5 %up.1 = bf16[768,640]{1,0:T(8,128)(2,1)} custom-call(bf16[32,16,128]{2,1,0:T(8,128)(2,1)S(1)} %all-to-all-done.2.rank_ref, bf16[768,384]{1,0:T(8,128)(2,1)S(1)} %bitcast.17, bf16[4096,640]{1,0:T(8,128)(2,1)S(1)} %bitcast.18, bf16[384,640]{1,0:T(8,128)(2,1)S(1)} %copy-done.3, bf16[384,640]{1,0:T(8,128)(2,1)S(1)} %collective-permute-done.6.refs_1_, ...), custom_call_target="tpu_custom_call" | custom-call | flops 8000000000 | bytes 16777216 | tf_op jit(solution)/shard_map/up/pallas_call | solution.py:257
  167.9 4.8 %all-to-all-start.3 = ((bf16[8,96,640]{2,1,0:T(8,128)(2,1)}), bf16[8,96,640]{2,1,0:T(8,128)(2,1)S(1)}, u32[]{:S(2)}, u32[]{:S(2)}) async-start(bf16[8,96,640]{2,1,0:T(8,128)(2,1)} %bitcast.9), calls=%async_computation.3 | async-start | bytes 1966080 | tf_op jit(solution)/shard_map/all_to_all | solution.py:270
  172.7 2.7 %collective-permute-start.8 = (bf16[384,640]{1,0:T(8,128)(2,1)S(1)}, bf16[384,640]{1,0:T(8,128)(2,1)}, u32[]{:S(2)}, u32[]{:S(2)}) collective-permute-start(bf16[384,640]{1,0:T(8,128)(2,1)S(1)} %copy-done.9), channel_id=1, source_target_pairs={{0,96},{32,0},{64,32},{96,64},{1,97},{33,1},{65,33},{97,65},{2,98}... | collective-permute-start | bytes 1474568 | tf_op jit(solution)/shard_map/ppermute | solution.py:251
  175.4 18.5 %collective-permute-done.8 = bf16[384,640]{1,0:T(8,128)(2,1)} collective-permute-done((bf16[384,640]{1,0:T(8,128)(2,1)S(1)}, bf16[384,640]{1,0:T(8,128)(2,1)}, u32[]{:S(2)}, u32[]{:S(2)}) %collective-permute-start.8) | collective-permute-done | bytes 491552 | tf_op jit(solution)/shard_map/ppermute | solution.py:251
  193.9 2.9 %fusion.2 = bf16[384,640]{1,0:T(8,128)(2,1)} fusion(bf16[384,640]{1,0:T(8,128)(2,1)S(1)} %copy-done.4, bf16[384,640]{1,0:T(8,128)(2,1)} %collective-permute-done.8, bf16[384,640]{1,0:T(8,128)(2,1)S(1)} %collective-permute-done.7.refs_2_, bf16[384,640]{1,0:T(8,128)(2,1)S(1)} %collective-permute-done.6.refs_1_, ...), kind=kOutput, calls=%fused_computation.6 | convolution fusion | flops 381468672 | bytes 3933696 | tf_op jit(solution)/shard_map/dot_general | solution.py:273
  (44 shorter events, 12.6 us)
Async XLA Ops:
  6.5 85.8 %all-gather.3.cloned.1.call-start = ((), (), s32[]{:S(2)}) async-start(), calls=%async_computation.6 | async-start | bytes 6684672 | tf_op jit(solution)/shard_map/all_gather | solution.py:225
  6.5 7.1 %collective-permute-start = (bf16[384,256]{1,0:T(8,128)(2,1)}, bf16[384,256]{1,0:T(8,128)(2,1)S(1)}, u32[]{:S(2)}, u32[]{:S(2)}) collective-permute-start(bf16[384,256]{1,0:T(8,128)(2,1)} %param.6), channel_id=1, source_target_pairs={{0,0},{2,2},{4,32},{6,34},{8,64},{10,66},{12,96},{14,98},{16,16},{... | collective-permute-start | bytes 589832 | tf_op jit(solution)/shard_map/ppermute | solution.py:200
  8.1 5.8 %collective-permute-start.1 = (bf16[384,256]{1,0:T(8,128)(2,1)}, bf16[384,256]{1,0:T(8,128)(2,1)S(1)}, u32[]{:S(2)}, u32[]{:S(2)}) collective-permute-start(bf16[384,256]{1,0:T(8,128)(2,1)} %param.6), channel_id=1, source_target_pairs={{0,2},{2,0},{4,34},{6,32},{8,66},{10,64},{12,98},{14,96},{16,18},{... | collective-permute-start | bytes 589832 | tf_op jit(solution)/shard_map/ppermute | solution.py:201
  11.3 3.5 %copy-start.5 = (bf16[1024,640]{1,0:T(8,128)(2,1)S(1)}, bf16[1024,640]{1,0:T(8,128)(2,1)}, u32[]{:S(2)}) copy-start(bf16[1024,640]{1,0:T(8,128)(2,1)} %own_ref.3) | copy-start | bytes 3932164
  15.9 41.1 %collective-permute-start.4 = (bf16[512,640]{1,0:T(8,128)(2,1)}, bf16[512,640]{1,0:T(8,128)(2,1)S(1)}, u32[]{:S(2)}, u32[]{:S(2)}) collective-permute-start(bf16[512,640]{1,0:T(8,128)(2,1)} %get-tuple-element.20), channel_id=1, source_target_pairs={{0,128},{128,0},{1,129},{129,1},{2,130},{130,2},{3,131},{131,3},{4... | collective-permute-start | bytes 1966088 | tf_op jit(solution)/shard_map/ppermute | solution.py:204
  19.8 37.2 %all-to-all-start = ((bf16[8,96,384]{2,1,0:T(8,128)(2,1)}), bf16[8,96,384]{2,1,0:T(8,128)(2,1)S(1)}, u32[]{:S(2)}, u32[]{:S(2)}) async-start(bf16[8,96,384]{2,1,0:T(8,128)(2,1)} %bitcast.4), calls=%async_computation | async-start | bytes 1179648 | tf_op jit(solution)/shard_map/all_to_all | solution.py:220
  45.4 11.6 %copy-start.1 = (bf16[64,256,64]{1,2,0:T(8,128)(2,1)S(1)}, bf16[64,256,64]{1,2,0:T(8,128)(2,1)}, u32[]{:S(2)}) copy-start(bf16[64,256,64]{1,2,0:T(8,128)(2,1)} %param.10) | copy-start | bytes 6291460
  45.4 34.7 %collective-permute-start.5 = (bf16[512,640]{1,0:T(8,128)(2,1)}, bf16[512,640]{1,0:T(8,128)(2,1)}, u32[]{:S(2)}, u32[]{:S(2)}) collective-permute-start(bf16[512,640]{1,0:T(8,128)(2,1)} %get-tuple-element.19), channel_id=1, source_target_pairs={{0,128},{128,0},{1,129},{129,1},{2,130},{130,2},{3,131},{131,3},{4... | collective-permute-start | bytes 1966088 | tf_op jit(solution)/shard_map/ppermute | solution.py:204
  50.8 58.1 %collective-permute-start.2 = (bf16[512,640]{1,0:T(8,128)(2,1)}, bf16[512,640]{1,0:T(8,128)(2,1)}, u32[]{:S(2)}, u32[]{:S(2)}) collective-permute-start(bf16[512,640]{1,0:T(8,128)(2,1)} %get-tuple-element.18), channel_id=1, source_target_pairs={{0,128},{128,0},{1,129},{129,1},{2,130},{130,2},{3,131},{131,3},{4... | collective-permute-start | bytes 1966088 | tf_op jit(solution)/shard_map/ppermute | solution.py:204
  57.0 5.7 %copy-start.2 = (bf16[512,640]{1,0:T(8,128)(2,1)}, bf16[512,640]{1,0:T(8,128)(2,1)S(1)}, u32[]{:S(2)}) copy-start(bf16[512,640]{1,0:T(8,128)(2,1)S(1)} %collective-permute-done.4._.far_low) | copy-start | bytes 1966084
  62.7 46.2 %all-to-all-start.1 = ((f32[32,16,128]{2,1,0:T(8,128)}), f32[32,16,128]{2,1,0:T(8,128)S(1)}, u32[]{:S(2)}, u32[]{:S(2)}) async-start(f32[32,16,128]{2,1,0:T(8,128)} %down.1.refs_0_), calls=%async_computation.1 | async-start | bytes 524288 | tf_op jit(solution)/shard_map/all_to_all | solution.py:237
  80.0 113.9 %reduce-scatter.2.cloned.1.call-start = ((), (), s32[]{:S(2)}) async-start(), calls=%async_computation.5 | async-start | bytes 2457600 | tf_op jit(solution)/shard_map/reduce_scatter | solution.py:239
  105.1 1.1 copy-start.6
  106.2 18.4 %collective-permute-start.3 = (bf16[512,640]{1,0:T(8,128)(2,1)S(1)}, bf16[512,640]{1,0:T(8,128)(2,1)S(1)}, u32[]{:S(2)}, u32[]{:S(2)}) collective-permute-start(bf16[512,640]{1,0:T(8,128)(2,1)S(1)} %copy-done.6), channel_id=1, source_target_pairs={{0,128},{128,0},{1,129},{129,1},{2,130},{130,2},{3,131},{131,3},{4... | collective-permute-start | bytes 1966088 | tf_op jit(solution)/shard_map/ppermute | solution.py:204
  111.3 33.6 %all-to-all-start.2 = ((bf16[32,16,128]{2,1,0:T(8,128)(2,1)}), bf16[32,16,128]{2,1,0:T(8,128)(2,1)S(1)}, u32[]{:S(2)}, u32[]{:S(2)}) async-start(bf16[32,16,128]{2,1,0:T(8,128)(2,1)} %sum.1.refs_0_), calls=%async_computation.2 | async-start | bytes 262144 | tf_op jit(solution)/shard_map/all_to_all | solution.py:248
  124.6 0.8 copy-start.8
  133.1 13.2 %collective-permute-start.7 = (bf16[384,640]{1,0:T(8,128)(2,1)}, bf16[384,640]{1,0:T(8,128)(2,1)S(1)}, u32[]{:S(2)}, u32[]{:S(2)}) collective-permute-start(bf16[384,640]{1,0:T(8,128)(2,1)} %get-tuple-element.14), channel_id=1, source_target_pairs={{0,32},{32,64},{64,96},{96,0},{1,33},{33,65},{65,97},{97,1},{2,34}... | collective-permute-start | bytes 1474568 | tf_op jit(solution)/shard_map/ppermute | solution.py:251
  133.2 24.7 %collective-permute-start.6 = (bf16[384,640]{1,0:T(8,128)(2,1)}, bf16[384,640]{1,0:T(8,128)(2,1)S(1)}, u32[]{:S(2)}, u32[]{:S(2)}) collective-permute-start(bf16[384,640]{1,0:T(8,128)(2,1)} %get-tuple-element.13.refs_0_), channel_id=1, source_target_pairs={{0,64},{32,96},{64,0},{96,32},{1,65},{33,97},{65,1},{97,33},{2,66}... | collective-permute-start | bytes 1474568 | tf_op jit(solution)/shard_map/ppermute | solution.py:251
  157.9 2.5 %copy-start = (bf16[64,64,640]{2,1,0:T(8,128)(2,1)S(1)}, bf16[64,64,640]{2,1,0:T(8,128)(2,1)}, u32[]{:S(2)}) copy-start(bf16[64,64,640]{2,1,0:T(8,128)(2,1)} %param.11) | copy-start | bytes 15728644
  160.3 1.0 copy-start.3
  167.9 4.8 %copy-start.9 = (bf16[384,640]{1,0:T(8,128)(2,1)S(1)}, bf16[384,640]{1,0:T(8,128)(2,1)}, u32[]{:S(2)}) copy-start(bf16[384,640]{1,0:T(8,128)(2,1)} %get-tuple-element.15) | copy-start | bytes 1474564
  167.9 26.0 %copy-start.4 = (bf16[384,640]{1,0:T(8,128)(2,1)S(1)}, bf16[384,640]{1,0:T(8,128)(2,1)}, u32[]{:S(2)}) copy-start(bf16[384,640]{1,0:T(8,128)(2,1)} %get-tuple-element.16.refs_0_) | copy-start | bytes 1474564
  167.9 26.0 %all-to-all-start.3 = ((bf16[8,96,640]{2,1,0:T(8,128)(2,1)}), bf16[8,96,640]{2,1,0:T(8,128)(2,1)S(1)}, u32[]{:S(2)}, u32[]{:S(2)}) async-start(bf16[8,96,640]{2,1,0:T(8,128)(2,1)} %bitcast.9), calls=%async_computation.3 | async-start | bytes 1966080 | tf_op jit(solution)/shard_map/all_to_all | solution.py:270
  172.7 21.2 %collective-permute-start.8 = (bf16[384,640]{1,0:T(8,128)(2,1)S(1)}, bf16[384,640]{1,0:T(8,128)(2,1)}, u32[]{:S(2)}, u32[]{:S(2)}) collective-permute-start(bf16[384,640]{1,0:T(8,128)(2,1)S(1)} %copy-done.9), channel_id=1, source_target_pairs={{0,96},{32,0},{64,32},{96,64},{1,97},{33,1},{65,33},{97,65},{2,98}... | collective-permute-start | bytes 1474568 | tf_op jit(solution)/shard_map/ppermute | solution.py:251
  (1 other events, 0.7 us)
Sparse Core Ops, SparseCore 0:
  14.9 77.4 all-gather.2
  105.2 30.2 reduce-scatter.1

commit v4 on v2

--- a/solution.py
+++ b/solution.py
@@ -1,3 +1,5 @@
+import functools
+
 import jax
 import jax.numpy as jnp
 from jax import lax
@@ -10,6 +12,7 @@
 SWAP = [(0, 1), (1, 0)]
 NX, NZ = 4, 8
 LANES = 128
+NEAR = (0, 1, 2, -1)
 HBM_SPEC = pl.BlockSpec(memory_space=pltpu.HBM)
 VMEM_SPEC = pl.BlockSpec(memory_space=pltpu.VMEM)
 COST = pl.CostEstimate(flops=8 * 10**9, bytes_accessed=16 * 2**20, transcendentals=0)
@@ -25,76 +28,94 @@
         for h in range(2):
             for xd in range(NX):
                 for yl in range(2):
-                    source = (xs * NZ + h * NX + xd) * 2 + yl
-                    pairs.append((source, (xd * NZ + h * NX + xs) * 2 + (yl ^ flip)))
+                    z = h * NX + xd
+                    to = (z + NEAR[(xs - xd) % NX]) % NZ
+                    pairs.append(((xs * NZ + z) * 2 + yl, (xd * NZ + to) * 2 + (yl ^ flip)))
     return pairs
 
 
-def multiply_kernel(flags, rows_ref, own_ref, far_low, far_high, *refs):
-    out_ref, lhs, rhs, lhs_sems, rhs_sems = refs[-5:]
-    yh, yl = flags[0], flags[1]
-    depth = own_ref.shape[0]
+def multiply_kernel(pieces, flags, rows_ref, up_ref, gate_ref, *refs):
+    far_refs = refs[: len(pieces)]
+    out_ref, done_ref, lhs, rhs, out, lhs_sems, rhs_sems, out_sems = refs[-8:]
+    yh, yl, here = flags[0], flags[1], flags[2]
+    depth, hidden = up_ref.shape
     width = depth // 4
+    chunks = []
+    for matrix, ref in enumerate((up_ref, gate_ref)):
+        chunks += [(ref, n * width, yh, matrix, n) for n in range(4)]
+    for (matrix, first, count), ref in zip(pieces, far_refs):
+        chunks += [(ref, n * width, 1 - yh, matrix, first + n) for n in range(count)]
     weights = []
-    for n in range(8):
-        block = yh if n < 4 else 1 - yh
-        ref = own_ref if n < 4 else (far_low if n < 6 else far_high)
-        first = (n % 4 if n < 4 else n % 2) * width
-        source_yl, source_core = (n // 2) % 2, n % 2
-        y = jnp.where(yl == source_yl, 0, 1)
-        to = pl.multiple_of(block * depth + (source_core * 2 + y) * width, width)
+    for n, (ref, at, block, matrix, source) in enumerate(chunks):
+        y = jnp.where(yl == source // 2, 0, 1)
+        to = pl.multiple_of(block * depth + (source % 2 * 2 + y) * width, width)
         weights.append(
             pltpu.make_async_copy(
-                ref.at[pl.ds(first, width), :],
-                rhs.at[pl.ds(to, width), :],
+                ref.at[pl.ds(at, width), :],
+                rhs.at[pl.ds(to, width), pl.ds(matrix * hidden, hidden)],
                 rhs_sems.at[n],
             )
         )
-    for copy in weights:
+    rows, stores = [], []
+    for n in range(NX):
+        rows.append(
+            [
+                pltpu.make_async_copy(
+                    rows_ref.at[lax.rem(h * NX + here + NEAR[n] + NZ, NZ) * 2 + core],
+                    lhs.at[n, :, pl.ds((h * 2 + core) * 2 * width, 2 * width)],
+                    lhs_sems.at[n, h * 2 + core],
+                )
+                for h in range(2)
+                for core in range(2)
+            ]
+        )
+        stores.append(
+            pltpu.make_async_copy(out.at[n], out_ref.at[lax.rem(here + n, NX)], out_sems.at[n])
+        )
+    for copy in weights + rows[0] + rows[1]:
         copy.start()
-    rows = [
-        [
-            pltpu.make_async_copy(
-                rows_ref.at[(h * NX + x) * 2 + core],
-                lhs.at[x, :, pl.ds((h * 2 + core) * 2 * width, 2 * width)],
-                lhs_sems.at[x, h * 2 + core],
-            )
-            for h in range(2)
-            for core in range(2)
-        ]
-        for x in range(NX)
-    ]
-    for copies in rows:
-        for copy in copies:
-            copy.start()
     for copy in weights:
         copy.wait()
-    for x, copies in enumerate(rows):
-        for copy in copies:
+    for n in range(NX):
+        for copy in rows[n]:
             copy.wait()
-        out_ref[x] = jnp.dot(
-            lhs[x], rhs[...], preferred_element_type=jnp.float32
-        ).astype(jnp.bfloat16)
-
-
-def multiply(rows, weights, weights_far, flags, *others):
-    count = rows.shape[1]
-    depth, hidden = weights.shape
+        if n + 2 < NX:
+            for copy in rows[n + 2]:
+                copy.start()
+        out[n] = jnp.dot(lhs[n], rhs[...], preferred_element_type=jnp.float32).astype(
+            jnp.bfloat16
+        )
+        stores[n].start()
+    done_ref[...] = jnp.zeros_like(done_ref)
+    for copy in stores:
+        copy.wait()
+
+
+def multiply(rows, proj_up, proj_gate, far, flags, *others):
+    size = rows.shape[1]
+    depth, hidden = proj_up.shape
+    pieces = [piece[:3] for piece in far]
     return pl.pallas_call(
-        multiply_kernel,
-        out_shape=jax.ShapeDtypeStruct((NX, count, hidden), jnp.bfloat16),
-        in_specs=[pl.BlockSpec(memory_space=pltpu.SMEM)] + [HBM_SPEC] * (4 + len(others)),
-        out_specs=VMEM_SPEC,
+        functools.partial(multiply_kernel, pieces),
+        out_shape=[
+            jax.ShapeDtypeStruct((NX, size, 2 * hidden), jnp.bfloat16),
+            jax.ShapeDtypeStruct((8, LANES), jnp.float32),
+        ],
+        in_specs=[pl.BlockSpec(memory_space=pltpu.SMEM)]
+        + [HBM_SPEC] * (3 + len(far) + len(others)),
+        out_specs=[HBM_SPEC, VMEM_SPEC],
         scratch_shapes=[
-            pltpu.VMEM((NX, count, 2 * depth), jnp.bfloat16),
-            pltpu.VMEM((2 * depth, hidden), jnp.bfloat16),
+            pltpu.VMEM((NX, size, 2 * depth), jnp.bfloat16),
+            pltpu.VMEM((2 * depth, 2 * hidden), jnp.bfloat16),
+            pltpu.VMEM((NX, size, 2 * hidden), jnp.bfloat16),
             pltpu.SemaphoreType.DMA((NX, 4)),
-            pltpu.SemaphoreType.DMA((8,)),
+            pltpu.SemaphoreType.DMA((16,)),
+            pltpu.SemaphoreType.DMA((NX,)),
         ],
         compiler_params=pltpu.CompilerParams(vmem_limit_bytes=56 * 2**20),
         cost_estimate=COST,
         name="multiply",
-    )(flags, rows, weights, *weights_far, *others)
+    )(flags, rows, proj_up, proj_gate, *[piece[3] for piece in far], *others)
 
 
 def names_of(recv_ref, tile, rows):
@@ -137,12 +158,14 @@
     out_ref[:, 8:, :] = jnp.where(left, low[:, 8:], 0.0)
 
 
-def sum_kernel(parts_ref, _, out_ref):
+def sum_kernel(parts_ref, *refs):
+    out_ref = refs[-1]
     total = jnp.sum(parts_ref[...], axis=0).astype(jnp.bfloat16)
     out_ref[...] = jnp.broadcast_to(total[None], out_ref.shape)
 
 
-def up_kernel(rank_ref, recv_ref, up_ref, _, __, out_ref, whole, spread):
+def up_kernel(rank_ref, recv_ref, up_ref, *refs):
+    out_ref, whole, spread = refs[-3:]
     slots, rank = recv_ref.shape[0], 64
     n = rank_ref.shape[0]
     packed = rank_ref[...].astype(jnp.float32)
@@ -179,15 +202,17 @@
     per_owner, _, rank = adapter_down.shape
     capacity = 2 * rows // owners
     slots = owners * capacity
-    flags = jnp.stack([lax.axis_index("yh"), lax.axis_index("yl")]).astype(jnp.int32)
+    flags = jnp.stack([lax.axis_index(name) for name in ("yh", "yl", "x")]).astype(jnp.int32)
 
     mine = lax.ppermute(states, ("x", "z", "yl"), start_pairs(0))
     other = lax.ppermute(states, ("x", "z", "yl"), start_pairs(1))
-    cut = proj_up.shape[0] // 2
-    up_far, gate_far = (
-        [lax.ppermute(part, "yh", SWAP) for part in (weights[:cut], weights[cut:])]
-        for weights in (proj_up, proj_gate)
-    )
+    quarter = proj_up.shape[0] // 4
+
+    def swap(matrix, first, count):
+        part = (proj_up, proj_gate)[matrix][first * quarter : (first + count) * quarter]
+        return matrix, first, count, lax.ppermute(part, "yh", SWAP)
+
+    far = [swap(0, 0, 1), swap(0, 1, 3), swap(1, 0, 2), swap(1, 2, 2)]
 
     target = opponent // per_owner
     choose = target[:, None] == jnp.arange(owners, dtype=jnp.int32)[None, :]
@@ -205,7 +230,7 @@
         send.reshape(owners, capacity, width + LANES), TRUNK, 0, 0, tiled=True
     ).reshape(slots, width + LANES)
 
-    mine, other = after((mine, other), send)
+    mine, other = after((mine, other), send, far[0][3])
     gathered = lax.all_gather(jnp.concatenate([mine, other], axis=1), ("z", "c"), axis=0)
 
     partial_rank = pl.pallas_call(
@@ -217,8 +242,10 @@
         compiler_params=pltpu.CompilerParams(vmem_limit_bytes=14 * 2**20),
         cost_estimate=COST,
         name="down",
-    )(recv, jnp.transpose(adapter_down, (0, 2, 1)).reshape(per_owner * rank, width), up_far[0])
+    )(recv, jnp.transpose(adapter_down, (0, 2, 1)).reshape(per_owner * rank, width), far[1][3])
     rank_parts = lax.all_to_all(partial_rank, ADAPTER, 0, 0, tiled=True)
+    partial, done = multiply(gathered, proj_up, proj_gate, far, flags, rank_parts)
+    total = lax.psum_scatter(partial, "x", scatter_dimension=0, tiled=False).astype(jnp.float32)
     rank_sum = pl.pallas_call(
         sum_kernel,
         out_shape=jax.ShapeDtypeStruct((n_adapter, 16, LANES), jnp.bfloat16),
@@ -226,14 +253,13 @@
         out_specs=VMEM_SPEC,
         cost_estimate=COST,
         name="sum",
-    )(rank_parts, up_far[1])
+    )(rank_parts, done)
     rank_half = lax.all_to_all(rank_sum, ADAPTER, 0, 0, tiled=True)
-    ups = multiply(gathered, proj_up, up_far, flags, rank_half, gate_far[0])
-    up_sum = lax.psum_scatter(ups, "x", scatter_dimension=0, tiled=False)
+
     offsets = pl.pallas_call(
         up_kernel,
         out_shape=jax.ShapeDtypeStruct((slots, hidden), jnp.bfloat16),
-        in_specs=[VMEM_SPEC] * 3 + [HBM_SPEC] * 2,
+        in_specs=[VMEM_SPEC] * 3 + [HBM_SPEC],
         out_specs=VMEM_SPEC,
         scratch_shapes=[
             pltpu.VMEM((slots, LANES), jnp.float32),
@@ -242,17 +268,14 @@
         compiler_params=pltpu.CompilerParams(vmem_limit_bytes=18 * 2**20),
         cost_estimate=COST,
         name="up",
-    )(rank_half, recv, adapter_up.reshape(per_owner * rank, hidden), ups, gate_far[1])
+    )(rank_half, recv, adapter_up.reshape(per_owner * rank, hidden), done)
     returned = lax.all_to_all(
         offsets.reshape(owners, capacity, hidden), TRUNK, 0, 0, tiled=True
     ).reshape(slots, hidden)
-    gates = multiply(gathered, proj_gate, gate_far, flags, offsets)
-    gate_parts = lax.all_to_all(after(gates, returned), "x", 0, 0, tiled=True)
     offset = lax.dot_general(
         placed, returned, (((0,), (0,)), ((), ())), preferred_element_type=jnp.float32
     )
-    gate_sum = jnp.sum(gate_parts.astype(jnp.float32), axis=0)
-    return (jax.nn.silu(gate_sum + offset) * up_sum.astype(jnp.float32)).astype(jnp.bfloat16)
+    return (jax.nn.silu(total[:, hidden:] + offset) * total[:, :hidden]).astype(jnp.bfloat16)
 
 
 def solution(mesh):

time: 202 us -> 184 us (0.911)
  waiting for transfers between devices: 32.1 us -> 47.7 us
  starting transfers between devices: 70.4 us -> 55.2 us
  Pallas kernels: 39.4 us -> 30 us
  blocking collectives: 27.6 us -> 21.6 us
  local copies, waits for them, and re-layouts: 10.4 us -> 7.8 us
    reduce_scatter x1, waiting for transfers between devices: 0.02 us -> 24.8 us  [on_device(): lax.psum_scatter(partial, 'x', scatter_dimension=0, tiled=False)]
    ppermute x4, waiting for transfers between devices: 0.01 us -> 9.94 us  [swap(): return (matrix, first, count, lax.ppermute(part, 'yh', SWAP))]
    pallas_call x2 -> x1, Pallas kernels: 25.5 us -> 16.1 us  [multiply(): pl.pallas_call(functools.partial(multiply_kernel, pieces), out_shape=[jax...]
    all_to_all x1, waiting for transfers between devices: 9.03 us -> 0.01 us  [on_device(): lax.all_to_all(offsets.reshape(owners, capacity, hidden), TRUNK, 0, 0, ti...]
    all_to_all x1, starting transfers between devices: 25.5 us -> 16.8 us  [on_device(): lax.all_to_all(send.reshape(owners, capacity, width + LANES), TRUNK, 0, 0...]
    all_to_all x1 -> x0, waiting for transfers between devices: 6.12 us -> none  [on_device(): rank_half = lax.all_to_all(rank_sum, ADAPTER, 0, 0, tiled=True)]
    all_to_all x1, blocking collectives: 27.6 us -> 21.6 us  [on_device(): rank_half = lax.all_to_all(rank_sum, ADAPTER, 0, 0, tiled=True)]
    ppermute x4, starting transfers between devices: 12 us -> 6.44 us  [swap(): return (matrix, first, count, lax.ppermute(part, 'yh', SWAP))]
  transfers between devices with their start and end apart: 12 -> 11, of which waited for: 5 -> 5; matrix products, arithmetic and copies ran while one was open for 3% -> 5% of each run, Pallas kernels for 20% -> 8%
where the time goes in v4:
time: 184 us; the launch traced here: 183 us
  starting transfers between devices  55.2 us (30%)
  waiting for transfers between devices  47.7 us (26%)
  Pallas kernels  30 us (16%)
  blocking collectives  21.6 us (12%)
  between operations  13.5 us (7%)
  local copies, waits for them, and re-layouts  7.8 us (4%)
  matrix products  4.16 us (2%)
  other arithmetic  3.43 us (2%)
    reduce_scatter x1, waiting for transfers between devices, on_device(): lax.psum_scatter(partial, 'x', scatter_dimension=0, tiled=False)  24.8 us
    all_to_all x1, blocking collectives, on_device(): rank_half = lax.all_to_all(rank_sum, ADAPTER, 0, 0, tiled=True)  21.6 us
    all_to_all x1, starting transfers between devices, on_device(): rank_parts = lax.all_to_all(partial_rank, ADAPTER, 0, 0, tiled=True)  20.1 us
    all_to_all x1, starting transfers between devices, on_device(): lax.all_to_all(send.reshape(owners, capacity, width + LANES), TRUNK, 0, 0...  16.8 us
    pallas_call x1, Pallas kernels, multiply(): pl.pallas_call(functools.partial(multiply_kernel, pieces), out_shape=[jax...  16.1 us
    ppermute x4, waiting for transfers between devices, swap(): return (matrix, first, count, lax.ppermute(part, 'yh', SWAP))  9.94 us
    all_to_all x1, starting transfers between devices, on_device(): lax.all_to_all(offsets.reshape(owners, capacity, hidden), TRUNK, 0, 0, ti...  7.94 us
    all_to_all x1, waiting for transfers between devices, on_device(): rank_parts = lax.all_to_all(partial_rank, ADAPTER, 0, 0, tiled=True)  7.66 us
  transfers between devices with their start and end apart: 11, of which 5 were waited for; matrix products, arithmetic and copies ran while one was open for 5% of the time, Pallas kernels for 8%

profile of v4, /device:TPU:1, one launch (start us, length us, event | category | flops | bytes accessed | tf_op | source)
XLA Modules:
  0.0 183.5 jit_solution(11636040333018107510)
XLA Ops:
  6.5 1.6 collective-permute-start
  8.1 2.1 %collective-permute-start.1 = (bf16[384,256]{1,0:T(8,128)(2,1)}, bf16[384,256]{1,0:T(8,128)(2,1)S(1)}, u32[]{:S(2)}, u32[]{:S(2)}) collective-permute-start(bf16[384,256]{1,0:T(8,128)(2,1)} %param.6), channel_id=1, source_target_pairs={{0,2},{2,0},{4,34},{6,32},{8,82},{10,80},{12,114},{14,112},{16,18}... | collective-permute-start | bytes 589832 | tf_op jit(solution)/shard_map/ppermute | solution.py:208
  10.2 1.0 slice.18
  11.2 2.7 %collective-permute-start.2 = (bf16[256,640]{1,0:T(8,128)(2,1)S(1)}, bf16[256,640]{1,0:T(8,128)(2,1)S(1)}, u32[]{:S(2)}, u32[]{:S(2)}) collective-permute-start(bf16[256,640]{1,0:T(8,128)(2,1)S(1)} %slice.18), channel_id=1, source_target_pairs={{0,128},{128,0},{1,129},{129,1},{2,130},{130,2},{3,131},{131,3},{4... | collective-permute-start | bytes 983048 | tf_op jit(solution)/shard_map/ppermute | solution.py:213
  15.0 2.4 %convolution_convert_fusion = bf16[768,384]{1,0:T(8,128)(2,1)} fusion(s32[384]{0:T(512)S(1)} %convert_add_fusion, bf16[384,128]{1,0:T(8,128)(2,1)S(1)} %broadcast_in_dim.7, bf16[384,256]{1,0:T(8,128)(2,1)} %param.6), kind=kOutput, calls=%fused_computation.1 | convolution fusion | flops 227672064 | bytes 886272 | tf_op jit(solution)/shard_map/dot_general | solution.py:228
  17.4 7.0 %collective-permute-done.2.refs_0_ = bf16[256,640]{1,0:T(8,128)(2,1)S(1)} collective-permute-done((bf16[256,640]{1,0:T(8,128)(2,1)S(1)}, bf16[256,640]{1,0:T(8,128)(2,1)S(1)}, u32[]{:S(2)}, u32[]{:S(2)}) %collective-permute-start.2) | collective-permute-done | bytes 327712 | tf_op jit(solution)/shard_map/ppermute | solution.py:213
  25.3 1.0 slice.19
  27.0 16.8 %all-to-all-start = ((bf16[8,96,384]{2,1,0:T(8,128)(2,1)}), bf16[8,96,384]{2,1,0:T(8,128)(2,1)S(1)}, u32[]{:S(2)}, u32[]{:S(2)}) async-start(bf16[8,96,384]{2,1,0:T(8,128)(2,1)} %bitcast.4), calls=%async_computation | async-start | bytes 1179648 | tf_op jit(solution)/shard_map/all_to_all | solution.py:229
  43.9 2.4 %fusion.12 = (bf16[512,640]{1,0:T(8,128)(2,1)}, bf16[512,640]{1,0:T(8,128)(2,1)S(1)}) fusion(bf16[1024,640]{1,0:T(8,128)(2,1)} %gate_ref.1), kind=kLoop, calls=%fused_computation.30 | loop fusion | bytes 2621440 | tf_op jit(solution)/shard_map/slice | solution.py:212
  46.2 3.0 %collective-permute-start.5 = (bf16[512,640]{1,0:T(8,128)(2,1)}, bf16[512,640]{1,0:T(8,128)(2,1)}, u32[]{:S(2)}, u32[]{:S(2)}) collective-permute-start(bf16[512,640]{1,0:T(8,128)(2,1)} %get-tuple-element.13), channel_id=1, source_target_pairs={{0,128},{128,0},{1,129},{129,1},{2,130},{130,2},{3,131},{131,3},{4... | collective-permute-start | bytes 1966088 | tf_op jit(solution)/shard_map/ppermute | solution.py:213
  49.2 5.3 %all-to-all-done = bf16[8,96,384]{2,1,0:T(8,128)(2,1)S(1)} async-done(((bf16[8,96,384]{2,1,0:T(8,128)(2,1)}), bf16[8,96,384]{2,1,0:T(8,128)(2,1)S(1)}, u32[]{:S(2)}, u32[]{:S(2)}) %all-to-all-start) | async-done | bytes 589856 | tf_op jit(solution)/shard_map/all_to_all | solution.py:229
  54.6 5.7 %down.1 = f32[32,16,128]{2,1,0:T(8,128)} custom-call(bf16[768,384]{1,0:T(8,128)(2,1)S(1)} %bitcast.16, bf16[4096,256]{1,0:T(8,128)(2,1)S(1)} %bitcast.19, bf16[768,640]{1,0:T(8,128)(2,1)} %collective-permute-done.3._.refs_1_), custom_call_target="tpu_custom_call" | custom-call | flops 8000000000 | bytes 16777216 | tf_op jit(solution)/shard_map/down/pallas_call | solution.py:236
  60.3 20.1 %all-to-all-start.1 = ((f32[32,16,128]{2,1,0:T(8,128)}), f32[32,16,128]{2,1,0:T(8,128)S(1)}, u32[]{:S(2)}, u32[]{:S(2)}) async-start(f32[32,16,128]{2,1,0:T(8,128)} %down.1), calls=%async_computation.1 | async-start | bytes 524288 | tf_op jit(solution)/shard_map/all_to_all | solution.py:246
  81.3 3.0 %collective-permute-done.4.refs_2_ = bf16[512,640]{1,0:T(8,128)(2,1)} collective-permute-done((bf16[512,640]{1,0:T(8,128)(2,1)S(1)}, bf16[512,640]{1,0:T(8,128)(2,1)}, u32[]{:S(2)}, u32[]{:S(2)}) %collective-permute-start.4) | collective-permute-done | bytes 655392 | tf_op jit(solution)/shard_map/ppermute | solution.py:213
  84.2 7.7 %all-to-all-done.1.refs_4_.parts_ref = f32[32,16,128]{2,1,0:T(8,128)S(1)} async-done(((f32[32,16,128]{2,1,0:T(8,128)}), f32[32,16,128]{2,1,0:T(8,128)S(1)}, u32[]{:S(2)}, u32[]{:S(2)}) %all-to-all-start.1) | async-done | bytes 262176 | tf_op jit(solution)/shard_map/all_to_all | solution.py:246
  92.6 16.1 %multiply.1 = (bf16[4,384,1280]{2,1,0:T(8,128)(2,1)}, f32[8,128]{1,0:T(8,128)}) custom-call(s32[3]{0:T(128)} %pad_add_fusion.flags, bf16[16,384,512]{2,1,0:T(8,128)(2,1)} %bitcast.21, bf16[1024,640]{1,0:T(8,128)(2,1)} %up_ref.1, bf16[1024,640]{1,0:T(8,128)(2,1)} %gate_ref.1, bf16[256,640]{1,0:T(8,128)(2,1)} %copy-done.5, ...), custom_call_target="tpu_custom_call" | custom-call | flops 8000000000 | bytes 16777216 | tf_op jit(solution)/shard_map/multiply/pallas_call | solution.py:98
  108.7 1.6 sum.1
  110.4 21.6 %all_to_all.20.rank_ref = bf16[32,16,128]{2,1,0:T(8,128)(2,1)S(1)} all-to-all(bf16[32,16,128]{2,1,0:T(8,128)(2,1)} %sum.1), channel_id=1, replica_groups=mesh['yh'=2,'x'=4,'z'=8,'yl'=2,'c'=2] {'z','yl','c'}, dimensions={0} | all-to-all | bytes 262144 | tf_op jit(solution)/shard_map/all_to_all | solution.py:257
  132.0 2.5 %copy-done = bf16[64,64,640]{2,1,0:T(8,128)(2,1)S(1)} copy-done((bf16[64,64,640]{2,1,0:T(8,128)(2,1)S(1)}, bf16[64,64,640]{2,1,0:T(8,128)(2,1)}, u32[]{:S(2)}) %copy-start) | copy-done | bytes 5242904
  134.5 6.5 %up.1 = bf16[768,640]{1,0:T(8,128)(2,1)} custom-call(bf16[32,16,128]{2,1,0:T(8,128)(2,1)S(1)} %all_to_all.20.rank_ref, bf16[768,384]{1,0:T(8,128)(2,1)S(1)} %bitcast.17, bf16[4096,640]{1,0:T(8,128)(2,1)S(1)} %bitcast.18, f32[8,128]{1,0:T(8,128)S(1)} %copy-done.2), custom_call_target="tpu_custom_call" | custom-call | flops 8000000000 | bytes 16777216 | tf_op jit(solution)/shard_map/up/pallas_call | solution.py:259
  141.0 7.9 %all-to-all-start.3 = ((bf16[8,96,640]{2,1,0:T(8,128)(2,1)}), bf16[8,96,640]{2,1,0:T(8,128)(2,1)S(1)}, u32[]{:S(2)}, u32[]{:S(2)}) async-start(bf16[8,96,640]{2,1,0:T(8,128)(2,1)} %bitcast.10), calls=%async_computation.4 | async-start | bytes 1966080 | tf_op jit(solution)/shard_map/all_to_all | solution.py:272
  149.0 24.8 %reduce-scatter.2.cloned.1.call-done = bf16[1,384,1280]{2,1,0:T(8,128)(2,1)} async-done(((bf16[4,384,1280]{2,1,0:T(8,128)(2,1)}), bf16[1,384,1280]{2,1,0:T(8,128)(2,1)}) %reduce-scatter.2.cloned.1.call-update) | async-done | bytes 983056 | tf_op jit(solution)/shard_map/reduce_scatter | solution.py:248
  173.7 1.3 bitcast_convert_fusion
  175.1 1.5 fusion.1
  (29 shorter events, 4.2 us)
Async XLA Ops:
  6.5 85.4 %all-gather.3.cloned.1.call-start = ((), (), s32[]{:S(2)}) async-start(), calls=%async_computation.6 | async-start | bytes 6684672 | tf_op jit(solution)/shard_map/all_gather | solution.py:234
  6.5 10.9 %collective-permute-start = (bf16[384,256]{1,0:T(8,128)(2,1)}, bf16[384,256]{1,0:T(8,128)(2,1)S(1)}, u32[]{:S(2)}, u32[]{:S(2)}) collective-permute-start(bf16[384,256]{1,0:T(8,128)(2,1)} %param.6), channel_id=1, source_target_pairs={{0,0},{2,2},{4,32},{6,34},{8,80},{10,82},{12,112},{14,114},{16,16}... | collective-permute-start | bytes 589832 | tf_op jit(solution)/shard_map/ppermute | solution.py:207
  8.1 9.3 %collective-permute-start.1 = (bf16[384,256]{1,0:T(8,128)(2,1)}, bf16[384,256]{1,0:T(8,128)(2,1)S(1)}, u32[]{:S(2)}, u32[]{:S(2)}) collective-permute-start(bf16[384,256]{1,0:T(8,128)(2,1)} %param.6), channel_id=1, source_target_pairs={{0,2},{2,0},{4,34},{6,32},{8,82},{10,80},{12,114},{14,112},{16,18}... | collective-permute-start | bytes 589832 | tf_op jit(solution)/shard_map/ppermute | solution.py:208
  11.2 13.2 %collective-permute-start.2 = (bf16[256,640]{1,0:T(8,128)(2,1)S(1)}, bf16[256,640]{1,0:T(8,128)(2,1)S(1)}, u32[]{:S(2)}, u32[]{:S(2)}) collective-permute-start(bf16[256,640]{1,0:T(8,128)(2,1)S(1)} %slice.18), channel_id=1, source_target_pairs={{0,128},{128,0},{1,129},{129,1},{2,130},{130,2},{3,131},{131,3},{4... | collective-permute-start | bytes 983048 | tf_op jit(solution)/shard_map/ppermute | solution.py:213
  15.0 10.3 %copy-start.3 = (bf16[1024,640]{1,0:T(8,128)(2,1)S(1)}, bf16[1024,640]{1,0:T(8,128)(2,1)}, u32[]{:S(2)}) copy-start(bf16[1024,640]{1,0:T(8,128)(2,1)} %up_ref.1) | copy-start | bytes 3932164
  24.4 1.9 %copy-start.5 = (bf16[256,640]{1,0:T(8,128)(2,1)}, bf16[256,640]{1,0:T(8,128)(2,1)S(1)}, u32[]{:S(2)}) copy-start(bf16[256,640]{1,0:T(8,128)(2,1)S(1)} %collective-permute-done.2.refs_0_) | copy-start | bytes 983044
  26.3 28.3 %collective-permute-start.3 = (bf16[768,640]{1,0:T(8,128)(2,1)}, bf16[768,640]{1,0:T(8,128)(2,1)}, u32[]{:S(2)}, u32[]{:S(2)}) collective-permute-start(bf16[768,640]{1,0:T(8,128)(2,1)} %slice.19), channel_id=1, source_target_pairs={{0,128},{128,0},{1,129},{129,1},{2,130},{130,2},{3,131},{131,3},{4... | collective-permute-start | bytes 2949128 | tf_op jit(solution)/shard_map/ppermute | solution.py:213
  27.0 27.5 %all-to-all-start = ((bf16[8,96,384]{2,1,0:T(8,128)(2,1)}), bf16[8,96,384]{2,1,0:T(8,128)(2,1)S(1)}, u32[]{:S(2)}, u32[]{:S(2)}) async-start(bf16[8,96,384]{2,1,0:T(8,128)(2,1)} %bitcast.4), calls=%async_computation | async-start | bytes 1179648 | tf_op jit(solution)/shard_map/all_to_all | solution.py:229
  43.9 10.7 %copy-start.1 = (bf16[64,256,64]{1,2,0:T(8,128)(2,1)S(1)}, bf16[64,256,64]{1,2,0:T(8,128)(2,1)}, u32[]{:S(2)}) copy-start(bf16[64,256,64]{1,2,0:T(8,128)(2,1)} %param.10) | copy-start | bytes 6291460
  46.2 35.0 %collective-permute-start.5 = (bf16[512,640]{1,0:T(8,128)(2,1)}, bf16[512,640]{1,0:T(8,128)(2,1)}, u32[]{:S(2)}, u32[]{:S(2)}) collective-permute-start(bf16[512,640]{1,0:T(8,128)(2,1)} %get-tuple-element.13), channel_id=1, source_target_pairs={{0,128},{128,0},{1,129},{129,1},{2,130},{130,2},{3,131},{131,3},{4... | collective-permute-start | bytes 1966088 | tf_op jit(solution)/shard_map/ppermute | solution.py:213
  49.2 35.0 %collective-permute-start.4 = (bf16[512,640]{1,0:T(8,128)(2,1)S(1)}, bf16[512,640]{1,0:T(8,128)(2,1)}, u32[]{:S(2)}, u32[]{:S(2)}) collective-permute-start(bf16[512,640]{1,0:T(8,128)(2,1)S(1)} %get-tuple-element.14), channel_id=1, source_target_pairs={{0,128},{128,0},{1,129},{129,1},{2,130},{130,2},{3,131},{131,3},{4... | collective-permute-start | bytes 1966088 | tf_op jit(solution)/shard_map/ppermute | solution.py:213
  60.3 31.6 %all-to-all-start.1 = ((f32[32,16,128]{2,1,0:T(8,128)}), f32[32,16,128]{2,1,0:T(8,128)S(1)}, u32[]{:S(2)}, u32[]{:S(2)}) async-start(f32[32,16,128]{2,1,0:T(8,128)} %down.1), calls=%async_computation.1 | async-start | bytes 524288 | tf_op jit(solution)/shard_map/all_to_all | solution.py:246
  80.5 93.3 %reduce-scatter.2.cloned.1.call-start = ((), (), s32[]{:S(2)}) async-start(), calls=%async_computation.5 | async-start | bytes 4915200 | tf_op jit(solution)/shard_map/reduce_scatter | solution.py:248
  91.9 0.7 copy-start.4
  108.7 23.3 %copy-start.2 = (f32[8,128]{1,0:T(8,128)S(1)}, f32[8,128]{1,0:T(8,128)}, u32[]{:S(2)}) copy-start(f32[8,128]{1,0:T(8,128)} %get-tuple-element.12.refs_0_) | copy-start | bytes 12292
  132.0 2.5 %copy-start = (bf16[64,64,640]{2,1,0:T(8,128)(2,1)S(1)}, bf16[64,64,640]{2,1,0:T(8,128)(2,1)}, u32[]{:S(2)}) copy-start(bf16[64,64,640]{2,1,0:T(8,128)(2,1)} %param.11) | copy-start | bytes 15728644
  141.0 34.0 %all-to-all-start.3 = ((bf16[8,96,640]{2,1,0:T(8,128)(2,1)}), bf16[8,96,640]{2,1,0:T(8,128)(2,1)S(1)}, u32[]{:S(2)}, u32[]{:S(2)}) async-start(bf16[8,96,640]{2,1,0:T(8,128)(2,1)} %bitcast.10), calls=%async_computation.4 | async-start | bytes 1966080 | tf_op jit(solution)/shard_map/all_to_all | solution.py:272
Sparse Core Ops, SparseCore 0:
  25.4 57.5 all-gather.2
  108.8 64.8 reduce-scatter.1

commit v5 on v4

--- a/solution.py
+++ b/solution.py
@@ -34,26 +34,22 @@
     return pairs
 
 
-def multiply_kernel(pieces, flags, rows_ref, up_ref, gate_ref, *refs):
+def multiply_kernel(pieces, flags, rows_ref, own_ref, *refs):
     far_refs = refs[: len(pieces)]
     out_ref, done_ref, lhs, rhs, out, lhs_sems, rhs_sems, out_sems = refs[-8:]
     yh, yl, here = flags[0], flags[1], flags[2]
-    depth, hidden = up_ref.shape
+    depth = own_ref.shape[0]
     width = depth // 4
-    chunks = []
-    for matrix, ref in enumerate((up_ref, gate_ref)):
-        chunks += [(ref, n * width, yh, matrix, n) for n in range(4)]
-    for (matrix, first, count), ref in zip(pieces, far_refs):
-        chunks += [(ref, n * width, 1 - yh, matrix, first + n) for n in range(count)]
+    chunks = [(own_ref, n * width, yh, n) for n in range(4)]
+    for (first, count), ref in zip(pieces, far_refs):
+        chunks += [(ref, n * width, 1 - yh, first + n) for n in range(count)]
     weights = []
-    for n, (ref, at, block, matrix, source) in enumerate(chunks):
+    for n, (ref, at, block, source) in enumerate(chunks):
         y = jnp.where(yl == source // 2, 0, 1)
         to = pl.multiple_of(block * depth + (source % 2 * 2 + y) * width, width)
         weights.append(
             pltpu.make_async_copy(
-                ref.at[pl.ds(at, width), :],
-                rhs.at[pl.ds(to, width), pl.ds(matrix * hidden, hidden)],
-                rhs_sems.at[n],
+                ref.at[pl.ds(at, width), :], rhs.at[pl.ds(to, width), :], rhs_sems.at[n]
             )
         )
     rows, stores = [], []
@@ -72,15 +68,15 @@
         stores.append(
             pltpu.make_async_copy(out.at[n], out_ref.at[lax.rem(here + n, NX)], out_sems.at[n])
         )
-    for copy in weights + rows[0] + rows[1]:
+    for copy in weights + rows[0]:
         copy.start()
     for copy in weights:
         copy.wait()
     for n in range(NX):
         for copy in rows[n]:
             copy.wait()
-        if n + 2 < NX:
-            for copy in rows[n + 2]:
+        if n + 1 < NX:
+            for copy in rows[n + 1]:
                 copy.start()
         out[n] = jnp.dot(lhs[n], rhs[...], preferred_element_type=jnp.float32).astype(
             jnp.bfloat16
@@ -91,31 +87,31 @@
         copy.wait()
 
 
-def multiply(rows, proj_up, proj_gate, far, flags, *others):
+def multiply(rows, weights, far, flags, *others):
     size = rows.shape[1]
-    depth, hidden = proj_up.shape
-    pieces = [piece[:3] for piece in far]
+    depth, hidden = weights.shape
+    pieces = [piece[:2] for piece in far]
     return pl.pallas_call(
         functools.partial(multiply_kernel, pieces),
         out_shape=[
-            jax.ShapeDtypeStruct((NX, size, 2 * hidden), jnp.bfloat16),
+            jax.ShapeDtypeStruct((NX, size, hidden), jnp.bfloat16),
             jax.ShapeDtypeStruct((8, LANES), jnp.float32),
         ],
         in_specs=[pl.BlockSpec(memory_space=pltpu.SMEM)]
-        + [HBM_SPEC] * (3 + len(far) + len(others)),
+        + [HBM_SPEC] * (2 + len(far) + len(others)),
         out_specs=[HBM_SPEC, VMEM_SPEC],
         scratch_shapes=[
             pltpu.VMEM((NX, size, 2 * depth), jnp.bfloat16),
-            pltpu.VMEM((2 * depth, 2 * hidden), jnp.bfloat16),
-            pltpu.VMEM((NX, size, 2 * hidden), jnp.bfloat16),
+            pltpu.VMEM((2 * depth, hidden), jnp.bfloat16),
+            pltpu.VMEM((NX, size, hidden), jnp.bfloat16),
             pltpu.SemaphoreType.DMA((NX, 4)),
-            pltpu.SemaphoreType.DMA((16,)),
+            pltpu.SemaphoreType.DMA((8,)),
             pltpu.SemaphoreType.DMA((NX,)),
         ],
         compiler_params=pltpu.CompilerParams(vmem_limit_bytes=56 * 2**20),
         cost_estimate=COST,
         name="multiply",
-    )(flags, rows, proj_up, proj_gate, *[piece[3] for piece in far], *others)
+    )(flags, rows, weights, *[piece[2] for piece in far], *others)
 
 
 def names_of(recv_ref, tile, rows):
@@ -208,11 +204,11 @@
     other = lax.ppermute(states, ("x", "z", "yl"), start_pairs(1))
     quarter = proj_up.shape[0] // 4
 
-    def swap(matrix, first, count):
-        part = (proj_up, proj_gate)[matrix][first * quarter : (first + count) * quarter]
-        return matrix, first, count, lax.ppermute(part, "yh", SWAP)
-
-    far = [swap(0, 0, 1), swap(0, 1, 3), swap(1, 0, 2), swap(1, 2, 2)]
+    def swap(weights, first, count, *others):
+        part = weights[first * quarter : (first + count) * quarter]
+        return first, count, lax.ppermute(after(part, *others), "yh", SWAP)
+
+    up_far = [swap(proj_up, 0, 1), swap(proj_up, 1, 3)]
 
     target = opponent // per_owner
     choose = target[:, None] == jnp.arange(owners, dtype=jnp.int32)[None, :]
@@ -230,9 +226,10 @@
         send.reshape(owners, capacity, width + LANES), TRUNK, 0, 0, tiled=True
     ).reshape(slots, width + LANES)
 
-    mine, other = after((mine, other), send, far[0][3])
+    mine, other = after((mine, other), send, up_far[0][2])
     gathered = lax.all_gather(jnp.concatenate([mine, other], axis=1), ("z", "c"), axis=0)
 
+    gate_far = [swap(proj_gate, 0, 2, recv), swap(proj_gate, 2, 2, recv)]
     partial_rank = pl.pallas_call(
         down_kernel,
         out_shape=jax.ShapeDtypeStruct((n_adapter, 16, LANES), jnp.float32),
@@ -242,19 +239,24 @@
         compiler_params=pltpu.CompilerParams(vmem_limit_bytes=14 * 2**20),
         cost_estimate=COST,
         name="down",
-    )(recv, jnp.transpose(adapter_down, (0, 2, 1)).reshape(per_owner * rank, width), far[1][3])
+    )(recv, jnp.transpose(adapter_down, (0, 2, 1)).reshape(per_owner * rank, width), up_far[1][2])
     rank_parts = lax.all_to_all(partial_rank, ADAPTER, 0, 0, tiled=True)
-    partial, done = multiply(gathered, proj_up, proj_gate, far, flags, rank_parts)
-    total = lax.psum_scatter(partial, "x", scatter_dimension=0, tiled=False).astype(jnp.float32)
+    def finish(partial):
+        return lax.psum_scatter(partial, "x", scatter_dimension=0, tiled=False).astype(jnp.float32)
+
+    ups, done = multiply(gathered, proj_up, up_far, flags, rank_parts, gate_far[0][2])
+    up_sum = finish(ups)
     rank_sum = pl.pallas_call(
         sum_kernel,
         out_shape=jax.ShapeDtypeStruct((n_adapter, 16, LANES), jnp.bfloat16),
-        in_specs=[VMEM_SPEC, HBM_SPEC],
+        in_specs=[VMEM_SPEC] + [HBM_SPEC],
         out_specs=VMEM_SPEC,
         cost_estimate=COST,
         name="sum",
     )(rank_parts, done)
     rank_half = lax.all_to_all(rank_sum, ADAPTER, 0, 0, tiled=True)
+    gates, done = multiply(gathered, proj_gate, gate_far, flags, rank_half)
+    gate_sum = finish(gates)
 
     offsets = pl.pallas_call(
         up_kernel,
@@ -275,7 +277,7 @@
     offset = lax.dot_general(
         placed, returned, (((0,), (0,)), ((), ())), preferred_element_type=jnp.float32
     )
-    return (jax.nn.silu(total[:, hidden:] + offset) * total[:, :hidden]).astype(jnp.bfloat16)
+    return (jax.nn.silu(gate_sum + offset) * up_sum).astype(jnp.bfloat16)
 
 
 def solution(mesh):

time: 184 us -> 189 us (1.027)
  blocking collectives: 21.6 us -> 33.2 us
  waiting for transfers between devices: 47.7 us -> 37.2 us
  Pallas kernels: 30 us -> 36.2 us
  starting transfers between devices: 55.2 us -> 50.4 us
  local copies, waits for them, and re-layouts: 7.8 us -> 10 us
    reduce_scatter x1 -> x2, waiting for transfers between devices: 24.8 us -> 0.04 us  [finish(): lax.psum_scatter(partial, 'x', scatter_dimension=0, tiled=False)]
    all_to_all x1, blocking collectives: 21.6 us -> 33.2 us  [on_device(): lax.all_to_all(offsets.reshape(owners, capacity, hidden), TRUNK, 0, 0, ti...]
    ppermute x4, waiting for transfers between devices: 9.94 us -> 17.9 us  [swap(): return (first, count, lax.ppermute(after(part, *others), 'yh', SWAP))]
    pallas_call x1 -> x2, Pallas kernels: 16.1 us -> 23.2 us  [multiply(): pl.pallas_call(functools.partial(multiply_kernel, pieces), out_shape=[jax...]
    all_to_all x1, waiting for transfers between devices: 7.66 us -> 10.8 us  [on_device(): rank_parts = lax.all_to_all(partial_rank, ADAPTER, 0, 0, tiled=True)]
    all_to_all x1, starting transfers between devices: 7.94 us -> 4.81 us  [on_device(): rank_half = lax.all_to_all(rank_sum, ADAPTER, 0, 0, tiled=True)]
    all_to_all x1, waiting for transfers between devices: 5.33 us -> 8.31 us  [on_device(): lax.all_to_all(send.reshape(owners, capacity, width + LANES), TRUNK, 0, 0...]
    unnamed x12 -> x18, local copies, waits for them, and re-layouts: 3.25 us -> 5.45 us
  transfers between devices with their start and end apart: 11 -> 12, of which waited for: 5 -> 5; matrix products, arithmetic and copies ran while one was open for 5% -> 5% of each run, Pallas kernels for 8% -> 13%
where the time goes in v5:
time: 189 us; the launch traced here: 188 us
  starting transfers between devices  50.4 us (27%)
  waiting for transfers between devices  37.2 us (20%)
  Pallas kernels  36.2 us (19%)
  blocking collectives  33.2 us (18%)
  between operations  13.2 us (7%)
  local copies, waits for them, and re-layouts  10 us (5%)
  other arithmetic  4.37 us (2%)
  matrix products  3.27 us (2%)
    all_to_all x1, blocking collectives, on_device(): lax.all_to_all(offsets.reshape(owners, capacity, hidden), TRUNK, 0, 0, ti...  33.2 us
    pallas_call x2, Pallas kernels, multiply(): pl.pallas_call(functools.partial(multiply_kernel, pieces), out_shape=[jax...  23.2 us
    all_to_all x1, starting transfers between devices, on_device(): rank_parts = lax.all_to_all(partial_rank, ADAPTER, 0, 0, tiled=True)  18.2 us
    ppermute x4, waiting for transfers between devices, swap(): return (first, count, lax.ppermute(after(part, *others), 'yh', SWAP))  17.9 us
    all_to_all x1, starting transfers between devices, on_device(): lax.all_to_all(send.reshape(owners, capacity, width + LANES), TRUNK, 0, 0...  16.8 us
    all_to_all x1, waiting for transfers between devices, on_device(): rank_parts = lax.all_to_all(partial_rank, ADAPTER, 0, 0, tiled=True)  10.8 us
    all_to_all x1, waiting for transfers between devices, on_device(): lax.all_to_all(send.reshape(owners, capacity, width + LANES), TRUNK, 0, 0...  8.31 us
    ppermute x4, starting transfers between devices, swap(): return (first, count, lax.ppermute(after(part, *others), 'yh', SWAP))  6.6 us
  transfers between devices with their start and end apart: 12, of which 5 were waited for; matrix products, arithmetic and copies ran while one was open for 5% of the time, Pallas kernels for 13%

profile of v5, /device:TPU:1, one launch (start us, length us, event | category | flops | bytes accessed | tf_op | source)
XLA Modules:
  0.0 187.9 jit_solution(201568571513124833)
XLA Ops:
  6.5 1.6 collective-permute-start
  8.1 2.1 %collective-permute-start.1 = (bf16[384,256]{1,0:T(8,128)(2,1)}, bf16[384,256]{1,0:T(8,128)(2,1)S(1)}, u32[]{:S(2)}, u32[]{:S(2)}) collective-permute-start(bf16[384,256]{1,0:T(8,128)(2,1)} %param.6), channel_id=1, source_target_pairs={{0,2},{2,0},{4,34},{6,32},{8,82},{10,80},{12,114},{14,112},{16,18}... | collective-permute-start | bytes 589832 | tf_op jit(solution)/shard_map/ppermute | solution.py:204
  10.2 1.0 slice.12
  11.2 2.7 %collective-permute-start.2 = (bf16[256,640]{1,0:T(8,128)(2,1)S(1)}, bf16[256,640]{1,0:T(8,128)(2,1)S(1)}, u32[]{:S(2)}, u32[]{:S(2)}) collective-permute-start(bf16[256,640]{1,0:T(8,128)(2,1)S(1)} %slice.12), channel_id=1, source_target_pairs={{0,128},{128,0},{1,129},{129,1},{2,130},{130,2},{3,131},{131,3},{4... | collective-permute-start | bytes 983048 | tf_op jit(solution)/shard_map/ppermute | solution.py:209
  15.0 2.4 %convolution_convert_fusion = bf16[768,384]{1,0:T(8,128)(2,1)} fusion(s32[384]{0:T(512)S(1)} %convert_add_fusion.1, bf16[384,128]{1,0:T(8,128)(2,1)S(1)} %broadcast_in_dim.7, bf16[384,256]{1,0:T(8,128)(2,1)} %param.6), kind=kOutput, calls=%fused_computation | convolution fusion | flops 227672064 | bytes 886272 | tf_op jit(solution)/shard_map/dot_general | solution.py:224
  17.4 7.0 %collective-permute-done.2.refs_0_ = bf16[256,640]{1,0:T(8,128)(2,1)S(1)} collective-permute-done((bf16[256,640]{1,0:T(8,128)(2,1)S(1)}, bf16[256,640]{1,0:T(8,128)(2,1)S(1)}, u32[]{:S(2)}, u32[]{:S(2)}) %collective-permute-start.2) | collective-permute-done | bytes 327712 | tf_op jit(solution)/shard_map/ppermute | solution.py:209
  25.3 1.0 slice.15
  27.1 16.8 %all-to-all-start = ((bf16[8,96,384]{2,1,0:T(8,128)(2,1)}), bf16[8,96,384]{2,1,0:T(8,128)(2,1)S(1)}, u32[]{:S(2)}, u32[]{:S(2)}) async-start(bf16[8,96,384]{2,1,0:T(8,128)(2,1)} %bitcast.4), calls=%async_computation | async-start | bytes 1179648 | tf_op jit(solution)/shard_map/all_to_all | solution.py:225
  43.9 2.4 %fusion.13 = (bf16[512,640]{1,0:T(8,128)(2,1)S(1)}, bf16[512,640]{1,0:T(8,128)(2,1)}) fusion(bf16[1024,640]{1,0:T(8,128)(2,1)} %own_ref.3), kind=kLoop, calls=%fused_computation.30 | loop fusion | bytes 2621440 | tf_op jit(solution)/shard_map/slice | solution.py:208
  46.3 8.3 %all-to-all-done = bf16[8,96,384]{2,1,0:T(8,128)(2,1)S(1)} async-done(((bf16[8,96,384]{2,1,0:T(8,128)(2,1)}), bf16[8,96,384]{2,1,0:T(8,128)(2,1)S(1)}, u32[]{:S(2)}, u32[]{:S(2)}) %all-to-all-start) | async-done | bytes 589856 | tf_op jit(solution)/shard_map/all_to_all | solution.py:225
  54.6 2.7 %collective-permute-start.3 = (bf16[512,640]{1,0:T(8,128)(2,1)}, bf16[512,640]{1,0:T(8,128)(2,1)}, u32[]{:S(2)}, u32[]{:S(2)}) collective-permute-start(bf16[512,640]{1,0:T(8,128)(2,1)} %get-tuple-element.15), channel_id=1, source_target_pairs={{0,128},{128,0},{1,129},{129,1},{2,130},{130,2},{3,131},{131,3},{4... | collective-permute-start | bytes 1966088 | tf_op jit(solution)/shard_map/ppermute | solution.py:209
  57.3 5.8 %down.1 = f32[32,16,128]{2,1,0:T(8,128)} custom-call(bf16[768,384]{1,0:T(8,128)(2,1)S(1)} %bitcast.20, bf16[4096,256]{1,0:T(8,128)(2,1)S(1)} %bitcast.23, bf16[768,640]{1,0:T(8,128)(2,1)} %collective-permute-done.5._.refs_1_), custom_call_target="tpu_custom_call" | custom-call | flops 8000000000 | bytes 16777216 | tf_op jit(solution)/shard_map/down/pallas_call | solution.py:233
  63.0 18.2 %all-to-all-start.1 = ((f32[32,16,128]{2,1,0:T(8,128)}), f32[32,16,128]{2,1,0:T(8,128)S(1)}, u32[]{:S(2)}, u32[]{:S(2)}) async-start(f32[32,16,128]{2,1,0:T(8,128)} %down.1), calls=%async_computation.1 | async-start | bytes 524288 | tf_op jit(solution)/shard_map/all_to_all | solution.py:243
  81.9 10.8 %all-to-all-done.1.refs_2_.parts_ref = f32[32,16,128]{2,1,0:T(8,128)S(1)} async-done(((f32[32,16,128]{2,1,0:T(8,128)}), f32[32,16,128]{2,1,0:T(8,128)S(1)}, u32[]{:S(2)}, u32[]{:S(2)}) %all-to-all-start.1) | async-done | bytes 262176 | tf_op jit(solution)/shard_map/all_to_all | solution.py:243
  93.4 11.6 %multiply.2 = (bf16[4,384,640]{2,1,0:T(8,128)(2,1)}, f32[8,128]{1,0:T(8,128)}) custom-call(s32[3]{0:T(128)} %pad_add_fusion.flags, bf16[16,384,512]{2,1,0:T(8,128)(2,1)} %bitcast.25, bf16[1024,640]{1,0:T(8,128)(2,1)} %own_ref.2, bf16[256,640]{1,0:T(8,128)(2,1)} %copy-done.8, bf16[768,640]{1,0:T(8,128)(2,1)} %collective-permute-done.5._.refs_1_, ...), custom_call_target="tpu_custom_call" | custom-call | flops 8000000000 | bytes 16777216 | tf_op jit(solution)/shard_map/multiply/pallas_call | solution.py:94
  105.5 1.6 sum.1
  107.2 4.8 %all-to-all-start.2 = ((bf16[32,16,128]{2,1,0:T(8,128)(2,1)}), bf16[32,16,128]{2,1,0:T(8,128)(2,1)S(1)}, u32[]{:S(2)}, u32[]{:S(2)}) async-start(bf16[32,16,128]{2,1,0:T(8,128)(2,1)} %sum.1), calls=%async_computation.2 | async-start | bytes 262144 | tf_op jit(solution)/shard_map/all_to_all | solution.py:257
  112.2 10.9 %collective-permute-done.4.refs_1_ = bf16[512,640]{1,0:T(8,128)(2,1)S(1)} collective-permute-done((bf16[512,640]{1,0:T(8,128)(2,1)S(1)}, bf16[512,640]{1,0:T(8,128)(2,1)S(1)}, u32[]{:S(2)}, u32[]{:S(2)}) %collective-permute-start.4) | collective-permute-done | bytes 655392 | tf_op jit(solution)/shard_map/ppermute | solution.py:209
  124.5 11.6 %multiply.3 = (bf16[4,384,640]{2,1,0:T(8,128)(2,1)}, f32[8,128]{1,0:T(8,128)}) custom-call(s32[3]{0:T(128)} %pad_add_fusion.flags, bf16[16,384,512]{2,1,0:T(8,128)(2,1)} %bitcast.26, bf16[1024,640]{1,0:T(8,128)(2,1)} %own_ref.3, bf16[512,640]{1,0:T(8,128)(2,1)} %collective-permute-done.3.refs_3_.refs_0_, bf16[512,640]{1,0:T(8,128)(2,1)} %copy-done.7, ...), custom_call_target="tpu_custom_call" | custom-call | flops 8000000000 | bytes 16777216 | tf_op jit(solution)/shard_map/multiply/pallas_call | solution.py:94
  136.2 0.9 copy-done.1
  137.1 2.5 %copy-done.2 = bf16[64,64,640]{2,1,0:T(8,128)(2,1)S(1)} copy-done((bf16[64,64,640]{2,1,0:T(8,128)(2,1)S(1)}, bf16[64,64,640]{2,1,0:T(8,128)(2,1)}, u32[]{:S(2)}) %copy-start.2) | copy-done | bytes 5242904
  139.6 5.6 %up.1 = bf16[768,640]{1,0:T(8,128)(2,1)S(1)} custom-call(bf16[32,16,128]{2,1,0:T(8,128)(2,1)S(1)} %copy-done.1, bf16[768,384]{1,0:T(8,128)(2,1)S(1)} %bitcast.21, bf16[4096,640]{1,0:T(8,128)(2,1)S(1)} %bitcast.22, f32[8,128]{1,0:T(8,128)S(1)} %copy-done.4), custom_call_target="tpu_custom_call" | custom-call | flops 8000000000 | bytes 16777216 | tf_op jit(solution)/shard_map/up/pallas_call | solution.py:261
  145.1 33.2 %all_to_all.20 = bf16[8,96,640]{2,1,0:T(8,128)(2,1)S(1)} all-to-all(bf16[8,96,640]{2,1,0:T(8,128)(2,1)S(1)} %bitcast.19), channel_id=1, replica_groups=mesh['yh'=2,'x'=4,'z'=8,'yl'=2,'c'=2] {'yh','x'}, dimensions={0} | all-to-all | bytes 1966080 | tf_op jit(solution)/shard_map/all_to_all | solution.py:274
  179.1 2.3 %fusion.2 = bf16[384,640]{1,0:T(8,128)(2,1)} fusion(f32[384,640]{1,0:T(8,128)S(1)} %fusion, bf16[1,384,640]{2,1,0:T(8,128)(2,1)} %reduce-scatter.5.cloned.1.call-done, bf16[1,384,640]{2,1,0:T(8,128)(2,1)} %reduce-scatter.3.cloned.1.call-done), kind=kLoop, calls=%fused_computation.6 | loop fusion | flops 2211840 | bytes 2457600 | tf_op jit(solution)/shard_map/convert_element_type | solution.py:280
  (39 shorter events, 6.9 us)
Async XLA Ops:
  6.5 86.2 %all-gather.3.cloned.1.call-start = ((), (), s32[]{:S(2)}) async-start(), calls=%async_computation.8 | async-start | bytes 6684672 | tf_op jit(solution)/shard_map/all_gather | solution.py:230
  6.5 10.8 %collective-permute-start = (bf16[384,256]{1,0:T(8,128)(2,1)}, bf16[384,256]{1,0:T(8,128)(2,1)S(1)}, u32[]{:S(2)}, u32[]{:S(2)}) collective-permute-start(bf16[384,256]{1,0:T(8,128)(2,1)} %param.6), channel_id=1, source_target_pairs={{0,0},{2,2},{4,32},{6,34},{8,80},{10,82},{12,112},{14,114},{16,16}... | collective-permute-start | bytes 589832 | tf_op jit(solution)/shard_map/ppermute | solution.py:203
  8.1 9.2 %collective-permute-start.1 = (bf16[384,256]{1,0:T(8,128)(2,1)}, bf16[384,256]{1,0:T(8,128)(2,1)S(1)}, u32[]{:S(2)}, u32[]{:S(2)}) collective-permute-start(bf16[384,256]{1,0:T(8,128)(2,1)} %param.6), channel_id=1, source_target_pairs={{0,2},{2,0},{4,34},{6,32},{8,82},{10,80},{12,114},{14,112},{16,18}... | collective-permute-start | bytes 589832 | tf_op jit(solution)/shard_map/ppermute | solution.py:204
  11.2 13.2 %collective-permute-start.2 = (bf16[256,640]{1,0:T(8,128)(2,1)S(1)}, bf16[256,640]{1,0:T(8,128)(2,1)S(1)}, u32[]{:S(2)}, u32[]{:S(2)}) collective-permute-start(bf16[256,640]{1,0:T(8,128)(2,1)S(1)} %slice.12), channel_id=1, source_target_pairs={{0,128},{128,0},{1,129},{129,1},{2,130},{130,2},{3,131},{131,3},{4... | collective-permute-start | bytes 983048 | tf_op jit(solution)/shard_map/ppermute | solution.py:209
  15.0 10.3 %copy-start.5 = (bf16[1024,640]{1,0:T(8,128)(2,1)S(1)}, bf16[1024,640]{1,0:T(8,128)(2,1)}, u32[]{:S(2)}) copy-start(bf16[1024,640]{1,0:T(8,128)(2,1)} %own_ref.2) | copy-start | bytes 3932164
  24.4 1.9 %copy-start.8 = (bf16[256,640]{1,0:T(8,128)(2,1)}, bf16[256,640]{1,0:T(8,128)(2,1)S(1)}, u32[]{:S(2)}) copy-start(bf16[256,640]{1,0:T(8,128)(2,1)S(1)} %collective-permute-done.2.refs_0_) | copy-start | bytes 983044
  26.3 31.0 %collective-permute-start.5 = (bf16[768,640]{1,0:T(8,128)(2,1)}, bf16[768,640]{1,0:T(8,128)(2,1)}, u32[]{:S(2)}, u32[]{:S(2)}) collective-permute-start(bf16[768,640]{1,0:T(8,128)(2,1)} %slice.15), channel_id=1, source_target_pairs={{0,128},{128,0},{1,129},{129,1},{2,130},{130,2},{3,131},{131,3},{4... | collective-permute-start | bytes 2949128 | tf_op jit(solution)/shard_map/ppermute | solution.py:209
  27.1 27.5 %all-to-all-start = ((bf16[8,96,384]{2,1,0:T(8,128)(2,1)}), bf16[8,96,384]{2,1,0:T(8,128)(2,1)S(1)}, u32[]{:S(2)}, u32[]{:S(2)}) async-start(bf16[8,96,384]{2,1,0:T(8,128)(2,1)} %bitcast.4), calls=%async_computation | async-start | bytes 1179648 | tf_op jit(solution)/shard_map/all_to_all | solution.py:225
  43.9 13.4 %copy-start.3 = (bf16[64,256,64]{1,2,0:T(8,128)(2,1)S(1)}, bf16[64,256,64]{1,2,0:T(8,128)(2,1)}, u32[]{:S(2)}) copy-start(bf16[64,256,64]{1,2,0:T(8,128)(2,1)} %param.10) | copy-start | bytes 6291460
  54.6 27.3 %collective-permute-start.3 = (bf16[512,640]{1,0:T(8,128)(2,1)}, bf16[512,640]{1,0:T(8,128)(2,1)}, u32[]{:S(2)}, u32[]{:S(2)}) collective-permute-start(bf16[512,640]{1,0:T(8,128)(2,1)} %get-tuple-element.15), channel_id=1, source_target_pairs={{0,128},{128,0},{1,129},{129,1},{2,130},{130,2},{3,131},{131,3},{4... | collective-permute-start | bytes 1966088 | tf_op jit(solution)/shard_map/ppermute | solution.py:209
  63.0 29.7 %all-to-all-start.1 = ((f32[32,16,128]{2,1,0:T(8,128)}), f32[32,16,128]{2,1,0:T(8,128)S(1)}, u32[]{:S(2)}, u32[]{:S(2)}) async-start(f32[32,16,128]{2,1,0:T(8,128)} %down.1), calls=%async_computation.1 | async-start | bytes 524288 | tf_op jit(solution)/shard_map/all_to_all | solution.py:243
  81.3 97.8 %reduce-scatter.5.cloned.1.call-start = ((), (), s32[]{:S(2)}) async-start(), calls=%async_computation.7 | async-start | bytes 2457600 | tf_op jit(solution)/shard_map/reduce_scatter | solution.py:245
  92.7 0.7 copy-start.6
  105.1 18.0 %collective-permute-start.4 = (bf16[512,640]{1,0:T(8,128)(2,1)S(1)}, bf16[512,640]{1,0:T(8,128)(2,1)S(1)}, u32[]{:S(2)}, u32[]{:S(2)}) collective-permute-start(bf16[512,640]{1,0:T(8,128)(2,1)S(1)} %get-tuple-element.16), channel_id=1, source_target_pairs={{0,128},{128,0},{1,129},{129,1},{2,130},{130,2},{3,131},{131,3},{4... | collective-permute-start | bytes 1966088 | tf_op jit(solution)/shard_map/ppermute | solution.py:209
  107.2 16.0 %all-to-all-start.2 = ((bf16[32,16,128]{2,1,0:T(8,128)(2,1)}), bf16[32,16,128]{2,1,0:T(8,128)(2,1)S(1)}, u32[]{:S(2)}, u32[]{:S(2)}) async-start(bf16[32,16,128]{2,1,0:T(8,128)(2,1)} %sum.1), calls=%async_computation.2 | async-start | bytes 262144 | tf_op jit(solution)/shard_map/all_to_all | solution.py:257
  112.0 67.1 %reduce-scatter.3.cloned.1.call-start = ((), (), s32[]{:S(2)}) async-start(), calls=%async_computation.6 | async-start | bytes 2457600 | tf_op jit(solution)/shard_map/reduce_scatter | solution.py:245
  123.1 0.8 copy-start.7
  123.9 0.7 copy-start
  136.2 0.9 copy-start.1
  136.2 0.9 copy-start.4
  137.1 2.5 %copy-start.2 = (bf16[64,64,640]{2,1,0:T(8,128)(2,1)S(1)}, bf16[64,64,640]{2,1,0:T(8,128)(2,1)}, u32[]{:S(2)}) copy-start(bf16[64,64,640]{2,1,0:T(8,128)(2,1)} %param.11) | copy-start | bytes 15728644
Sparse Core Ops, SparseCore 0:
  25.4 57.5 all-gather.2
  105.2 28.6 reduce-scatter.4
  136.5 41.4 reduce-scatter.2

commit v6 on v5

--- a/solution.py
+++ b/solution.py
@@ -122,7 +122,7 @@
     return (first + 1 + lax.broadcasted_iota(jnp.int32, (1, lanes), 1) // rank).astype(jnp.float32)
 
 
-def down_kernel(recv_ref, down_ref, _, out_ref, total):
+def down_kernel(recv_ref, down_ref, out_ref, total):
     slots, rank, width = recv_ref.shape[0], 64, 256
     tiles = 3
     rows = slots // tiles
@@ -208,7 +208,7 @@
         part = weights[first * quarter : (first + count) * quarter]
         return first, count, lax.ppermute(after(part, *others), "yh", SWAP)
 
-    up_far = [swap(proj_up, 0, 1), swap(proj_up, 1, 3)]
+    up_far = [swap(proj_up, 0, 1)]
 
     target = opponent // per_owner
     choose = target[:, None] == jnp.arange(owners, dtype=jnp.int32)[None, :]
@@ -229,35 +229,34 @@
     mine, other = after((mine, other), send, up_far[0][2])
     gathered = lax.all_gather(jnp.concatenate([mine, other], axis=1), ("z", "c"), axis=0)
 
-    gate_far = [swap(proj_gate, 0, 2, recv), swap(proj_gate, 2, 2, recv)]
+    up_far.append(swap(proj_up, 1, 3, recv))
     partial_rank = pl.pallas_call(
         down_kernel,
         out_shape=jax.ShapeDtypeStruct((n_adapter, 16, LANES), jnp.float32),
-        in_specs=[VMEM_SPEC] * 2 + [HBM_SPEC],
+        in_specs=[VMEM_SPEC] * 2,
         out_specs=VMEM_SPEC,
         scratch_shapes=[pltpu.VMEM((slots, LANES), jnp.float32)],
         compiler_params=pltpu.CompilerParams(vmem_limit_bytes=14 * 2**20),
         cost_estimate=COST,
         name="down",
-    )(recv, jnp.transpose(adapter_down, (0, 2, 1)).reshape(per_owner * rank, width), up_far[1][2])
+    )(recv, jnp.transpose(adapter_down, (0, 2, 1)).reshape(per_owner * rank, width))
     rank_parts = lax.all_to_all(partial_rank, ADAPTER, 0, 0, tiled=True)
-    def finish(partial):
-        return lax.psum_scatter(partial, "x", scatter_dimension=0, tiled=False).astype(jnp.float32)
-
-    ups, done = multiply(gathered, proj_up, up_far, flags, rank_parts, gate_far[0][2])
-    up_sum = finish(ups)
     rank_sum = pl.pallas_call(
         sum_kernel,
         out_shape=jax.ShapeDtypeStruct((n_adapter, 16, LANES), jnp.bfloat16),
-        in_specs=[VMEM_SPEC] + [HBM_SPEC],
+        in_specs=[VMEM_SPEC, HBM_SPEC],
         out_specs=VMEM_SPEC,
         cost_estimate=COST,
         name="sum",
-    )(rank_parts, done)
+    )(rank_parts, up_far[1][2])
     rank_half = lax.all_to_all(rank_sum, ADAPTER, 0, 0, tiled=True)
-    gates, done = multiply(gathered, proj_gate, gate_far, flags, rank_half)
-    gate_sum = finish(gates)
-
+    gate_far = [swap(proj_gate, first, 2, rank_sum) for first in (0, 2)]
+
+    def finish(partial):
+        return lax.psum_scatter(partial, "x", scatter_dimension=0, tiled=False).astype(jnp.float32)
+
+    ups, done = multiply(gathered, proj_up, up_far, flags, rank_half, gate_far[0][2])
+    up_sum = finish(ups)
     offsets = pl.pallas_call(
         up_kernel,
         out_shape=jax.ShapeDtypeStruct((slots, hidden), jnp.bfloat16),
@@ -274,6 +273,8 @@
     returned = lax.all_to_all(
         offsets.reshape(owners, capacity, hidden), TRUNK, 0, 0, tiled=True
     ).reshape(slots, hidden)
+    gates, _ = multiply(gathered, proj_gate, gate_far, flags, offsets)
+    gate_sum = finish(gates)
     offset = lax.dot_general(
         placed, returned, (((0,), (0,)), ((), ())), preferred_element_type=jnp.float32
     )

time: 189 us -> 193 us (1.021)
  waiting for transfers between devices: 37.2 us -> 64.2 us
  blocking collectives: 33.2 us -> 19.1 us
  starting transfers between devices: 50.4 us -> 39.8 us
    reduce_scatter x2, waiting for transfers between devices: 0.04 us -> 14.7 us  [finish(): lax.psum_scatter(partial, 'x', scatter_dimension=0, tiled=False)]
    all_to_all x1, blocking collectives: 33.2 us -> 19.1 us  [on_device(): lax.all_to_all(offsets.reshape(owners, capacity, hidden), TRUNK, 0, 0, ti...]
    all_to_all x1, waiting for transfers between devices: 0.1 us -> 11.8 us  [on_device(): rank_half = lax.all_to_all(rank_sum, ADAPTER, 0, 0, tiled=True)]
    all_to_all x1, starting transfers between devices: 18.2 us -> 6.8 us  [on_device(): rank_parts = lax.all_to_all(partial_rank, ADAPTER, 0, 0, tiled=True)]
    ppermute x4, waiting for transfers between devices: 17.9 us -> 14.2 us  [swap(): return (first, count, lax.ppermute(after(part, *others), 'yh', SWAP))]
    all_to_all x1, waiting for transfers between devices: 10.8 us -> 13.2 us  [on_device(): rank_parts = lax.all_to_all(partial_rank, ADAPTER, 0, 0, tiled=True)]
    unnamed x18 -> x22, local copies, waits for them, and re-layouts: 5.45 us -> 7.03 us
  transfers between devices with their start and end apart: 12 -> 12, of which waited for: 5 -> 6; matrix products, arithmetic and copies ran while one was open for 5% -> 5% of each run, Pallas kernels for 13% -> 13%
where the time goes in v6:
time: 193 us; the launch traced here: 192 us
  waiting for transfers between devices  64.2 us (33%)
  starting transfers between devices  39.8 us (21%)
  Pallas kernels  36.1 us (19%)
  blocking collectives  19.1 us (10%)
  between operations  13.3 us (7%)
  local copies, waits for them, and re-layouts  11.8 us (6%)
  other arithmetic  4.41 us (2%)
  matrix products  3.15 us (2%)
    pallas_call x2, Pallas kernels, multiply(): pl.pallas_call(functools.partial(multiply_kernel, pieces), out_shape=[jax...  23.2 us
    all_to_all x1, blocking collectives, on_device(): lax.all_to_all(offsets.reshape(owners, capacity, hidden), TRUNK, 0, 0, ti...  19.1 us
    all_to_all x1, starting transfers between devices, on_device(): lax.all_to_all(send.reshape(owners, capacity, width + LANES), TRUNK, 0, 0...  17 us
    reduce_scatter x2, waiting for transfers between devices, finish(): lax.psum_scatter(partial, 'x', scatter_dimension=0, tiled=False)  14.7 us
    ppermute x4, waiting for transfers between devices, swap(): return (first, count, lax.ppermute(after(part, *others), 'yh', SWAP))  14.2 us
    all_to_all x1, waiting for transfers between devices, on_device(): rank_parts = lax.all_to_all(partial_rank, ADAPTER, 0, 0, tiled=True)  13.2 us
    all_to_all x1, waiting for transfers between devices, on_device(): rank_half = lax.all_to_all(rank_sum, ADAPTER, 0, 0, tiled=True)  11.8 us
    all_to_all x1, waiting for transfers between devices, on_device(): lax.all_to_all(send.reshape(owners, capacity, width + LANES), TRUNK, 0, 0...  10.2 us
  transfers between devices with their start and end apart: 12, of which 6 were waited for; matrix products, arithmetic and copies ran while one was open for 5% of the time, Pallas kernels for 13%

profile of v6, /device:TPU:1, one launch (start us, length us, event | category | flops | bytes accessed | tf_op | source)
XLA Modules:
  0.0 191.8 jit_solution(7628052491434996471)
XLA Ops:
  6.5 1.6 collective-permute-start
  8.1 2.1 %collective-permute-start.1 = (bf16[384,256]{1,0:T(8,128)(2,1)}, bf16[384,256]{1,0:T(8,128)(2,1)S(1)}, u32[]{:S(2)}, u32[]{:S(2)}) collective-permute-start(bf16[384,256]{1,0:T(8,128)(2,1)} %param.6), channel_id=1, source_target_pairs={{0,2},{2,0},{4,34},{6,32},{8,82},{10,80},{12,114},{14,112},{16,18}... | collective-permute-start | bytes 589832 | tf_op jit(solution)/shard_map/ppermute | solution.py:204
  11.2 2.7 %collective-permute-start.2 = (bf16[256,640]{1,0:T(8,128)(2,1)S(1)}, bf16[256,640]{1,0:T(8,128)(2,1)S(1)}, u32[]{:S(2)}, u32[]{:S(2)}) collective-permute-start(bf16[256,640]{1,0:T(8,128)(2,1)S(1)} %slice.12), channel_id=1, source_target_pairs={{0,128},{128,0},{1,129},{129,1},{2,130},{130,2},{3,131},{131,3},{4... | collective-permute-start | bytes 983048 | tf_op jit(solution)/shard_map/ppermute | solution.py:209
  15.0 2.2 %convolution_convert_fusion = bf16[768,384]{1,0:T(8,128)(2,1)} fusion(s32[384]{0:T(512)S(1)} %convert_add_fusion.1, bf16[384,128]{1,0:T(8,128)(2,1)S(1)} %broadcast_in_dim.7, bf16[384,256]{1,0:T(8,128)(2,1)} %param.6), kind=kOutput, calls=%fused_computation | convolution fusion | flops 227672064 | bytes 886272 | tf_op jit(solution)/shard_map/dot_general | solution.py:224
  17.2 7.2 %collective-permute-done.2.refs_0_ = bf16[256,640]{1,0:T(8,128)(2,1)S(1)} collective-permute-done((bf16[256,640]{1,0:T(8,128)(2,1)S(1)}, bf16[256,640]{1,0:T(8,128)(2,1)S(1)}, u32[]{:S(2)}, u32[]{:S(2)}) %collective-permute-start.2) | collective-permute-done | bytes 327712 | tf_op jit(solution)/shard_map/ppermute | solution.py:209
  25.3 17.0 %all-to-all-start = ((bf16[8,96,384]{2,1,0:T(8,128)(2,1)}), bf16[8,96,384]{2,1,0:T(8,128)(2,1)S(1)}, u32[]{:S(2)}, u32[]{:S(2)}) async-start(bf16[8,96,384]{2,1,0:T(8,128)(2,1)} %bitcast.4), calls=%async_computation | async-start | bytes 1179648 | tf_op jit(solution)/shard_map/all_to_all | solution.py:225
  42.3 2.2 %slice.14 = bf16[768,640]{1,0:T(8,128)(2,1)} slice(bf16[1024,640]{1,0:T(8,128)(2,1)} %own_ref.2), slice={[256:1024], [0:640]} | slice | bytes 1966080 | tf_op jit(solution)/shard_map/slice | solution.py:208
  44.5 10.2 %all-to-all-done = bf16[8,96,384]{2,1,0:T(8,128)(2,1)S(1)} async-done(((bf16[8,96,384]{2,1,0:T(8,128)(2,1)}), bf16[8,96,384]{2,1,0:T(8,128)(2,1)S(1)}, u32[]{:S(2)}, u32[]{:S(2)}) %all-to-all-start) | async-done | bytes 589856 | tf_op jit(solution)/shard_map/all_to_all | solution.py:225
  54.9 5.7 %down.1 = f32[32,16,128]{2,1,0:T(8,128)} custom-call(bf16[768,384]{1,0:T(8,128)(2,1)S(1)} %bitcast.20, bf16[4096,256]{1,0:T(8,128)(2,1)S(1)} %bitcast.23), custom_call_target="tpu_custom_call" | custom-call | flops 8000000000 | bytes 16777216 | tf_op jit(solution)/shard_map/down/pallas_call | solution.py:233
  60.7 6.8 %all-to-all-start.1 = ((f32[32,16,128]{2,1,0:T(8,128)}), f32[32,16,128]{2,1,0:T(8,128)S(1)}, u32[]{:S(2)}, u32[]{:S(2)}) async-start(f32[32,16,128]{2,1,0:T(8,128)} %down.1), calls=%async_computation.1 | async-start | bytes 524288 | tf_op jit(solution)/shard_map/all_to_all | solution.py:243
  68.9 13.2 %all-to-all-done.1.parts_ref = f32[32,16,128]{2,1,0:T(8,128)S(1)} async-done(((f32[32,16,128]{2,1,0:T(8,128)}), f32[32,16,128]{2,1,0:T(8,128)S(1)}, u32[]{:S(2)}, u32[]{:S(2)}) %all-to-all-start.1) | async-done | bytes 262176 | tf_op jit(solution)/shard_map/all_to_all | solution.py:243
  82.8 1.6 sum.1
  84.5 2.9 %collective-permute-start.4 = (bf16[512,640]{1,0:T(8,128)(2,1)S(1)}, bf16[512,640]{1,0:T(8,128)(2,1)S(1)}, u32[]{:S(2)}, u32[]{:S(2)}) collective-permute-start(bf16[512,640]{1,0:T(8,128)(2,1)S(1)} %get-tuple-element.16), channel_id=1, source_target_pairs={{0,128},{128,0},{1,129},{129,1},{2,130},{130,2},{3,131},{131,3},{4... | collective-permute-start | bytes 1966088 | tf_op jit(solution)/shard_map/ppermute | solution.py:209
  87.3 4.8 %all-to-all-start.2 = ((bf16[32,16,128]{2,1,0:T(8,128)(2,1)}), bf16[32,16,128]{2,1,0:T(8,128)(2,1)S(1)}, u32[]{:S(2)}, u32[]{:S(2)}) async-start(bf16[32,16,128]{2,1,0:T(8,128)(2,1)} %sum.1), calls=%async_computation.2 | async-start | bytes 262144 | tf_op jit(solution)/shard_map/all_to_all | solution.py:252
  92.8 11.8 %all-to-all-done.2.refs_2_.rank_ref = bf16[32,16,128]{2,1,0:T(8,128)(2,1)S(1)} async-done(((bf16[32,16,128]{2,1,0:T(8,128)(2,1)}), bf16[32,16,128]{2,1,0:T(8,128)(2,1)S(1)}, u32[]{:S(2)}, u32[]{:S(2)}) %all-to-all-start.2) | async-done | bytes 131104 | tf_op jit(solution)/shard_map/all_to_all | solution.py:252
  105.4 11.6 %multiply.2 = (bf16[4,384,640]{2,1,0:T(8,128)(2,1)}, f32[8,128]{1,0:T(8,128)}) custom-call(s32[3]{0:T(128)} %pad_add_fusion.flags, bf16[16,384,512]{2,1,0:T(8,128)(2,1)} %bitcast.25, bf16[1024,640]{1,0:T(8,128)(2,1)} %own_ref.2, bf16[256,640]{1,0:T(8,128)(2,1)} %copy-done.10, bf16[768,640]{1,0:T(8,128)(2,1)} %collective-permute-done.3.refs_0_.refs_1_, ...), custom_call_target="tpu_custom_call" | custom-call | flops 8000000000 | bytes 16777216 | tf_op jit(solution)/shard_map/multiply/pallas_call | solution.py:94
  117.1 1.6 collective-permute-start.5
  118.8 2.5 %copy-done.4 = bf16[64,64,640]{2,1,0:T(8,128)(2,1)S(1)} copy-done((bf16[64,64,640]{2,1,0:T(8,128)(2,1)S(1)}, bf16[64,64,640]{2,1,0:T(8,128)(2,1)}, u32[]{:S(2)}) %copy-start.4) | copy-done | bytes 5242904
  121.3 5.6 %up.1.refs_2_ = bf16[768,640]{1,0:T(8,128)(2,1)S(1)} custom-call(bf16[32,16,128]{2,1,0:T(8,128)(2,1)S(1)} %copy-done.3, bf16[768,384]{1,0:T(8,128)(2,1)S(1)} %bitcast.21, bf16[4096,640]{1,0:T(8,128)(2,1)S(1)} %bitcast.22, f32[8,128]{1,0:T(8,128)S(1)} %copy-done.6), custom_call_target="tpu_custom_call" | custom-call | flops 8000000000 | bytes 16777216 | tf_op jit(solution)/shard_map/up/pallas_call | solution.py:260
  127.8 7.0 %collective-permute-done.5.refs_1_ = bf16[512,640]{1,0:T(8,128)(2,1)S(1)} collective-permute-done((bf16[512,640]{1,0:T(8,128)(2,1)S(1)}, bf16[512,640]{1,0:T(8,128)(2,1)S(1)}, u32[]{:S(2)}, u32[]{:S(2)}) %collective-permute-start.5) | collective-permute-done | bytes 655392 | tf_op jit(solution)/shard_map/ppermute | solution.py:209
  135.7 11.6 %multiply.3 = (bf16[4,384,640]{2,1,0:T(8,128)(2,1)}, f32[8,128]{1,0:T(8,128)}) custom-call(s32[3]{0:T(128)} %pad_add_fusion.flags, bf16[16,384,512]{2,1,0:T(8,128)(2,1)} %bitcast.26, bf16[1024,640]{1,0:T(8,128)(2,1)} %own_ref.3, bf16[512,640]{1,0:T(8,128)(2,1)} %copy-done.8, bf16[512,640]{1,0:T(8,128)(2,1)} %copy-done.9, bf16[768,640]{1,0:T(8,128)(2,1)} %copy-done), custom_call_target="tpu_custom_call" | custom-call | flops 8000000000 | bytes 16777216 | tf_op jit(solution)/shard_map/multiply/pallas_call | solution.py:94
  148.5 19.1 %all_to_all.20 = bf16[8,96,640]{2,1,0:T(8,128)(2,1)S(1)} all-to-all(bf16[8,96,640]{2,1,0:T(8,128)(2,1)S(1)} %bitcast.19), channel_id=1, replica_groups=mesh['yh'=2,'x'=4,'z'=8,'yl'=2,'c'=2] {'yh','x'}, dimensions={0} | all-to-all | bytes 1966080 | tf_op jit(solution)/shard_map/all_to_all | solution.py:273
  168.3 14.7 %reduce-scatter.3.cloned.1.call-done = bf16[1,384,640]{2,1,0:T(8,128)(2,1)} async-done(((bf16[4,384,640]{2,1,0:T(8,128)(2,1)}), bf16[1,384,640]{2,1,0:T(8,128)(2,1)}) %reduce-scatter.3.cloned.1.call-update) | async-done | bytes 491536 | tf_op jit(solution)/shard_map/reduce_scatter | solution.py:256
  183.0 2.3 %fusion.2 = bf16[384,640]{1,0:T(8,128)(2,1)} fusion(f32[384,640]{1,0:T(8,128)S(1)} %fusion, bf16[1,384,640]{2,1,0:T(8,128)(2,1)} %reduce-scatter.5.cloned.1.call-done, bf16[1,384,640]{2,1,0:T(8,128)(2,1)} %reduce-scatter.3.cloned.1.call-done), kind=kLoop, calls=%fused_computation.6 | loop fusion | flops 2211840 | bytes 2457600 | tf_op jit(solution)/shard_map/convert_element_type | solution.py:281
  (43 shorter events, 10.6 us)
Async XLA Ops:
  6.5 98.0 %all-gather.3.cloned.1.call-start = ((), (), s32[]{:S(2)}) async-start(), calls=%async_computation.8 | async-start | bytes 6684672 | tf_op jit(solution)/shard_map/all_gather | solution.py:230
  6.5 10.7 %collective-permute-start = (bf16[384,256]{1,0:T(8,128)(2,1)}, bf16[384,256]{1,0:T(8,128)(2,1)S(1)}, u32[]{:S(2)}, u32[]{:S(2)}) collective-permute-start(bf16[384,256]{1,0:T(8,128)(2,1)} %param.6), channel_id=1, source_target_pairs={{0,0},{2,2},{4,32},{6,34},{8,80},{10,82},{12,112},{14,114},{16,16}... | collective-permute-start | bytes 589832 | tf_op jit(solution)/shard_map/ppermute | solution.py:203
  8.1 9.1 %collective-permute-start.1 = (bf16[384,256]{1,0:T(8,128)(2,1)}, bf16[384,256]{1,0:T(8,128)(2,1)S(1)}, u32[]{:S(2)}, u32[]{:S(2)}) collective-permute-start(bf16[384,256]{1,0:T(8,128)(2,1)} %param.6), channel_id=1, source_target_pairs={{0,2},{2,0},{4,34},{6,32},{8,82},{10,80},{12,114},{14,112},{16,18}... | collective-permute-start | bytes 589832 | tf_op jit(solution)/shard_map/ppermute | solution.py:204
  11.2 13.2 %collective-permute-start.2 = (bf16[256,640]{1,0:T(8,128)(2,1)S(1)}, bf16[256,640]{1,0:T(8,128)(2,1)S(1)}, u32[]{:S(2)}, u32[]{:S(2)}) collective-permute-start(bf16[256,640]{1,0:T(8,128)(2,1)S(1)} %slice.12), channel_id=1, source_target_pairs={{0,128},{128,0},{1,129},{129,1},{2,130},{130,2},{3,131},{131,3},{4... | collective-permute-start | bytes 983048 | tf_op jit(solution)/shard_map/ppermute | solution.py:209
  24.4 20.1 %copy-start.10 = (bf16[256,640]{1,0:T(8,128)(2,1)}, bf16[256,640]{1,0:T(8,128)(2,1)S(1)}, u32[]{:S(2)}) copy-start(bf16[256,640]{1,0:T(8,128)(2,1)S(1)} %collective-permute-done.2.refs_0_) | copy-start | bytes 983044
  25.3 29.7 %copy-start.5 = (bf16[64,256,64]{1,2,0:T(8,128)(2,1)S(1)}, bf16[64,256,64]{1,2,0:T(8,128)(2,1)}, u32[]{:S(2)}) copy-start(bf16[64,256,64]{1,2,0:T(8,128)(2,1)} %param.10) | copy-start | bytes 6291460
  25.3 29.4 %all-to-all-start = ((bf16[8,96,384]{2,1,0:T(8,128)(2,1)}), bf16[8,96,384]{2,1,0:T(8,128)(2,1)S(1)}, u32[]{:S(2)}, u32[]{:S(2)}) async-start(bf16[8,96,384]{2,1,0:T(8,128)(2,1)} %bitcast.4), calls=%async_computation | async-start | bytes 1179648 | tf_op jit(solution)/shard_map/all_to_all | solution.py:225
  54.7 27.5 %collective-permute-start.3 = (bf16[768,640]{1,0:T(8,128)(2,1)}, bf16[768,640]{1,0:T(8,128)(2,1)}, u32[]{:S(2)}, u32[]{:S(2)}) collective-permute-start(bf16[768,640]{1,0:T(8,128)(2,1)} %slice.14), channel_id=1, source_target_pairs={{0,128},{128,0},{1,129},{129,1},{2,130},{130,2},{3,131},{131,3},{4... | collective-permute-start | bytes 2949128 | tf_op jit(solution)/shard_map/ppermute | solution.py:209
  60.7 21.5 %all-to-all-start.1 = ((f32[32,16,128]{2,1,0:T(8,128)}), f32[32,16,128]{2,1,0:T(8,128)S(1)}, u32[]{:S(2)}, u32[]{:S(2)}) async-start(f32[32,16,128]{2,1,0:T(8,128)} %down.1), calls=%async_computation.1 | async-start | bytes 524288 | tf_op jit(solution)/shard_map/all_to_all | solution.py:243
  82.1 0.7 copy-start.7
  84.5 20.1 %collective-permute-start.4 = (bf16[512,640]{1,0:T(8,128)(2,1)S(1)}, bf16[512,640]{1,0:T(8,128)(2,1)S(1)}, u32[]{:S(2)}, u32[]{:S(2)}) collective-permute-start(bf16[512,640]{1,0:T(8,128)(2,1)S(1)} %get-tuple-element.16), channel_id=1, source_target_pairs={{0,128},{128,0},{1,129},{129,1},{2,130},{130,2},{3,131},{131,3},{4... | collective-permute-start | bytes 1966088 | tf_op jit(solution)/shard_map/ppermute | solution.py:209
  87.3 17.2 %all-to-all-start.2 = ((bf16[32,16,128]{2,1,0:T(8,128)(2,1)}), bf16[32,16,128]{2,1,0:T(8,128)(2,1)S(1)}, u32[]{:S(2)}, u32[]{:S(2)}) async-start(bf16[32,16,128]{2,1,0:T(8,128)(2,1)} %sum.1), calls=%async_computation.2 | async-start | bytes 262144 | tf_op jit(solution)/shard_map/all_to_all | solution.py:252
  92.1 76.2 %reduce-scatter.5.cloned.1.call-start = ((), (), s32[]{:S(2)}) async-start(), calls=%async_computation.7 | async-start | bytes 2457600 | tf_op jit(solution)/shard_map/reduce_scatter | solution.py:256
  104.5 0.6 copy-start.2
  104.6 0.9 copy-start.8
  117.0 1.7 copy-start.3
  117.1 1.7 copy-start.6
  117.1 65.9 %reduce-scatter.3.cloned.1.call-start = ((), (), s32[]{:S(2)}) async-start(), calls=%async_computation.6 | async-start | bytes 2457600 | tf_op jit(solution)/shard_map/reduce_scatter | solution.py:256
  117.1 17.7 %collective-permute-start.5 = (bf16[512,640]{1,0:T(8,128)(2,1)S(1)}, bf16[512,640]{1,0:T(8,128)(2,1)S(1)}, u32[]{:S(2)}, u32[]{:S(2)}) collective-permute-start(bf16[512,640]{1,0:T(8,128)(2,1)S(1)} %get-tuple-element.17), channel_id=1, source_target_pairs={{0,128},{128,0},{1,129},{129,1},{2,130},{130,2},{3,131},{131,3},{4... | collective-permute-start | bytes 1966088 | tf_op jit(solution)/shard_map/ppermute | solution.py:209
  118.8 2.5 %copy-start.4 = (bf16[64,64,640]{2,1,0:T(8,128)(2,1)S(1)}, bf16[64,64,640]{2,1,0:T(8,128)(2,1)}, u32[]{:S(2)}) copy-start(bf16[64,64,640]{2,1,0:T(8,128)(2,1)} %param.11) | copy-start | bytes 15728644
  126.8 1.0 copy-start
  134.8 0.9 copy-start.9
  147.3 1.2 copy-start.1
Sparse Core Ops, SparseCore 0:
  25.4 63.1 all-gather.2
  117.2 26.6 reduce-scatter.4
  147.5 35.5 reduce-scatter.2

commit v7 on v5

--- a/solution.py
+++ b/solution.py
@@ -122,7 +122,7 @@
     return (first + 1 + lax.broadcasted_iota(jnp.int32, (1, lanes), 1) // rank).astype(jnp.float32)
 
 
-def down_kernel(recv_ref, down_ref, _, out_ref, total):
+def down_kernel(recv_ref, down_ref, out_ref, total):
     slots, rank, width = recv_ref.shape[0], 64, 256
     tiles = 3
     rows = slots // tiles
@@ -208,7 +208,7 @@
         part = weights[first * quarter : (first + count) * quarter]
         return first, count, lax.ppermute(after(part, *others), "yh", SWAP)
 
-    up_far = [swap(proj_up, 0, 1), swap(proj_up, 1, 3)]
+    up_far = [swap(proj_up, 0, 1)]
 
     target = opponent // per_owner
     choose = target[:, None] == jnp.arange(owners, dtype=jnp.int32)[None, :]
@@ -229,17 +229,18 @@
     mine, other = after((mine, other), send, up_far[0][2])
     gathered = lax.all_gather(jnp.concatenate([mine, other], axis=1), ("z", "c"), axis=0)
 
-    gate_far = [swap(proj_gate, 0, 2, recv), swap(proj_gate, 2, 2, recv)]
+    up_far.append(swap(proj_up, 1, 3, recv))
     partial_rank = pl.pallas_call(
         down_kernel,
         out_shape=jax.ShapeDtypeStruct((n_adapter, 16, LANES), jnp.float32),
-        in_specs=[VMEM_SPEC] * 2 + [HBM_SPEC],
+        in_specs=[VMEM_SPEC] * 2,
         out_specs=VMEM_SPEC,
         scratch_shapes=[pltpu.VMEM((slots, LANES), jnp.float32)],
         compiler_params=pltpu.CompilerParams(vmem_limit_bytes=14 * 2**20),
         cost_estimate=COST,
         name="down",
-    )(recv, jnp.transpose(adapter_down, (0, 2, 1)).reshape(per_owner * rank, width), up_far[1][2])
+    )(recv, jnp.transpose(adapter_down, (0, 2, 1)).reshape(per_owner * rank, width))
+    gate_far = [swap(proj_gate, first, 2, partial_rank) for first in (0, 2)]
     rank_parts = lax.all_to_all(partial_rank, ADAPTER, 0, 0, tiled=True)
     def finish(partial):
         return lax.psum_scatter(partial, "x", scatter_dimension=0, tiled=False).astype(jnp.float32)

time: 189 us -> 189 us (level)
  waiting for transfers between devices: 37.2 us -> 52.1 us
  starting transfers between devices: 50.4 us -> 42 us
  blocking collectives: 33.2 us -> 29 us
    all_to_all x1, waiting for transfers between devices: 10.8 us -> 22.3 us  [on_device(): rank_parts = lax.all_to_all(partial_rank, ADAPTER, 0, 0, tiled=True)]
    all_to_all x1, starting transfers between devices: 18.2 us -> 7.07 us  [on_device(): rank_parts = lax.all_to_all(partial_rank, ADAPTER, 0, 0, tiled=True)]
    all_to_all x1, blocking collectives: 33.2 us -> 29 us  [on_device(): lax.all_to_all(offsets.reshape(owners, capacity, hidden), TRUNK, 0, 0, ti...]
    all_to_all x1, waiting for transfers between devices: 0.1 us -> 3.43 us  [on_device(): rank_half = lax.all_to_all(rank_sum, ADAPTER, 0, 0, tiled=True)]
    ppermute x4, waiting for transfers between devices: 17.9 us -> 14.7 us  [swap(): return (first, count, lax.ppermute(after(part, *others), 'yh', SWAP))]
    all_to_all x1, starting transfers between devices: 4.81 us -> 6.88 us  [on_device(): rank_half = lax.all_to_all(rank_sum, ADAPTER, 0, 0, tiled=True)]
    unnamed x18 -> x22, local copies, waits for them, and re-layouts: 5.45 us -> 5.49 us
  transfers between devices with their start and end apart: 12 -> 12, of which waited for: 5 -> 7; matrix products, arithmetic and copies ran while one was open for 5% -> 4% of each run, Pallas kernels for 13% -> 13%
where the time goes in v7:
time: 189 us
  waiting for transfers between devices  52.1 us (28%)
  starting transfers between devices  42 us (22%)
  Pallas kernels  36.2 us (19%)
  blocking collectives  29 us (15%)
  between operations  13.2 us (7%)
  local copies, waits for them, and re-layouts  8.6 us (5%)
  other arithmetic  4.36 us (2%)
  matrix products  3.2 us (2%)
    all_to_all x1, blocking collectives, on_device(): lax.all_to_all(offsets.reshape(owners, capacity, hidden), TRUNK, 0, 0, ti...  29 us
    pallas_call x2, Pallas kernels, multiply(): pl.pallas_call(functools.partial(multiply_kernel, pieces), out_shape=[jax...  23.2 us
    all_to_all x1, waiting for transfers between devices, on_device(): rank_parts = lax.all_to_all(partial_rank, ADAPTER, 0, 0, tiled=True)  22.3 us
    all_to_all x1, starting transfers between devices, on_device(): lax.all_to_all(send.reshape(owners, capacity, width + LANES), TRUNK, 0, 0...  16.9 us
    ppermute x4, waiting for transfers between devices, swap(): return (first, count, lax.ppermute(after(part, *others), 'yh', SWAP))  14.7 us
    all_to_all x1, waiting for transfers between devices, on_device(): lax.all_to_all(send.reshape(owners, capacity, width + LANES), TRUNK, 0, 0...  9.73 us
    ppermute x4, starting transfers between devices, swap(): return (first, count, lax.ppermute(after(part, *others), 'yh', SWAP))  7.21 us
    all_to_all x1, starting transfers between devices, on_device(): rank_parts = lax.all_to_all(partial_rank, ADAPTER, 0, 0, tiled=True)  7.07 us
  transfers between devices with their start and end apart: 12, of which 7 were waited for; matrix products, arithmetic and copies ran while one was open for 4% of the time, Pallas kernels for 13%

profile of v7, /device:TPU:1, one launch (start us, length us, event | category | flops | bytes accessed | tf_op | source)
XLA Modules:
  0.0 188.6 jit_solution(6001899412046544497)
XLA Ops:
  6.5 1.6 collective-permute-start
  8.1 2.1 %collective-permute-start.1 = (bf16[384,256]{1,0:T(8,128)(2,1)}, bf16[384,256]{1,0:T(8,128)(2,1)S(1)}, u32[]{:S(2)}, u32[]{:S(2)}) collective-permute-start(bf16[384,256]{1,0:T(8,128)(2,1)} %param.6), channel_id=1, source_target_pairs={{0,2},{2,0},{4,34},{6,32},{8,82},{10,80},{12,114},{14,112},{16,18}... | collective-permute-start | bytes 589832 | tf_op jit(solution)/shard_map/ppermute | solution.py:204
  11.2 2.7 %collective-permute-start.2 = (bf16[256,640]{1,0:T(8,128)(2,1)S(1)}, bf16[256,640]{1,0:T(8,128)(2,1)S(1)}, u32[]{:S(2)}, u32[]{:S(2)}) collective-permute-start(bf16[256,640]{1,0:T(8,128)(2,1)S(1)} %slice.12), channel_id=1, source_target_pairs={{0,128},{128,0},{1,129},{129,1},{2,130},{130,2},{3,131},{131,3},{4... | collective-permute-start | bytes 983048 | tf_op jit(solution)/shard_map/ppermute | solution.py:209
  15.0 2.3 %convolution_convert_fusion = bf16[768,384]{1,0:T(8,128)(2,1)} fusion(s32[384]{0:T(512)S(1)} %convert_add_fusion.1, bf16[384,128]{1,0:T(8,128)(2,1)S(1)} %broadcast_in_dim.7, bf16[384,256]{1,0:T(8,128)(2,1)} %param.6), kind=kOutput, calls=%fused_computation | convolution fusion | flops 227672064 | bytes 886272 | tf_op jit(solution)/shard_map/dot_general | solution.py:224
  17.3 7.1 %collective-permute-done.2.refs_0_ = bf16[256,640]{1,0:T(8,128)(2,1)S(1)} collective-permute-done((bf16[256,640]{1,0:T(8,128)(2,1)S(1)}, bf16[256,640]{1,0:T(8,128)(2,1)S(1)}, u32[]{:S(2)}, u32[]{:S(2)}) %collective-permute-start.2) | collective-permute-done | bytes 327712 | tf_op jit(solution)/shard_map/ppermute | solution.py:209
  25.3 16.9 %all-to-all-start = ((bf16[8,96,384]{2,1,0:T(8,128)(2,1)}), bf16[8,96,384]{2,1,0:T(8,128)(2,1)S(1)}, u32[]{:S(2)}, u32[]{:S(2)}) async-start(bf16[8,96,384]{2,1,0:T(8,128)(2,1)} %bitcast.4), calls=%async_computation | async-start | bytes 1179648 | tf_op jit(solution)/shard_map/all_to_all | solution.py:225
  44.8 9.7 %all-to-all-done = bf16[8,96,384]{2,1,0:T(8,128)(2,1)S(1)} async-done(((bf16[8,96,384]{2,1,0:T(8,128)(2,1)}), bf16[8,96,384]{2,1,0:T(8,128)(2,1)S(1)}, u32[]{:S(2)}, u32[]{:S(2)}) %all-to-all-start) | async-done | bytes 589856 | tf_op jit(solution)/shard_map/all_to_all | solution.py:225
  54.8 5.8 %down.1 = f32[32,16,128]{2,1,0:T(8,128)} custom-call(bf16[768,384]{1,0:T(8,128)(2,1)S(1)} %bitcast.20, bf16[4096,256]{1,0:T(8,128)(2,1)S(1)} %bitcast.23), custom_call_target="tpu_custom_call" | custom-call | flops 8000000000 | bytes 16777216 | tf_op jit(solution)/shard_map/down/pallas_call | solution.py:233
  60.5 2.7 %collective-permute-start.3 = (bf16[512,640]{1,0:T(8,128)(2,1)}, bf16[512,640]{1,0:T(8,128)(2,1)S(1)}, u32[]{:S(2)}, u32[]{:S(2)}) collective-permute-start(bf16[512,640]{1,0:T(8,128)(2,1)} %get-tuple-element.16), channel_id=1, source_target_pairs={{0,128},{128,0},{1,129},{129,1},{2,130},{130,2},{3,131},{131,3},{4... | collective-permute-start | bytes 1966088 | tf_op jit(solution)/shard_map/ppermute | solution.py:209
  63.2 7.1 %all-to-all-start.1 = ((f32[32,16,128]{2,1,0:T(8,128)}), f32[32,16,128]{2,1,0:T(8,128)S(1)}, u32[]{:S(2)}, u32[]{:S(2)}) async-start(f32[32,16,128]{2,1,0:T(8,128)} %down.1), calls=%async_computation.1 | async-start | bytes 524288 | tf_op jit(solution)/shard_map/all_to_all | solution.py:244
  70.9 22.3 %all-to-all-done.1.refs_2_.parts_ref = f32[32,16,128]{2,1,0:T(8,128)S(1)} async-done(((f32[32,16,128]{2,1,0:T(8,128)}), f32[32,16,128]{2,1,0:T(8,128)S(1)}, u32[]{:S(2)}, u32[]{:S(2)}) %all-to-all-start.1) | async-done | bytes 262176 | tf_op jit(solution)/shard_map/all_to_all | solution.py:244
  93.2 1.9 %collective-permute-done.3.refs_3_.refs_0_ = bf16[512,640]{1,0:T(8,128)(2,1)S(1)} collective-permute-done((bf16[512,640]{1,0:T(8,128)(2,1)}, bf16[512,640]{1,0:T(8,128)(2,1)S(1)}, u32[]{:S(2)}, u32[]{:S(2)}) %collective-permute-start.3) | collective-permute-done | bytes 655392 | tf_op jit(solution)/shard_map/ppermute | solution.py:209
  96.0 11.6 %multiply.2 = (bf16[4,384,640]{2,1,0:T(8,128)(2,1)}, f32[8,128]{1,0:T(8,128)}) custom-call(s32[3]{0:T(128)} %pad_add_fusion.flags, bf16[16,384,512]{2,1,0:T(8,128)(2,1)} %bitcast.25, bf16[1024,640]{1,0:T(8,128)(2,1)} %own_ref.2, bf16[256,640]{1,0:T(8,128)(2,1)} %copy-done.10, bf16[768,640]{1,0:T(8,128)(2,1)} %collective-permute-done.5.refs_1_, ...), custom_call_target="tpu_custom_call" | custom-call | flops 8000000000 | bytes 16777216 | tf_op jit(solution)/shard_map/multiply/pallas_call | solution.py:94
  107.6 1.5 collective-permute-start.4
  109.2 1.6 sum.1
  110.8 6.9 %all-to-all-start.2 = ((bf16[32,16,128]{2,1,0:T(8,128)(2,1)}), bf16[32,16,128]{2,1,0:T(8,128)(2,1)S(1)}, u32[]{:S(2)}, u32[]{:S(2)}) async-start(bf16[32,16,128]{2,1,0:T(8,128)(2,1)} %sum.1), calls=%async_computation.2 | async-start | bytes 262144 | tf_op jit(solution)/shard_map/all_to_all | solution.py:258
  117.9 5.7 %collective-permute-done.4.refs_1_ = bf16[512,640]{1,0:T(8,128)(2,1)S(1)} collective-permute-done((bf16[512,640]{1,0:T(8,128)(2,1)S(1)}, bf16[512,640]{1,0:T(8,128)(2,1)S(1)}, u32[]{:S(2)}, u32[]{:S(2)}) %collective-permute-start.4) | collective-permute-done | bytes 655392 | tf_op jit(solution)/shard_map/ppermute | solution.py:209
  123.6 3.4 %all-to-all-done.2.refs_2_.rank_ref = bf16[32,16,128]{2,1,0:T(8,128)(2,1)S(1)} async-done(((bf16[32,16,128]{2,1,0:T(8,128)(2,1)}), bf16[32,16,128]{2,1,0:T(8,128)(2,1)S(1)}, u32[]{:S(2)}, u32[]{:S(2)}) %all-to-all-start.2) | async-done | bytes 131104 | tf_op jit(solution)/shard_map/all_to_all | solution.py:258
  127.7 11.6 %multiply.3 = (bf16[4,384,640]{2,1,0:T(8,128)(2,1)}, f32[8,128]{1,0:T(8,128)}) custom-call(s32[3]{0:T(128)} %pad_add_fusion.flags, bf16[16,384,512]{2,1,0:T(8,128)(2,1)} %bitcast.26, bf16[1024,640]{1,0:T(8,128)(2,1)} %own_ref.3, bf16[512,640]{1,0:T(8,128)(2,1)} %copy-done.8, bf16[512,640]{1,0:T(8,128)(2,1)} %copy-done.9, bf16[32,16,128]{2,1,0:T(8,128)(2,1)} %copy-done), custom_call_target="tpu_custom_call" | custom-call | flops 8000000000 | bytes 16777216 | tf_op jit(solution)/shard_map/multiply/pallas_call | solution.py:94
  140.2 2.5 %copy-done.2 = bf16[64,64,640]{2,1,0:T(8,128)(2,1)S(1)} copy-done((bf16[64,64,640]{2,1,0:T(8,128)(2,1)S(1)}, bf16[64,64,640]{2,1,0:T(8,128)(2,1)}, u32[]{:S(2)}) %copy-start.2) | copy-done | bytes 5242904
  142.7 5.6 %up.1 = bf16[768,640]{1,0:T(8,128)(2,1)S(1)} custom-call(bf16[32,16,128]{2,1,0:T(8,128)(2,1)S(1)} %copy-done.1, bf16[768,384]{1,0:T(8,128)(2,1)S(1)} %bitcast.21, bf16[4096,640]{1,0:T(8,128)(2,1)S(1)} %bitcast.22, f32[8,128]{1,0:T(8,128)S(1)} %copy-done.4), custom_call_target="tpu_custom_call" | custom-call | flops 8000000000 | bytes 16777216 | tf_op jit(solution)/shard_map/up/pallas_call | solution.py:262
  148.3 29.0 %all_to_all.20 = bf16[8,96,640]{2,1,0:T(8,128)(2,1)S(1)} all-to-all(bf16[8,96,640]{2,1,0:T(8,128)(2,1)S(1)} %bitcast.19), channel_id=1, replica_groups=mesh['yh'=2,'x'=4,'z'=8,'yl'=2,'c'=2] {'yh','x'}, dimensions={0} | all-to-all | bytes 1966080 | tf_op jit(solution)/shard_map/all_to_all | solution.py:275
  178.0 1.8 reduce-scatter.3.cloned.1.call-done
  179.8 2.3 %fusion.2 = bf16[384,640]{1,0:T(8,128)(2,1)} fusion(f32[384,640]{1,0:T(8,128)S(1)} %fusion, bf16[1,384,640]{2,1,0:T(8,128)(2,1)} %reduce-scatter.5.cloned.1.call-done, bf16[1,384,640]{2,1,0:T(8,128)(2,1)} %reduce-scatter.3.cloned.1.call-done), kind=kLoop, calls=%fused_computation.6 | loop fusion | flops 2211840 | bytes 2457600 | tf_op jit(solution)/shard_map/convert_element_type | solution.py:281
  (43 shorter events, 9.7 us)
Async XLA Ops:
  6.5 88.6 %all-gather.3.cloned.1.call-start = ((), (), s32[]{:S(2)}) async-start(), calls=%async_computation.8 | async-start | bytes 6684672 | tf_op jit(solution)/shard_map/all_gather | solution.py:230
  6.5 10.7 %collective-permute-start = (bf16[384,256]{1,0:T(8,128)(2,1)}, bf16[384,256]{1,0:T(8,128)(2,1)S(1)}, u32[]{:S(2)}, u32[]{:S(2)}) collective-permute-start(bf16[384,256]{1,0:T(8,128)(2,1)} %param.6), channel_id=1, source_target_pairs={{0,0},{2,2},{4,32},{6,34},{8,80},{10,82},{12,112},{14,114},{16,16}... | collective-permute-start | bytes 589832 | tf_op jit(solution)/shard_map/ppermute | solution.py:203
  8.1 9.2 %collective-permute-start.1 = (bf16[384,256]{1,0:T(8,128)(2,1)}, bf16[384,256]{1,0:T(8,128)(2,1)S(1)}, u32[]{:S(2)}, u32[]{:S(2)}) collective-permute-start(bf16[384,256]{1,0:T(8,128)(2,1)} %param.6), channel_id=1, source_target_pairs={{0,2},{2,0},{4,34},{6,32},{8,82},{10,80},{12,114},{14,112},{16,18}... | collective-permute-start | bytes 589832 | tf_op jit(solution)/shard_map/ppermute | solution.py:204
  11.2 13.2 %collective-permute-start.2 = (bf16[256,640]{1,0:T(8,128)(2,1)S(1)}, bf16[256,640]{1,0:T(8,128)(2,1)S(1)}, u32[]{:S(2)}, u32[]{:S(2)}) collective-permute-start(bf16[256,640]{1,0:T(8,128)(2,1)S(1)} %slice.12), channel_id=1, source_target_pairs={{0,128},{128,0},{1,129},{129,1},{2,130},{130,2},{3,131},{131,3},{4... | collective-permute-start | bytes 983048 | tf_op jit(solution)/shard_map/ppermute | solution.py:209
  17.3 24.9 %copy-start.5 = (bf16[1024,640]{1,0:T(8,128)(2,1)S(1)}, bf16[1024,640]{1,0:T(8,128)(2,1)}, u32[]{:S(2)}) copy-start(bf16[1024,640]{1,0:T(8,128)(2,1)} %own_ref.2) | copy-start | bytes 3932164
  24.4 17.7 %copy-start.10 = (bf16[256,640]{1,0:T(8,128)(2,1)}, bf16[256,640]{1,0:T(8,128)(2,1)S(1)}, u32[]{:S(2)}) copy-start(bf16[256,640]{1,0:T(8,128)(2,1)S(1)} %collective-permute-done.2.refs_0_) | copy-start | bytes 983044
  25.3 29.3 %all-to-all-start = ((bf16[8,96,384]{2,1,0:T(8,128)(2,1)}), bf16[8,96,384]{2,1,0:T(8,128)(2,1)S(1)}, u32[]{:S(2)}, u32[]{:S(2)}) async-start(bf16[8,96,384]{2,1,0:T(8,128)(2,1)} %bitcast.4), calls=%async_computation | async-start | bytes 1179648 | tf_op jit(solution)/shard_map/all_to_all | solution.py:225
  42.1 1.7 copy-start.6
  43.8 11.0 %copy-start.3 = (bf16[64,256,64]{1,2,0:T(8,128)(2,1)S(1)}, bf16[64,256,64]{1,2,0:T(8,128)(2,1)}, u32[]{:S(2)}) copy-start(bf16[64,256,64]{1,2,0:T(8,128)(2,1)} %param.10) | copy-start | bytes 6291460
  54.5 40.6 %collective-permute-start.5 = (bf16[768,640]{1,0:T(8,128)(2,1)}, bf16[768,640]{1,0:T(8,128)(2,1)}, u32[]{:S(2)}, u32[]{:S(2)}) collective-permute-start(bf16[768,640]{1,0:T(8,128)(2,1)} %slice.15), channel_id=1, source_target_pairs={{0,128},{128,0},{1,129},{129,1},{2,130},{130,2},{3,131},{131,3},{4... | collective-permute-start | bytes 2949128 | tf_op jit(solution)/shard_map/ppermute | solution.py:209
  60.5 34.6 %collective-permute-start.3 = (bf16[512,640]{1,0:T(8,128)(2,1)}, bf16[512,640]{1,0:T(8,128)(2,1)S(1)}, u32[]{:S(2)}, u32[]{:S(2)}) collective-permute-start(bf16[512,640]{1,0:T(8,128)(2,1)} %get-tuple-element.16), channel_id=1, source_target_pairs={{0,128},{128,0},{1,129},{129,1},{2,130},{130,2},{3,131},{131,3},{4... | collective-permute-start | bytes 1966088 | tf_op jit(solution)/shard_map/ppermute | solution.py:209
  63.2 30.0 %all-to-all-start.1 = ((f32[32,16,128]{2,1,0:T(8,128)}), f32[32,16,128]{2,1,0:T(8,128)S(1)}, u32[]{:S(2)}, u32[]{:S(2)}) async-start(f32[32,16,128]{2,1,0:T(8,128)} %down.1), calls=%async_computation.1 | async-start | bytes 524288 | tf_op jit(solution)/shard_map/all_to_all | solution.py:244
  70.3 107.7 %reduce-scatter.5.cloned.1.call-start = ((), (), s32[]{:S(2)}) async-start(), calls=%async_computation.7 | async-start | bytes 2457600 | tf_op jit(solution)/shard_map/reduce_scatter | solution.py:246
  93.2 2.0 %copy-start.7 = (f32[32,16,128]{2,1,0:T(8,128)}, f32[32,16,128]{2,1,0:T(8,128)S(1)}, u32[]{:S(2)}) copy-start(f32[32,16,128]{2,1,0:T(8,128)S(1)} %all-to-all-done.1.refs_2_.parts_ref) | copy-start | bytes 786436
  95.1 0.8 copy-start.8
  107.6 16.0 %collective-permute-start.4 = (bf16[512,640]{1,0:T(8,128)(2,1)S(1)}, bf16[512,640]{1,0:T(8,128)(2,1)S(1)}, u32[]{:S(2)}, u32[]{:S(2)}) collective-permute-start(bf16[512,640]{1,0:T(8,128)(2,1)S(1)} %get-tuple-element.17), channel_id=1, source_target_pairs={{0,128},{128,0},{1,129},{129,1},{2,130},{130,2},{3,131},{131,3},{4... | collective-permute-start | bytes 1966088 | tf_op jit(solution)/shard_map/ppermute | solution.py:209
  110.8 16.2 %all-to-all-start.2 = ((bf16[32,16,128]{2,1,0:T(8,128)(2,1)}), bf16[32,16,128]{2,1,0:T(8,128)(2,1)S(1)}, u32[]{:S(2)}, u32[]{:S(2)}) async-start(bf16[32,16,128]{2,1,0:T(8,128)(2,1)} %sum.1), calls=%async_computation.2 | async-start | bytes 262144 | tf_op jit(solution)/shard_map/all_to_all | solution.py:258
  117.7 62.1 %reduce-scatter.3.cloned.1.call-start = ((), (), s32[]{:S(2)}) async-start(), calls=%async_computation.6 | async-start | bytes 2457600 | tf_op jit(solution)/shard_map/reduce_scatter | solution.py:246
  123.6 3.4 %copy-start.9 = (bf16[512,640]{1,0:T(8,128)(2,1)}, bf16[512,640]{1,0:T(8,128)(2,1)S(1)}, u32[]{:S(2)}) copy-start(bf16[512,640]{1,0:T(8,128)(2,1)S(1)} %collective-permute-done.4.refs_1_) | copy-start | bytes 1966084
  127.0 0.7 copy-start
  139.3 0.9 copy-start.1
  139.3 0.9 copy-start.4
  140.2 2.5 %copy-start.2 = (bf16[64,64,640]{2,1,0:T(8,128)(2,1)S(1)}, bf16[64,64,640]{2,1,0:T(8,128)(2,1)}, u32[]{:S(2)}) copy-start(bf16[64,64,640]{2,1,0:T(8,128)(2,1)} %param.11) | copy-start | bytes 15728644
Sparse Core Ops, SparseCore 0:
  25.4 63.1 all-gather.2
  107.7 27.9 reduce-scatter.4
  139.5 40.2 reduce-scatter.2

commit v8 on v4

--- a/solution.py
+++ b/solution.py
@@ -212,7 +212,7 @@
         part = (proj_up, proj_gate)[matrix][first * quarter : (first + count) * quarter]
         return matrix, first, count, lax.ppermute(part, "yh", SWAP)
 
-    far = [swap(0, 0, 1), swap(0, 1, 3), swap(1, 0, 2), swap(1, 2, 2)]
+    far = [swap(0, 0, 2), swap(0, 2, 2), swap(1, 0, 2), swap(1, 2, 2)]
 
     target = opponent // per_owner
     choose = target[:, None] == jnp.arange(owners, dtype=jnp.int32)[None, :]
@@ -245,7 +245,7 @@
     )(recv, jnp.transpose(adapter_down, (0, 2, 1)).reshape(per_owner * rank, width), far[1][3])
     rank_parts = lax.all_to_all(partial_rank, ADAPTER, 0, 0, tiled=True)
     partial, done = multiply(gathered, proj_up, proj_gate, far, flags, rank_parts)
-    total = lax.psum_scatter(partial, "x", scatter_dimension=0, tiled=False).astype(jnp.float32)
+    total = lax.psum_scatter(partial, "x", scatter_dimension=0, tiled=False)
     rank_sum = pl.pallas_call(
         sum_kernel,
         out_shape=jax.ShapeDtypeStruct((n_adapter, 16, LANES), jnp.bfloat16),
@@ -275,7 +275,9 @@
     offset = lax.dot_general(
         placed, returned, (((0,), (0,)), ((), ())), preferred_element_type=jnp.float32
     )
-    return (jax.nn.silu(total[:, hidden:] + offset) * total[:, :hidden]).astype(jnp.bfloat16)
+    up_sum, gate_sum = total[:, :hidden], total[:, hidden:]
+    gate = gate_sum.astype(jnp.float32) + offset
+    return (jax.nn.silu(gate) * up_sum.astype(jnp.float32)).astype(jnp.bfloat16)
 
 
 def solution(mesh):

time: 184 us -> 183 us (level)
  blocking collectives: 21.6 us -> 49.3 us
  starting transfers between devices: 55.2 us -> 40.4 us
  waiting for transfers between devices: 47.7 us -> 35.1 us
  other arithmetic: 3.43 us -> 1.45 us
    all_to_all x0 -> x1, blocking collectives: none -> 31.1 us  [on_device(): lax.all_to_all(offsets.reshape(owners, capacity, hidden), TRUNK, 0, 0, ti...]
    reduce_scatter x1, waiting for transfers between devices: 24.8 us -> 0.69 us  [on_device(): total = lax.psum_scatter(partial, 'x', scatter_dimension=0, tiled=False)]
    ppermute x4, waiting for transfers between devices: 9.94 us -> 24.8 us  [swap(): return (matrix, first, count, lax.ppermute(part, 'yh', SWAP))]
    all_to_all x1, starting transfers between devices: 20.1 us -> 12 us  [on_device(): rank_parts = lax.all_to_all(partial_rank, ADAPTER, 0, 0, tiled=True)]
    all_to_all x1 -> x0, starting transfers between devices: 7.94 us -> none  [on_device(): lax.all_to_all(offsets.reshape(owners, capacity, hidden), TRUNK, 0, 0, ti...]
    all_to_all x1, waiting for transfers between devices: 7.66 us -> 3.52 us  [on_device(): rank_parts = lax.all_to_all(partial_rank, ADAPTER, 0, 0, tiled=True)]
    all_to_all x1, blocking collectives: 21.6 us -> 18.2 us  [on_device(): rank_half = lax.all_to_all(rank_sum, ADAPTER, 0, 0, tiled=True)]
    unnamed x12 -> x16, local copies, waits for them, and re-layouts: 3.25 us -> 4.12 us
  transfers between devices with their start and end apart: 11 -> 10, of which waited for: 5 -> 5; matrix products, arithmetic and copies ran while one was open for 5% -> 4% of each run, Pallas kernels for 8% -> 7%
where the time goes in v8:
time: 183 us; the launch traced here: 182 us
  blocking collectives  49.3 us (27%)
  starting transfers between devices  40.4 us (22%)
  waiting for transfers between devices  35.1 us (19%)
  Pallas kernels  29 us (16%)
  between operations  13.5 us (7%)
  local copies, waits for them, and re-layouts  9.12 us (5%)
  matrix products  4.33 us (2%)
    all_to_all x1, blocking collectives, on_device(): lax.all_to_all(offsets.reshape(owners, capacity, hidden), TRUNK, 0, 0, ti...  31.1 us
    ppermute x4, waiting for transfers between devices, swap(): return (matrix, first, count, lax.ppermute(part, 'yh', SWAP))  24.8 us
    all_to_all x1, blocking collectives, on_device(): rank_half = lax.all_to_all(rank_sum, ADAPTER, 0, 0, tiled=True)  18.2 us
    all_to_all x1, starting transfers between devices, on_device(): lax.all_to_all(send.reshape(owners, capacity, width + LANES), TRUNK, 0, 0...  18.1 us
    pallas_call x1, Pallas kernels, multiply(): pl.pallas_call(functools.partial(multiply_kernel, pieces), out_shape=[jax...  16.1 us
    all_to_all x1, starting transfers between devices, on_device(): rank_parts = lax.all_to_all(partial_rank, ADAPTER, 0, 0, tiled=True)  12 us
    ppermute x4, starting transfers between devices, swap(): return (matrix, first, count, lax.ppermute(part, 'yh', SWAP))  6.21 us
    all_to_all x1, waiting for transfers between devices, on_device(): lax.all_to_all(send.reshape(owners, capacity, width + LANES), TRUNK, 0, 0...  6.04 us
  transfers between devices with their start and end apart: 10, of which 5 were waited for; matrix products, arithmetic and copies ran while one was open for 4% of the time, Pallas kernels for 7%

profile of v8, /device:TPU:1, one launch (start us, length us, event | category | flops | bytes accessed | tf_op | source)
XLA Modules:
  0.0 182.2 jit_solution(8935498978243063979)
XLA Ops:
  6.5 1.7 collective-permute-start
  8.2 2.1 %collective-permute-start.1 = (bf16[384,256]{1,0:T(8,128)(2,1)}, bf16[384,256]{1,0:T(8,128)(2,1)S(1)}, u32[]{:S(2)}, u32[]{:S(2)}) collective-permute-start(bf16[384,256]{1,0:T(8,128)(2,1)} %param.6), channel_id=1, source_target_pairs={{0,2},{2,0},{4,34},{6,32},{8,82},{10,80},{12,114},{14,112},{16,18}... | collective-permute-start | bytes 589832 | tf_op jit(solution)/shard_map/ppermute | solution.py:208
  10.4 2.3 %fusion.12 = (bf16[512,640]{1,0:T(8,128)(2,1)}, bf16[512,640]{1,0:T(8,128)(2,1)S(1)}) fusion(bf16[1024,640]{1,0:T(8,128)(2,1)} %up_ref.1), kind=kLoop, calls=%fused_computation.29 | loop fusion | bytes 2621440 | tf_op jit(solution)/shard_map/slice | solution.py:212
  12.7 2.6 %collective-permute-start.2 = (bf16[512,640]{1,0:T(8,128)(2,1)S(1)}, bf16[512,640]{1,0:T(8,128)(2,1)S(1)}, u32[]{:S(2)}, u32[]{:S(2)}) collective-permute-start(bf16[512,640]{1,0:T(8,128)(2,1)S(1)} %get-tuple-element.16), channel_id=1, source_target_pairs={{0,128},{128,0},{1,129},{129,1},{2,130},{130,2},{3,131},{131,3},{4... | collective-permute-start | bytes 1966088 | tf_op jit(solution)/shard_map/ppermute | solution.py:213
  15.6 1.4 convolution_convert_fusion
  17.0 14.5 %collective-permute-done.2.refs_0_ = bf16[512,640]{1,0:T(8,128)(2,1)S(1)} collective-permute-done((bf16[512,640]{1,0:T(8,128)(2,1)S(1)}, bf16[512,640]{1,0:T(8,128)(2,1)S(1)}, u32[]{:S(2)}, u32[]{:S(2)}) %collective-permute-start.2) | collective-permute-done | bytes 655392 | tf_op jit(solution)/shard_map/ppermute | solution.py:213
  31.6 0.8 copy-done.6
  32.4 0.8 pad_maximum_fusion
  33.8 18.1 %all-to-all-start = ((bf16[8,96,384]{2,1,0:T(8,128)(2,1)}), bf16[8,96,384]{2,1,0:T(8,128)(2,1)S(1)}, u32[]{:S(2)}, u32[]{:S(2)}) async-start(bf16[8,96,384]{2,1,0:T(8,128)(2,1)} %bitcast.4), calls=%async_computation | async-start | bytes 1179648 | tf_op jit(solution)/shard_map/all_to_all | solution.py:229
  51.9 2.6 %fusion.11 = (bf16[512,640]{1,0:T(8,128)(2,1)}, bf16[512,640]{1,0:T(8,128)(2,1)}) fusion(bf16[1024,640]{1,0:T(8,128)(2,1)} %gate_ref.1), kind=kLoop, calls=%fused_computation.28 | loop fusion | bytes 2621440 | tf_op jit(solution)/shard_map/slice | solution.py:212
  54.5 3.0 %collective-permute-start.5 = (bf16[512,640]{1,0:T(8,128)(2,1)}, bf16[512,640]{1,0:T(8,128)(2,1)}, u32[]{:S(2)}, u32[]{:S(2)}) collective-permute-start(bf16[512,640]{1,0:T(8,128)(2,1)} %get-tuple-element.13), channel_id=1, source_target_pairs={{0,128},{128,0},{1,129},{129,1},{2,130},{130,2},{3,131},{131,3},{4... | collective-permute-start | bytes 1966088 | tf_op jit(solution)/shard_map/ppermute | solution.py:213
  57.5 6.0 %all-to-all-done = bf16[8,96,384]{2,1,0:T(8,128)(2,1)S(1)} async-done(((bf16[8,96,384]{2,1,0:T(8,128)(2,1)}), bf16[8,96,384]{2,1,0:T(8,128)(2,1)S(1)}, u32[]{:S(2)}, u32[]{:S(2)}) %all-to-all-start) | async-done | bytes 589856 | tf_op jit(solution)/shard_map/all_to_all | solution.py:229
  63.6 5.7 %down.1 = f32[32,16,128]{2,1,0:T(8,128)} custom-call(bf16[768,384]{1,0:T(8,128)(2,1)S(1)} %bitcast.15, bf16[4096,256]{1,0:T(8,128)(2,1)S(1)} %bitcast.18, bf16[512,640]{1,0:T(8,128)(2,1)S(1)} %collective-permute-done.3._.refs_1_), custom_call_target="tpu_custom_call" | custom-call | flops 8000000000 | bytes 16777216 | tf_op jit(solution)/shard_map/down/pallas_call | solution.py:236
  69.3 12.0 %all-to-all-start.1 = ((f32[32,16,128]{2,1,0:T(8,128)}), f32[32,16,128]{2,1,0:T(8,128)S(1)}, u32[]{:S(2)}, u32[]{:S(2)}) async-start(f32[32,16,128]{2,1,0:T(8,128)} %down.1), calls=%async_computation.1 | async-start | bytes 524288 | tf_op jit(solution)/shard_map/all_to_all | solution.py:246
  82.2 10.2 %collective-permute-done.4.refs_2_ = bf16[512,640]{1,0:T(8,128)(2,1)} collective-permute-done((bf16[512,640]{1,0:T(8,128)(2,1)}, bf16[512,640]{1,0:T(8,128)(2,1)}, u32[]{:S(2)}, u32[]{:S(2)}) %collective-permute-start.4) | collective-permute-done | bytes 655392 | tf_op jit(solution)/shard_map/ppermute | solution.py:213
  92.5 3.5 %all-to-all-done.1.refs_4_.parts_ref = f32[32,16,128]{2,1,0:T(8,128)S(1)} async-done(((f32[32,16,128]{2,1,0:T(8,128)}), f32[32,16,128]{2,1,0:T(8,128)S(1)}, u32[]{:S(2)}, u32[]{:S(2)}) %all-to-all-start.1) | async-done | bytes 262176 | tf_op jit(solution)/shard_map/all_to_all | solution.py:246
  96.0 0.7 copy-done.4
  96.7 16.1 %multiply.1 = (bf16[4,384,1280]{2,1,0:T(8,128)(2,1)}, f32[8,128]{1,0:T(8,128)}) custom-call(s32[3]{0:T(128)} %pad_add_fusion.flags, bf16[16,384,512]{2,1,0:T(8,128)(2,1)} %bitcast.20, bf16[1024,640]{1,0:T(8,128)(2,1)} %up_ref.1, bf16[1024,640]{1,0:T(8,128)(2,1)} %gate_ref.1, bf16[512,640]{1,0:T(8,128)(2,1)} %copy-done.6, bf16[512,640]{1,0:T(8,128)(2,1)} %copy-done.2, ...), custom_call_target="tpu_custom_call" | custom-call | flops 8000000000 | bytes 16777216 | tf_op jit(solution)/shard_map/multiply/pallas_call | solution.py:98
  112.8 1.6 sum.1
  114.5 18.2 %all_to_all.20.rank_ref = bf16[32,16,128]{2,1,0:T(8,128)(2,1)S(1)} all-to-all(bf16[32,16,128]{2,1,0:T(8,128)(2,1)} %sum.1), channel_id=1, replica_groups=mesh['yh'=2,'x'=4,'z'=8,'yl'=2,'c'=2] {'z','yl','c'}, dimensions={0} | all-to-all | bytes 262144 | tf_op jit(solution)/shard_map/all_to_all | solution.py:257
  132.7 2.5 %copy-done = bf16[64,64,640]{2,1,0:T(8,128)(2,1)S(1)} copy-done((bf16[64,64,640]{2,1,0:T(8,128)(2,1)S(1)}, bf16[64,64,640]{2,1,0:T(8,128)(2,1)}, u32[]{:S(2)}) %copy-start) | copy-done | bytes 5242904
  135.2 5.6 %up.1 = bf16[768,640]{1,0:T(8,128)(2,1)S(1)} custom-call(bf16[32,16,128]{2,1,0:T(8,128)(2,1)S(1)} %all_to_all.20.rank_ref, bf16[768,384]{1,0:T(8,128)(2,1)S(1)} %bitcast.16, bf16[4096,640]{1,0:T(8,128)(2,1)S(1)} %bitcast.17, f32[8,128]{1,0:T(8,128)S(1)} %copy-done.3), custom_call_target="tpu_custom_call" | custom-call | flops 8000000000 | bytes 16777216 | tf_op jit(solution)/shard_map/up/pallas_call | solution.py:259
  140.8 31.1 %all_to_all.21 = bf16[8,96,640]{2,1,0:T(8,128)(2,1)S(1)} all-to-all(bf16[8,96,640]{2,1,0:T(8,128)(2,1)S(1)} %bitcast.14), channel_id=1, replica_groups=mesh['yh'=2,'x'=4,'z'=8,'yl'=2,'c'=2] {'yh','x'}, dimensions={0} | all-to-all | bytes 1966080 | tf_op jit(solution)/shard_map/all_to_all | solution.py:272
  172.6 2.8 %multiply_convert_fusion = bf16[384,640]{1,0:T(8,128)(2,1)} fusion(bf16[384,1280]{1,0:T(8,128)(2,1)} %bitcast.21, bf16[768,640]{1,0:T(8,128)(2,1)S(1)} %bitcast.19, s32[384]{0:T(512)S(1)} %convert_add_fusion), kind=kOutput, calls=%fused_computation.5 | convolution fusion | flops 379994112 | bytes 2459136 | tf_op jit(solution)/shard_map/dot_general | solution.py:275
  (30 shorter events, 2.6 us)
Async XLA Ops:
  6.5 9.1 %copy-start.7 = (bf16[384,256]{1,0:T(8,128)(2,1)S(1)}, bf16[384,256]{1,0:T(8,128)(2,1)}, u32[]{:S(2)}) copy-start(bf16[384,256]{1,0:T(8,128)(2,1)} %param.6) | copy-start | bytes 589828
  6.5 8.7 %copy-start.5 = (s32[384]{0:T(512)S(1)}, s32[384]{0:T(512)}, u32[]{:S(2)}) copy-start(s32[384]{0:T(512)} %param.7) | copy-start | bytes 4612
  6.5 89.5 %all-gather.3.cloned.1.call-start = ((), (), s32[]{:S(2)}) async-start(), calls=%async_computation.6 | async-start | bytes 6684672 | tf_op jit(solution)/shard_map/all_gather | solution.py:234
  6.5 10.5 %collective-permute-start = (bf16[384,256]{1,0:T(8,128)(2,1)}, bf16[384,256]{1,0:T(8,128)(2,1)S(1)}, u32[]{:S(2)}, u32[]{:S(2)}) collective-permute-start(bf16[384,256]{1,0:T(8,128)(2,1)} %param.6), channel_id=1, source_target_pairs={{0,0},{2,2},{4,32},{6,34},{8,80},{10,82},{12,112},{14,114},{16,16}... | collective-permute-start | bytes 589832 | tf_op jit(solution)/shard_map/ppermute | solution.py:207
  8.2 8.8 %collective-permute-start.1 = (bf16[384,256]{1,0:T(8,128)(2,1)}, bf16[384,256]{1,0:T(8,128)(2,1)S(1)}, u32[]{:S(2)}, u32[]{:S(2)}) collective-permute-start(bf16[384,256]{1,0:T(8,128)(2,1)} %param.6), channel_id=1, source_target_pairs={{0,2},{2,0},{4,34},{6,32},{8,82},{10,80},{12,114},{14,112},{16,18}... | collective-permute-start | bytes 589832 | tf_op jit(solution)/shard_map/ppermute | solution.py:208
  12.7 18.9 %collective-permute-start.2 = (bf16[512,640]{1,0:T(8,128)(2,1)S(1)}, bf16[512,640]{1,0:T(8,128)(2,1)S(1)}, u32[]{:S(2)}, u32[]{:S(2)}) collective-permute-start(bf16[512,640]{1,0:T(8,128)(2,1)S(1)} %get-tuple-element.16), channel_id=1, source_target_pairs={{0,128},{128,0},{1,129},{129,1},{2,130},{130,2},{3,131},{131,3},{4... | collective-permute-start | bytes 1966088 | tf_op jit(solution)/shard_map/ppermute | solution.py:213
  31.6 0.8 copy-start.6
  33.2 30.4 %collective-permute-start.3 = (bf16[512,640]{1,0:T(8,128)(2,1)}, bf16[512,640]{1,0:T(8,128)(2,1)S(1)}, u32[]{:S(2)}, u32[]{:S(2)}) collective-permute-start(bf16[512,640]{1,0:T(8,128)(2,1)} %get-tuple-element.15), channel_id=1, source_target_pairs={{0,128},{128,0},{1,129},{129,1},{2,130},{130,2},{3,131},{131,3},{4... | collective-permute-start | bytes 1966088 | tf_op jit(solution)/shard_map/ppermute | solution.py:213
  33.8 29.8 %all-to-all-start = ((bf16[8,96,384]{2,1,0:T(8,128)(2,1)}), bf16[8,96,384]{2,1,0:T(8,128)(2,1)S(1)}, u32[]{:S(2)}, u32[]{:S(2)}) async-start(bf16[8,96,384]{2,1,0:T(8,128)(2,1)} %bitcast.4), calls=%async_computation | async-start | bytes 1179648 | tf_op jit(solution)/shard_map/all_to_all | solution.py:229
  51.9 11.6 %copy-start.1 = (bf16[64,256,64]{1,2,0:T(8,128)(2,1)S(1)}, bf16[64,256,64]{1,2,0:T(8,128)(2,1)}, u32[]{:S(2)}) copy-start(bf16[64,256,64]{1,2,0:T(8,128)(2,1)} %param.10) | copy-start | bytes 6291460
  54.5 27.7 %collective-permute-start.5 = (bf16[512,640]{1,0:T(8,128)(2,1)}, bf16[512,640]{1,0:T(8,128)(2,1)}, u32[]{:S(2)}, u32[]{:S(2)}) collective-permute-start(bf16[512,640]{1,0:T(8,128)(2,1)} %get-tuple-element.13), channel_id=1, source_target_pairs={{0,128},{128,0},{1,129},{129,1},{2,130},{130,2},{3,131},{131,3},{4... | collective-permute-start | bytes 1966088 | tf_op jit(solution)/shard_map/ppermute | solution.py:213
  57.5 35.0 %collective-permute-start.4 = (bf16[512,640]{1,0:T(8,128)(2,1)}, bf16[512,640]{1,0:T(8,128)(2,1)}, u32[]{:S(2)}, u32[]{:S(2)}) collective-permute-start(bf16[512,640]{1,0:T(8,128)(2,1)} %get-tuple-element.14), channel_id=1, source_target_pairs={{0,128},{128,0},{1,129},{129,1},{2,130},{130,2},{3,131},{131,3},{4... | collective-permute-start | bytes 1966088 | tf_op jit(solution)/shard_map/ppermute | solution.py:213
  63.6 5.8 %copy-start.2 = (bf16[512,640]{1,0:T(8,128)(2,1)}, bf16[512,640]{1,0:T(8,128)(2,1)S(1)}, u32[]{:S(2)}) copy-start(bf16[512,640]{1,0:T(8,128)(2,1)S(1)} %collective-permute-done.3._.refs_1_) | copy-start | bytes 1966084
  69.3 26.7 %all-to-all-start.1 = ((f32[32,16,128]{2,1,0:T(8,128)}), f32[32,16,128]{2,1,0:T(8,128)S(1)}, u32[]{:S(2)}, u32[]{:S(2)}) async-start(f32[32,16,128]{2,1,0:T(8,128)} %down.1), calls=%async_computation.1 | async-start | bytes 524288 | tf_op jit(solution)/shard_map/all_to_all | solution.py:246
  81.3 91.3 %reduce-scatter.2.cloned.1.call-start = ((), (), s32[]{:S(2)}) async-start(), calls=%async_computation.5 | async-start | bytes 4915200 | tf_op jit(solution)/shard_map/reduce_scatter | solution.py:248
  96.0 0.7 copy-start.4
  112.8 19.8 %copy-start.3 = (f32[8,128]{1,0:T(8,128)S(1)}, f32[8,128]{1,0:T(8,128)}, u32[]{:S(2)}) copy-start(f32[8,128]{1,0:T(8,128)} %get-tuple-element.12.refs_0_) | copy-start | bytes 12292
  132.7 2.5 %copy-start = (bf16[64,64,640]{2,1,0:T(8,128)(2,1)S(1)}, bf16[64,64,640]{2,1,0:T(8,128)(2,1)}, u32[]{:S(2)}) copy-start(bf16[64,64,640]{2,1,0:T(8,128)(2,1)} %param.11) | copy-start | bytes 15728644
Sparse Core Ops, SparseCore 0:
  33.3 62.1 all-gather.2
  113.0 59.6 reduce-scatter.1

commit v9 on v8

--- a/solution.py
+++ b/solution.py
@@ -72,15 +72,15 @@
         stores.append(
             pltpu.make_async_copy(out.at[n], out_ref.at[lax.rem(here + n, NX)], out_sems.at[n])
         )
-    for copy in weights + rows[0] + rows[1]:
+    for copy in weights + rows[0]:
         copy.start()
     for copy in weights:
         copy.wait()
     for n in range(NX):
         for copy in rows[n]:
             copy.wait()
-        if n + 2 < NX:
-            for copy in rows[n + 2]:
+        if n + 1 < NX:
+            for copy in rows[n + 1]:
                 copy.start()
         out[n] = jnp.dot(lhs[n], rhs[...], preferred_element_type=jnp.float32).astype(
             jnp.bfloat16
@@ -212,7 +212,7 @@
         part = (proj_up, proj_gate)[matrix][first * quarter : (first + count) * quarter]
         return matrix, first, count, lax.ppermute(part, "yh", SWAP)
 
-    far = [swap(0, 0, 2), swap(0, 2, 2), swap(1, 0, 2), swap(1, 2, 2)]
+    far = [swap(0, 0, 1), swap(0, 1, 3), swap(1, 0, 2), swap(1, 2, 2)]
 
     target = opponent // per_owner
     choose = target[:, None] == jnp.arange(owners, dtype=jnp.int32)[None, :]

time: 183 us -> 184 us (level)
  waiting for transfers between devices: 35.1 us -> 23.6 us
  starting transfers between devices: 40.4 us -> 47.3 us
  blocking collectives: 49.3 us -> 54.6 us
    ppermute x4, waiting for transfers between devices: 24.8 us -> 9.88 us  [swap(): return (matrix, first, count, lax.ppermute(part, 'yh', SWAP))]
    all_to_all x1, starting transfers between devices: 12 us -> 20.1 us  [on_device(): rank_parts = lax.all_to_all(partial_rank, ADAPTER, 0, 0, tiled=True)]
    all_to_all x1, waiting for transfers between devices: 3.52 us -> 7.65 us  [on_device(): rank_parts = lax.all_to_all(partial_rank, ADAPTER, 0, 0, tiled=True)]
    all_to_all x1, blocking collectives: 18.2 us -> 21.6 us  [on_device(): rank_half = lax.all_to_all(rank_sum, ADAPTER, 0, 0, tiled=True)]
    unnamed x16 -> x12, local copies, waits for them, and re-layouts: 4.12 us -> 3.25 us
    slice x2 -> x3, local copies, waits for them, and re-layouts: 4.88 us -> 4.45 us  [swap(): (proj_up, proj_gate)[matrix][first * quarter:(first + count) * quarter]]
  transfers between devices with their start and end apart: 10 -> 10, of which waited for: 5 -> 5; matrix products, arithmetic and copies ran while one was open for 4% -> 5% of each run, Pallas kernels for 7% -> 7%
where the time goes in v9:
time: 184 us; the launch traced here: 183 us
  blocking collectives  54.6 us (30%)
  starting transfers between devices  47.3 us (26%)
  Pallas kernels  28.8 us (16%)
  waiting for transfers between devices  23.6 us (13%)
  between operations  13.5 us (7%)
  local copies, waits for them, and re-layouts  7.82 us (4%)
  matrix products  5.38 us (3%)
  other arithmetic  2.18 us (1%)
    all_to_all x1, blocking collectives, on_device(): lax.all_to_all(offsets.reshape(owners, capacity, hidden), TRUNK, 0, 0, ti...  33 us
    all_to_all x1, blocking collectives, on_device(): rank_half = lax.all_to_all(rank_sum, ADAPTER, 0, 0, tiled=True)  21.6 us
    all_to_all x1, starting transfers between devices, on_device(): rank_parts = lax.all_to_all(partial_rank, ADAPTER, 0, 0, tiled=True)  20.1 us
    all_to_all x1, starting transfers between devices, on_device(): lax.all_to_all(send.reshape(owners, capacity, width + LANES), TRUNK, 0, 0...  16.8 us
    pallas_call x1, Pallas kernels, multiply(): pl.pallas_call(functools.partial(multiply_kernel, pieces), out_shape=[jax...  15.8 us
    ppermute x4, waiting for transfers between devices, swap(): return (matrix, first, count, lax.ppermute(part, 'yh', SWAP))  9.88 us
    all_to_all x1, waiting for transfers between devices, on_device(): rank_parts = lax.all_to_all(partial_rank, ADAPTER, 0, 0, tiled=True)  7.65 us
    ppermute x4, starting transfers between devices, swap(): return (matrix, first, count, lax.ppermute(part, 'yh', SWAP))  6.44 us
  transfers between devices with their start and end apart: 10, of which 5 were waited for; matrix products, arithmetic and copies ran while one was open for 5% of the time, Pallas kernels for 7%

profile of v9, /device:TPU:1, one launch (start us, length us, event | category | flops | bytes accessed | tf_op | source)
XLA Modules:
  0.0 183.1 jit_solution(6151016635340251587)
XLA Ops:
  6.5 1.6 collective-permute-start
  8.1 2.1 %collective-permute-start.1 = (bf16[384,256]{1,0:T(8,128)(2,1)}, bf16[384,256]{1,0:T(8,128)(2,1)S(1)}, u32[]{:S(2)}, u32[]{:S(2)}) collective-permute-start(bf16[384,256]{1,0:T(8,128)(2,1)} %param.6), channel_id=1, source_target_pairs={{0,2},{2,0},{4,34},{6,32},{8,82},{10,80},{12,114},{14,112},{16,18}... | collective-permute-start | bytes 589832 | tf_op jit(solution)/shard_map/ppermute | solution.py:208
  10.2 1.0 slice.18
  11.2 2.7 %collective-permute-start.2 = (bf16[256,640]{1,0:T(8,128)(2,1)S(1)}, bf16[256,640]{1,0:T(8,128)(2,1)S(1)}, u32[]{:S(2)}, u32[]{:S(2)}) collective-permute-start(bf16[256,640]{1,0:T(8,128)(2,1)S(1)} %slice.18), channel_id=1, source_target_pairs={{0,128},{128,0},{1,129},{129,1},{2,130},{130,2},{3,131},{131,3},{4... | collective-permute-start | bytes 983048 | tf_op jit(solution)/shard_map/ppermute | solution.py:213
  15.0 2.4 %convolution_convert_fusion = bf16[768,384]{1,0:T(8,128)(2,1)} fusion(s32[384]{0:T(512)S(1)} %convert_add_fusion, bf16[384,128]{1,0:T(8,128)(2,1)S(1)} %broadcast_in_dim.7, bf16[384,256]{1,0:T(8,128)(2,1)} %param.6), kind=kOutput, calls=%fused_computation.1 | convolution fusion | flops 227672064 | bytes 886272 | tf_op jit(solution)/shard_map/dot_general | solution.py:228
  17.4 7.0 %collective-permute-done.2.refs_0_ = bf16[256,640]{1,0:T(8,128)(2,1)S(1)} collective-permute-done((bf16[256,640]{1,0:T(8,128)(2,1)S(1)}, bf16[256,640]{1,0:T(8,128)(2,1)S(1)}, u32[]{:S(2)}, u32[]{:S(2)}) %collective-permute-start.2) | collective-permute-done | bytes 327712 | tf_op jit(solution)/shard_map/ppermute | solution.py:213
  24.4 0.8 pad_maximum_fusion
  25.3 1.1 slice.19
  26.3 0.7 collective-permute-start.3
  27.1 16.8 %all-to-all-start = ((bf16[8,96,384]{2,1,0:T(8,128)(2,1)}), bf16[8,96,384]{2,1,0:T(8,128)(2,1)S(1)}, u32[]{:S(2)}, u32[]{:S(2)}) async-start(bf16[8,96,384]{2,1,0:T(8,128)(2,1)} %bitcast.4), calls=%async_computation | async-start | bytes 1179648 | tf_op jit(solution)/shard_map/all_to_all | solution.py:229
  43.9 2.4 %fusion.11 = (bf16[512,640]{1,0:T(8,128)(2,1)}, bf16[512,640]{1,0:T(8,128)(2,1)S(1)}) fusion(bf16[1024,640]{1,0:T(8,128)(2,1)} %gate_ref.1), kind=kLoop, calls=%fused_computation.28 | loop fusion | bytes 2621440 | tf_op jit(solution)/shard_map/slice | solution.py:212
  46.3 3.0 %collective-permute-start.5 = (bf16[512,640]{1,0:T(8,128)(2,1)}, bf16[512,640]{1,0:T(8,128)(2,1)}, u32[]{:S(2)}, u32[]{:S(2)}) collective-permute-start(bf16[512,640]{1,0:T(8,128)(2,1)} %get-tuple-element.13), channel_id=1, source_target_pairs={{0,128},{128,0},{1,129},{129,1},{2,130},{130,2},{3,131},{131,3},{4... | collective-permute-start | bytes 1966088 | tf_op jit(solution)/shard_map/ppermute | solution.py:213
  49.3 5.3 %all-to-all-done = bf16[8,96,384]{2,1,0:T(8,128)(2,1)S(1)} async-done(((bf16[8,96,384]{2,1,0:T(8,128)(2,1)}), bf16[8,96,384]{2,1,0:T(8,128)(2,1)S(1)}, u32[]{:S(2)}, u32[]{:S(2)}) %all-to-all-start) | async-done | bytes 589856 | tf_op jit(solution)/shard_map/all_to_all | solution.py:229
  54.6 5.7 %down.1 = f32[32,16,128]{2,1,0:T(8,128)} custom-call(bf16[768,384]{1,0:T(8,128)(2,1)S(1)} %bitcast.15, bf16[4096,256]{1,0:T(8,128)(2,1)S(1)} %bitcast.18, bf16[768,640]{1,0:T(8,128)(2,1)} %collective-permute-done.3._.refs_1_), custom_call_target="tpu_custom_call" | custom-call | flops 8000000000 | bytes 16777216 | tf_op jit(solution)/shard_map/down/pallas_call | solution.py:236
  60.3 20.1 %all-to-all-start.1 = ((f32[32,16,128]{2,1,0:T(8,128)}), f32[32,16,128]{2,1,0:T(8,128)S(1)}, u32[]{:S(2)}, u32[]{:S(2)}) async-start(f32[32,16,128]{2,1,0:T(8,128)} %down.1), calls=%async_computation.1 | async-start | bytes 524288 | tf_op jit(solution)/shard_map/all_to_all | solution.py:246
  81.4 2.9 %collective-permute-done.4.refs_2_ = bf16[512,640]{1,0:T(8,128)(2,1)} collective-permute-done((bf16[512,640]{1,0:T(8,128)(2,1)S(1)}, bf16[512,640]{1,0:T(8,128)(2,1)}, u32[]{:S(2)}, u32[]{:S(2)}) %collective-permute-start.4) | collective-permute-done | bytes 655392 | tf_op jit(solution)/shard_map/ppermute | solution.py:213
  84.3 7.7 %all-to-all-done.1.refs_4_.parts_ref = f32[32,16,128]{2,1,0:T(8,128)S(1)} async-done(((f32[32,16,128]{2,1,0:T(8,128)}), f32[32,16,128]{2,1,0:T(8,128)S(1)}, u32[]{:S(2)}, u32[]{:S(2)}) %all-to-all-start.1) | async-done | bytes 262176 | tf_op jit(solution)/shard_map/all_to_all | solution.py:246
  92.6 15.8 %multiply.1 = (bf16[4,384,1280]{2,1,0:T(8,128)(2,1)}, f32[8,128]{1,0:T(8,128)}) custom-call(s32[3]{0:T(128)} %pad_add_fusion.flags, bf16[16,384,512]{2,1,0:T(8,128)(2,1)} %bitcast.20, bf16[1024,640]{1,0:T(8,128)(2,1)} %up_ref.1, bf16[1024,640]{1,0:T(8,128)(2,1)} %gate_ref.1, bf16[256,640]{1,0:T(8,128)(2,1)} %copy-done.5, ...), custom_call_target="tpu_custom_call" | custom-call | flops 8000000000 | bytes 16777216 | tf_op jit(solution)/shard_map/multiply/pallas_call | solution.py:98
  108.5 1.6 sum.1
  110.2 21.6 %all_to_all.20.rank_ref = bf16[32,16,128]{2,1,0:T(8,128)(2,1)S(1)} all-to-all(bf16[32,16,128]{2,1,0:T(8,128)(2,1)} %sum.1), channel_id=1, replica_groups=mesh['yh'=2,'x'=4,'z'=8,'yl'=2,'c'=2] {'z','yl','c'}, dimensions={0} | all-to-all | bytes 262144 | tf_op jit(solution)/shard_map/all_to_all | solution.py:257
  131.8 2.5 %copy-done = bf16[64,64,640]{2,1,0:T(8,128)(2,1)S(1)} copy-done((bf16[64,64,640]{2,1,0:T(8,128)(2,1)S(1)}, bf16[64,64,640]{2,1,0:T(8,128)(2,1)}, u32[]{:S(2)}) %copy-start) | copy-done | bytes 5242904
  134.3 5.6 %up.1 = bf16[768,640]{1,0:T(8,128)(2,1)S(1)} custom-call(bf16[32,16,128]{2,1,0:T(8,128)(2,1)S(1)} %all_to_all.20.rank_ref, bf16[768,384]{1,0:T(8,128)(2,1)S(1)} %bitcast.16, bf16[4096,640]{1,0:T(8,128)(2,1)S(1)} %bitcast.17, f32[8,128]{1,0:T(8,128)S(1)} %copy-done.2), custom_call_target="tpu_custom_call" | custom-call | flops 8000000000 | bytes 16777216 | tf_op jit(solution)/shard_map/up/pallas_call | solution.py:259
  139.8 33.0 %all_to_all.21 = bf16[8,96,640]{2,1,0:T(8,128)(2,1)S(1)} all-to-all(bf16[8,96,640]{2,1,0:T(8,128)(2,1)S(1)} %bitcast.14), channel_id=1, replica_groups=mesh['yh'=2,'x'=4,'z'=8,'yl'=2,'c'=2] {'yh','x'}, dimensions={0} | all-to-all | bytes 1966080 | tf_op jit(solution)/shard_map/all_to_all | solution.py:272
  173.5 2.8 %multiply_convert_fusion = bf16[384,640]{1,0:T(8,128)(2,1)} fusion(bf16[384,1280]{1,0:T(8,128)(2,1)} %bitcast.21, bf16[768,640]{1,0:T(8,128)(2,1)S(1)} %bitcast.19, s32[384]{0:T(512)S(1)} %convert_add_fusion), kind=kOutput, calls=%fused_computation.5 | convolution fusion | flops 379994112 | bytes 2459136 | tf_op jit(solution)/shard_map/dot_general | solution.py:275
  (27 shorter events, 3.4 us)
Async XLA Ops:
  6.5 85.4 %all-gather.3.cloned.1.call-start = ((), (), s32[]{:S(2)}) async-start(), calls=%async_computation.6 | async-start | bytes 6684672 | tf_op jit(solution)/shard_map/all_gather | solution.py:234
  6.5 10.9 %collective-permute-start = (bf16[384,256]{1,0:T(8,128)(2,1)}, bf16[384,256]{1,0:T(8,128)(2,1)S(1)}, u32[]{:S(2)}, u32[]{:S(2)}) collective-permute-start(bf16[384,256]{1,0:T(8,128)(2,1)} %param.6), channel_id=1, source_target_pairs={{0,0},{2,2},{4,32},{6,34},{8,80},{10,82},{12,112},{14,114},{16,16}... | collective-permute-start | bytes 589832 | tf_op jit(solution)/shard_map/ppermute | solution.py:207
  8.1 9.3 %collective-permute-start.1 = (bf16[384,256]{1,0:T(8,128)(2,1)}, bf16[384,256]{1,0:T(8,128)(2,1)S(1)}, u32[]{:S(2)}, u32[]{:S(2)}) collective-permute-start(bf16[384,256]{1,0:T(8,128)(2,1)} %param.6), channel_id=1, source_target_pairs={{0,2},{2,0},{4,34},{6,32},{8,82},{10,80},{12,114},{14,112},{16,18}... | collective-permute-start | bytes 589832 | tf_op jit(solution)/shard_map/ppermute | solution.py:208
  11.2 13.2 %collective-permute-start.2 = (bf16[256,640]{1,0:T(8,128)(2,1)S(1)}, bf16[256,640]{1,0:T(8,128)(2,1)S(1)}, u32[]{:S(2)}, u32[]{:S(2)}) collective-permute-start(bf16[256,640]{1,0:T(8,128)(2,1)S(1)} %slice.18), channel_id=1, source_target_pairs={{0,128},{128,0},{1,129},{129,1},{2,130},{130,2},{3,131},{131,3},{4... | collective-permute-start | bytes 983048 | tf_op jit(solution)/shard_map/ppermute | solution.py:213
  15.0 10.3 %copy-start.3 = (bf16[1024,640]{1,0:T(8,128)(2,1)S(1)}, bf16[1024,640]{1,0:T(8,128)(2,1)}, u32[]{:S(2)}) copy-start(bf16[1024,640]{1,0:T(8,128)(2,1)} %up_ref.1) | copy-start | bytes 3932164
  24.4 1.9 %copy-start.5 = (bf16[256,640]{1,0:T(8,128)(2,1)}, bf16[256,640]{1,0:T(8,128)(2,1)S(1)}, u32[]{:S(2)}) copy-start(bf16[256,640]{1,0:T(8,128)(2,1)S(1)} %collective-permute-done.2.refs_0_) | copy-start | bytes 983044
  26.3 28.3 %collective-permute-start.3 = (bf16[768,640]{1,0:T(8,128)(2,1)}, bf16[768,640]{1,0:T(8,128)(2,1)}, u32[]{:S(2)}, u32[]{:S(2)}) collective-permute-start(bf16[768,640]{1,0:T(8,128)(2,1)} %slice.19), channel_id=1, source_target_pairs={{0,128},{128,0},{1,129},{129,1},{2,130},{130,2},{3,131},{131,3},{4... | collective-permute-start | bytes 2949128 | tf_op jit(solution)/shard_map/ppermute | solution.py:213
  27.1 27.5 %all-to-all-start = ((bf16[8,96,384]{2,1,0:T(8,128)(2,1)}), bf16[8,96,384]{2,1,0:T(8,128)(2,1)S(1)}, u32[]{:S(2)}, u32[]{:S(2)}) async-start(bf16[8,96,384]{2,1,0:T(8,128)(2,1)} %bitcast.4), calls=%async_computation | async-start | bytes 1179648 | tf_op jit(solution)/shard_map/all_to_all | solution.py:229
  43.9 10.7 %copy-start.1 = (bf16[64,256,64]{1,2,0:T(8,128)(2,1)S(1)}, bf16[64,256,64]{1,2,0:T(8,128)(2,1)}, u32[]{:S(2)}) copy-start(bf16[64,256,64]{1,2,0:T(8,128)(2,1)} %param.10) | copy-start | bytes 6291460
  46.3 35.1 %collective-permute-start.5 = (bf16[512,640]{1,0:T(8,128)(2,1)}, bf16[512,640]{1,0:T(8,128)(2,1)}, u32[]{:S(2)}, u32[]{:S(2)}) collective-permute-start(bf16[512,640]{1,0:T(8,128)(2,1)} %get-tuple-element.13), channel_id=1, source_target_pairs={{0,128},{128,0},{1,129},{129,1},{2,130},{130,2},{3,131},{131,3},{4... | collective-permute-start | bytes 1966088 | tf_op jit(solution)/shard_map/ppermute | solution.py:213
  49.2 35.0 %collective-permute-start.4 = (bf16[512,640]{1,0:T(8,128)(2,1)S(1)}, bf16[512,640]{1,0:T(8,128)(2,1)}, u32[]{:S(2)}, u32[]{:S(2)}) collective-permute-start(bf16[512,640]{1,0:T(8,128)(2,1)S(1)} %get-tuple-element.14), channel_id=1, source_target_pairs={{0,128},{128,0},{1,129},{129,1},{2,130},{130,2},{3,131},{131,3},{4... | collective-permute-start | bytes 1966088 | tf_op jit(solution)/shard_map/ppermute | solution.py:213
  60.3 31.6 %all-to-all-start.1 = ((f32[32,16,128]{2,1,0:T(8,128)}), f32[32,16,128]{2,1,0:T(8,128)S(1)}, u32[]{:S(2)}, u32[]{:S(2)}) async-start(f32[32,16,128]{2,1,0:T(8,128)} %down.1), calls=%async_computation.1 | async-start | bytes 524288 | tf_op jit(solution)/shard_map/all_to_all | solution.py:246
  80.5 93.1 %reduce-scatter.2.cloned.1.call-start = ((), (), s32[]{:S(2)}) async-start(), calls=%async_computation.5 | async-start | bytes 4915200 | tf_op jit(solution)/shard_map/reduce_scatter | solution.py:248
  91.9 0.7 copy-start.4
  108.5 23.3 %copy-start.2 = (f32[8,128]{1,0:T(8,128)S(1)}, f32[8,128]{1,0:T(8,128)}, u32[]{:S(2)}) copy-start(f32[8,128]{1,0:T(8,128)} %get-tuple-element.12.refs_0_) | copy-start | bytes 12292
  131.8 2.5 %copy-start = (bf16[64,64,640]{2,1,0:T(8,128)(2,1)S(1)}, bf16[64,64,640]{2,1,0:T(8,128)(2,1)}, u32[]{:S(2)}) copy-start(bf16[64,64,640]{2,1,0:T(8,128)(2,1)} %param.11) | copy-start | bytes 15728644
Sparse Core Ops, SparseCore 0:
  25.4 57.5 all-gather.2
  108.6 64.8 reduce-scatter.1
